TPU v7x, 32 devices: a whole 2x2x4 slice. The times are simulated.
32 devices in a mesh: bead: 8 (over z, core), space: 4 (over y, x).
Axes of the slice: x: 2, y: 2, z: 4, core: 2. Of those that a mesh axis runs over, the one named last changes fastest.
Arguments:
- positions: float32 [3, 32, 16384], P(None, 'bead', 'space'), may hold values from -0.12 to 2.12
- momenta: float32 [3, 32, 16384], P(None, 'bead', 'space'), may hold values from -6 to 6
- atom_types: int32 [16384], P('space'), may hold values from 0 to 3
- neighbours: int32 [128, 5], P('space'), may hold values from 0 to 127, as said below
- thermal_noise: float32 [2, 3, 32, 16384], P(None, None, 'bead', 'space'), may hold values from -6 to 6
Outputs:
- positions_out: float32 [3, 32, 16384], P(None, 'bead', 'space')
- momenta_out: float32 [3, 32, 16384], P(None, 'bead', 'space')
Inputs may be any that keep to these rules, and one draw needn't show every extreme that they name: `neighbours`: the row of block b holds 5 different blocks within 4 blocks of b, b itself and one block exactly 4 away among them.
All inputs are finite; a program needn't handle non-finite values.
Results may differ from a plain program's by a relative error of at most 0.0003.
Values sent between devices are 32-bit elements; how exact they have to be, the bound alone decides.
No kernel may reach another device: no remote copies, remote signals or barrier semaphores. Data moves between devices by JAX's collectives and lax.ppermute only.
A program may use at most 64 MiB of HBM per device.

v0:
```python
import functools
import math

import jax
import jax.numpy as jnp
import numpy as np
from jax import lax
from jax.experimental import pallas as pl
from jax.experimental.pallas import tpu as pltpu
from jax.sharding import PartitionSpec as P

BLOCK = 128
HALO = 4

half_step = 0.025
time_step = 0.05
chain_freq = 12.0
thermal = 0.375
centroid_friction = 1.0
screening = 4.0
softening = 0.09
CHARGES = (1.0, -1.0, 0.6, -1.4)
MASSES = (1.0, 2.0, 3.0, 4.0)

PAIR_ROWS = 24
PAIR_PAD = 32
SUM_ROWS = 16
QUAD = 4
FRAME = 8
f32 = jnp.float32
bf16 = jnp.bfloat16


def mode_constants(bead_total):
    j = np.arange(bead_total)[:, None]
    k = np.arange(bead_total)[None, :]
    half = bead_total // 2
    phase = 2.0 * np.pi * ((j * k) % bead_total) / bead_total
    plain = 1.0 / math.sqrt(bead_total)
    paired = math.sqrt(2.0 / bead_total)
    matrix = np.where(
        k == 0,
        plain,
        np.where(
            k < half,
            paired * np.cos(phase),
            np.where(k == half, plain * np.cos(phase), paired * np.sin(phase)),
        ),
    )
    modes = np.arange(bead_total)
    frequency = 2.0 * chain_freq * np.sin(np.pi * modes / bead_total)
    angle = frequency * time_step
    ratio = np.where(modes == 0, time_step, np.sin(angle) / np.where(modes == 0, 1.0, frequency))
    friction = np.where(modes == 0, centroid_friction, 2.0 * frequency)
    damping = np.exp(-friction * time_step)
    kick = np.sqrt(1.0 - damping * damping)
    tables = np.stack([np.cos(angle), ratio, frequency * np.sin(angle), damping, kick])
    tables = np.broadcast_to(tables[:, :, None], tables.shape + (BLOCK,))
    return matrix.astype(np.float32), np.ascontiguousarray(tables).astype(np.float32)


def split3(v):
    one = v.astype(bf16).astype(f32)
    rest = v - one
    two = rest.astype(bf16).astype(f32)
    three = (rest - two).astype(bf16).astype(f32)
    return one, two, three


def pair_rows(coords, norm, own):
    rows = []
    for v in coords:
        one, two, three = split3(v)
        if own:
            one, two, three = -2.0 * one, -2.0 * two, -2.0 * three
            rows += [one, one, two, two, one, three]
        else:
            rows += [one, two, one, two, three, one]
    ones = [jnp.ones_like(norm)] * 3
    norms = list(split3(norm))
    return rows + (norms + ones if own else ones + norms)


SCALE = 1.0 / (screening * math.log(2.0))


def weigh(square):
    inverse = lax.rsqrt(square)
    decay = jnp.exp2(-(square * inverse))
    return decay * ((inverse * inverse) * (inverse + math.log(2.0)))


def whole_quads(beads):
    return -(-beads // QUAD) * QUAD


def add_forces(form, blocks, margin, listed, offset_ref, charge_ref, coord_ref, scratch):
    rows_ref, sums_ref, far_ref, heavy_ref, near_ref, total_ref, force_ref, *buffers = scratch
    weight_refs = buffers
    beads = coord_ref.shape[1]
    pairs = beads // 2
    frame = min(FRAME, blocks)
    width = frame + 2 * margin
    middle = margin + (frame - 1) / 2.0
    at_once = max(1, 8 // beads)
    lines = at_once * beads
    units = blocks * pairs

    def put(ref, k, value):
        ref[k * lines:(k + 1) * lines, :] = value

    def centred(block, place):
        spans = [pl.ds(pl.multiple_of((block + i) * BLOCK, BLOCK), BLOCK) for i in range(at_once)]
        coords = [
            (jnp.concatenate([coord_ref[c, :, lanes] for lanes in spans], axis=0) - 1.0) * SCALE for c in range(3)
        ]
        shift = jnp.concatenate(
            [jnp.full((beads, BLOCK), SCALE, f32) * ((place + i).astype(f32) - middle) for i in range(at_once)], axis=0
        )
        coords[0] = coords[0] + shift
        norm = coords[0] * coords[0] + coords[1] * coords[1] + coords[2] * coords[2]
        charge = jnp.concatenate(
            [jnp.broadcast_to(charge_ref[:, lanes], (beads, BLOCK)) for lanes in spans], axis=0
        )
        return coords, norm, charge

    nothing = jnp.zeros((lines, BLOCK), f32)
    for k in range(PAIR_ROWS, PAIR_PAD):
        put(rows_ref, k, nothing)
    for k in range(12, SUM_ROWS):
        put(sums_ref, k, nothing)
    blank = jnp.zeros((PAIR_PAD, BLOCK), f32)

    def one_frame(at_frame, carry):
        first = at_frame * frame

        def one_table(step, inner):
            place = step * at_once
            coords, norm, charge = centred(first + place, place)
            for k, row in enumerate(pair_rows(coords, norm, False)):
                put(rows_ref, k, row)
            for c, v in enumerate([charge] + [charge * x for x in coords]):
                for level, part in enumerate(split3(v)):
                    put(sums_ref, level * 4 + c, part)
            for i in range(at_once):
                at = at_frame * width + place + i
                for quad in range(beads // QUAD):
                    low = i * beads + quad * QUAD
                    four = jnp.concatenate(
                        [rows_ref[pl.ds(low + j, PAIR_PAD, stride=lines), :] for j in range(QUAD)], axis=0
                    )
                    far_ref[at, quad] = jnp.transpose(four).astype(bf16)
                    for half in range(2):
                        heavy_ref[at, 2 * quad + half] = jnp.concatenate(
                            [
                                sums_ref[pl.ds(low + 2 * half + j, SUM_ROWS, stride=lines), :]
                                for j in range(2)
                            ],
                            axis=0,
                        ).astype(bf16)
            return inner

        lax.fori_loop(0, width // at_once, one_table, 0)

        def one_own(step, inner):
            block = step * at_once
            coords, norm, _ = centred(first + margin + block, block + margin)
            for k, row in enumerate(pair_rows(coords, norm + softening * SCALE * SCALE, True)):
                put(rows_ref, k, row)
            for i in range(at_once):
                for pair in range(pairs):
                    columns = []
                    for j in range(2):
                        own = rows_ref[pl.ds(i * beads + 2 * pair + j, PAIR_PAD, stride=lines), :]
                        spot = 2 * pair % QUAD + j
                        columns.append(
                            jnp.concatenate([own if k == spot else blank for k in range(QUAD)], axis=0)
                        )
                    near_ref[(first + block + i) * pairs + pair] = jnp.concatenate(columns, axis=1).astype(bf16)
            return inner

        lax.fori_loop(0, frame // at_once, one_own, 0)
        return carry

    lax.fori_loop(0, blocks // frame, one_frame, 0)

    def places(unit):
        block = unit // pairs
        at_frame = block // frame
        base = at_frame * width + block - at_frame * frame + margin
        return [base + offset_ref[block * listed + m] for m in range(listed)], unit - block * pairs

    def weights(ats, pair, unit, m):
        far = far_ref[ats[m], pair // (QUAD // 2)]
        weight = weigh(jnp.dot(far, near_ref[unit], preferred_element_type=f32))
        high = weight.astype(bf16)
        return high, (weight - high.astype(f32)).astype(bf16)

    def weighted(ats, pair, m, both):
        table = heavy_ref[ats[m], pair]
        return jnp.dot(jnp.concatenate([table, table], axis=1), both, preferred_element_type=f32)

    def keep(total, slot):
        for i in range(2):
            cols = slice(i * BLOCK, (i + 1) * BLOCK)
            row = i * SUM_ROWS
            spot = pl.ds(pl.multiple_of((2 * slot + i) * 8, 8), 8)
            total_ref[spot, :] = total[row:row + 8, cols] + total[row + 8:row + 16, cols]

    def whole_unit(unit):
        ats, pair = places(unit)
        keep(
            sum(weighted(ats, pair, m, jnp.concatenate(weights(ats, pair, unit, m), axis=0)) for m in range(listed)),
            unit,
        )

    def one_unit(unit, now, other):
        before = jnp.maximum(unit - 1, 0)
        ats, pair = places(unit)
        before_ats, before_pair = places(before)
        total = jnp.zeros((2 * SUM_ROWS, 2 * BLOCK), f32)
        for m in range(listed):
            spot = slice(2 * m * BLOCK, 2 * (m + 1) * BLOCK)
            weight_refs[now][spot, :] = jnp.concatenate(weights(ats, pair, unit, m), axis=0)
            total = total + weighted(before_ats, before_pair, m, weight_refs[other][spot, :])
        keep(total, jnp.where(unit == 0, units, unit - 1))

    def two_units(step, carry):
        if form == "whole":
            whole_unit(2 * step)
            whole_unit(2 * step + 1)
        else:
            one_unit(2 * step, 0, 1)
            one_unit(2 * step + 1, 1, 0)
        return carry

    lax.fori_loop(0, units // 2, two_units, 0)
    if form != "whole":
        last_ats, last_pair = places(units - 1)
        keep(
            sum(
                weighted(last_ats, last_pair, m, weight_refs[1][2 * m * BLOCK:2 * (m + 1) * BLOCK, :])
                for m in range(listed)
            ),
            units - 1,
        )

    def one_block(block, carry):
        at_frame = block // frame
        place = block - at_frame * frame + margin
        lanes = pl.ds(pl.multiple_of((block + margin) * BLOCK, BLOCK), BLOCK)
        coords = [(coord_ref[c, :, lanes] - 1.0) * SCALE for c in range(3)]
        coords[0] = coords[0] + SCALE * (place.astype(f32) - middle)
        charge = jnp.broadcast_to(SCALE * SCALE * charge_ref[:, lanes], coords[0].shape)

        def summed(c):
            return (
                total_ref[pl.ds(block * beads * 8 + c, beads, stride=8), :]
                + total_ref[pl.ds(block * beads * 8 + c + 4, beads, stride=8), :]
            )

        near = summed(0)
        own = pl.ds(pl.multiple_of(block * BLOCK, BLOCK), BLOCK)
        for c in range(3):
            force_ref[c, :, own] = charge * (coords[c] * near - summed(c + 1))
        return carry

    lax.fori_loop(0, blocks, one_block, 0)


def force_scratch(local, blocks, margin, listed):
    beads = whole_quads(local)
    frame = min(FRAME, blocks)
    tables = (frame + 2 * margin) * (blocks // frame)
    lines = max(8, beads)
    units = blocks * beads // 2
    return [
        pltpu.VMEM((3, beads, (blocks + 2 * margin) * BLOCK), f32),
        pltpu.VMEM((PAIR_PAD * lines, BLOCK), f32),
        pltpu.VMEM((SUM_ROWS * lines, BLOCK), f32),
        pltpu.VMEM((tables, beads // QUAD, BLOCK, QUAD * PAIR_PAD), bf16),
        pltpu.VMEM((tables, beads // 2, 2 * SUM_ROWS, BLOCK), bf16),
        pltpu.VMEM((units, QUAD * PAIR_PAD, 2 * BLOCK), bf16),
        pltpu.VMEM(((units + 1) * 16, BLOCK), f32),
        pltpu.VMEM((3, beads, blocks * BLOCK), f32),
        pltpu.VMEM((2 * listed * BLOCK, 2 * BLOCK), bf16),
        pltpu.VMEM((2 * listed * BLOCK, 2 * BLOCK), bf16),
    ]


def call(kernel, args, smem_count, shapes, scratch, work, in_specs=None):
    vmem = pl.BlockSpec(memory_space=pltpu.VMEM)
    smem = pl.BlockSpec(memory_space=pltpu.SMEM)
    return pl.pallas_call(
        kernel,
        out_shape=[jax.ShapeDtypeStruct(shape, f32) for shape in shapes],
        grid=() if in_specs is None else (1,),
        in_specs=in_specs or [smem] * smem_count + [vmem] * (len(args) - smem_count),
        out_specs=[vmem] * len(shapes),
        scratch_shapes=scratch,
        compiler_params=pltpu.CompilerParams(vmem_limit_bytes=(40 if in_specs is None else 62) * 1024 * 1024),
        cost_estimate=pl.CostEstimate(
            flops=20 * work + 1024, bytes_accessed=4 * 1024 * 1024, transcendentals=2 * work
        ),
    )(*args)


def row_of(c, block, blocks, local):
    return (c * blocks + block) * local


def unpack_beads(source, base, blocks, local, target, offset):
    for c in range(3):
        for block in range(blocks):
            row = row_of(base + c, block, blocks, local)
            lane = offset + block * BLOCK
            for group in range(source.shape[0]):
                target[c, group * local:(group + 1) * local, lane:lane + BLOCK] = source[group, row:row + local, :]


def pack_beads(value, c, blocks, local, target):
    for block in range(blocks):
        row = row_of(c, block, blocks, local)
        for group in range(target.shape[0]):
            target[group, row:row + local, :] = value[
                group * local:(group + 1) * local, block * BLOCK:(block + 1) * BLOCK
            ]


FORCE = 6


def clear(coord_ref, local):
    if coord_ref.shape[1] != local:
        coord_ref[...] = jnp.zeros(coord_ref.shape, f32)


def message_kernel(x_ref, p_ref, noise_ref, types_ref, offsets_ref, message_ref, charge_ref, mass_ref):
    steps = noise_ref.shape[0]
    _, local, edge = message_ref.shape
    types = types_ref[...]
    charge = jnp.zeros(types.shape, f32)
    mass = jnp.zeros(types.shape, f32)
    for kind in range(4):
        charge = jnp.where(types == kind, CHARGES[kind], charge)
        mass = jnp.where(types == kind, MASSES[kind], mass)
    charge_ref[...] = charge
    mass_ref[...] = mass
    for c in range(3):
        message_ref[c] = x_ref[c, :, :edge]
        message_ref[3 + c] = x_ref[c, :, edge:2 * edge]
        message_ref[6 + c] = p_ref[c, :, :edge]
        for step in range(steps):
            message_ref[9 + 3 * step + c] = noise_ref[step, c, :, :edge]
    at = 9 + 3 * steps
    for i, row in enumerate([charge[:, :edge], charge[:, edge:2 * edge], mass[:, :edge], offsets_ref[...]]):
        message_ref[at + i] = jnp.broadcast_to(row, (local, edge))


def pack_kernel(blocks, x_ref, noise_ref, message_ref, out_ref):
    steps = noise_ref.shape[0]
    _, local, edge = message_ref.shape
    atoms = x_ref.shape[2]
    for c in range(3 + 3 * steps):
        for block in range(atoms // BLOCK):
            at = edge + block * BLOCK
            if at >= atoms:
                value = message_ref[c if c < 3 else 6 + c, :, at - atoms:at - atoms + BLOCK]
            elif c < 3:
                value = x_ref[c, :, at:at + BLOCK]
            else:
                value = noise_ref[c // 3 - 1, c % 3, :, at:at + BLOCK]
            row = row_of(c, block % blocks, blocks, local)
            out_ref[block // blocks, row:row + local, :] = value


def first_kernel(
    shares, margin, listed, offset_ref, charge_ref, x_ref, message_ref, p_ref, pout_ref, coord_ref, *scratch
):
    _, local, atoms = x_ref.shape
    blocks = atoms // BLOCK
    each = blocks // shares
    edge = margin * BLOCK
    clear(coord_ref, local)
    for c in range(3):
        coord_ref[c, :local, 0:atoms] = x_ref[c]
        for part in range(2):
            coord_ref[c, :local, atoms + part * edge:atoms + (part + 1) * edge] = message_ref[3 * part + c]
    add_forces("whole", blocks, margin, listed, offset_ref, charge_ref, coord_ref, scratch)
    force_ref = scratch[FORCE]
    for c in range(3):
        for block in range(blocks):
            lanes = slice(block * BLOCK, (block + 1) * BLOCK)
            at = block * BLOCK + edge
            if at < atoms:
                moment = p_ref[c, :, at:at + BLOCK]
            else:
                moment = message_ref[6 + c, :, at - atoms:at - atoms + BLOCK]
            row = row_of(c, block % each, each, local)
            pout_ref[block // each, row:row + local, :] = moment + half_step * force_ref[c, :local, lanes]


def last_kernel(
    margin, listed, offset_ref, charge_ref, both_ref, message_ref, xout_ref, pout_ref, coord_ref, *scratch
):
    shares = both_ref.shape[0]
    _, local, atoms = xout_ref.shape
    blocks = atoms // BLOCK
    each = blocks // shares
    edge = margin * BLOCK

    def taken(c, block):
        row = row_of(c, block % each, each, local)
        return both_ref[block // each, row:row + local, :]

    clear(coord_ref, local)
    for c in range(3):
        for part in range(2):
            coord_ref[c, :local, part * edge:(part + 1) * edge] = message_ref[3 * part + c]
        for block in range(blocks):
            at = 2 * edge + block * BLOCK
            coord_ref[c, :local, at:at + BLOCK] = taken(c, block)
        xout_ref[c] = coord_ref[c, :local, edge:edge + atoms]
    add_forces("late", blocks, margin, listed, offset_ref, charge_ref, coord_ref, scratch)
    force_ref = scratch[FORCE]
    for c in range(3):
        for block in range(blocks):
            lanes = slice(block * BLOCK, (block + 1) * BLOCK)
            moment = message_ref[6 + c, :, lanes] if block < margin else taken(3 + c, block - margin)
            pout_ref[c, :, lanes] = moment + half_step * force_ref[c, :local, lanes]


def thermostat(coords, moments, noises, mass_ref, matrix_ref, matrix_t_ref, table_ref, store):
    beads, width = moments[0].shape
    cosine, ratio, stiffness, damping, kick = [
        jnp.concatenate([table_ref[i]] * (width // BLOCK), axis=1) for i in range(5)
    ]
    mass = jnp.broadcast_to(mass_ref[...], (beads, width))
    spread = kick * jnp.sqrt(thermal * mass)
    drift = ratio / mass
    stiff = stiffness * mass
    multiply = functools.partial(jnp.dot, precision=lax.Precision.HIGHEST, preferred_element_type=f32)
    for c in range(3):
        mode_x = multiply(matrix_t_ref[...], coords[c])
        mode_p = damping * multiply(matrix_t_ref[...], moments[c]) + spread * noises[c]
        store(
            c,
            multiply(matrix_ref[...], cosine * mode_x + drift * mode_p),
            multiply(matrix_ref[...], cosine * mode_p - stiff * mode_x),
        )


def modes_kernel(
    blocks, noise_base, rest_ref, p_ref, mass_ref, matrix_ref, matrix_t_ref, table_ref,
    xout_ref, pout_ref, coord_ref, moment_ref, noise_ref,
):
    local = p_ref.shape[1] // (3 * blocks)
    unpack_beads(rest_ref, 0, blocks, local, coord_ref, 0)
    unpack_beads(p_ref, 0, blocks, local, moment_ref, 0)
    unpack_beads(rest_ref, noise_base, blocks, local, noise_ref, 0)

    def store(c, x, p):
        pack_beads(x, c, blocks, local, xout_ref)
        pack_beads(p, c, blocks, local, pout_ref)

    thermostat(
        *[[ref[c] for c in range(3)] for ref in (coord_ref, moment_ref, noise_ref)],
        mass_ref, matrix_ref, matrix_t_ref, table_ref, store,
    )


def middle_kernel(hops, blocks, listed, noise_base, joined, offset_ref, charge_ref, *refs):
    parts = 2 * hops + 1
    x_refs = refs[:parts]
    p_ref, noise_ref, mass_ref, matrix_ref, matrix_t_ref, table_ref = refs[parts:parts + 6]
    outs = refs[parts + 6:parts + (7 if joined else 8)]
    coord_ref, *scratch = refs[parts + len(outs) + 6:]
    beads = coord_ref.shape[1]
    local = beads // p_ref.shape[0]
    width = blocks * BLOCK
    for part in range(parts):
        unpack_beads(x_refs[part], 0, blocks, local, coord_ref, part * width)
    add_forces("late", blocks, hops * blocks, listed, offset_ref, charge_ref, coord_ref, scratch)
    force_ref = scratch[FORCE]
    unpack_beads(p_ref, 0, blocks, local, coord_ref, 0)
    unpack_beads(noise_ref, noise_base, blocks, local, coord_ref, (parts - 1) * width)

    def share(c, part):
        return coord_ref[c, :, part * width:(part + 1) * width]

    def store(c, x, p):
        pack_beads(x, c, blocks, local, outs[0])
        if joined:
            pack_beads(p, 3 + c, blocks, local, outs[0])
        else:
            pack_beads(p, c, blocks, local, outs[1])

    thermostat(
        [share(c, hops) for c in range(3)],
        [share(c, 0) + 2.0 * half_step * force_ref[c] for c in range(3)],
        [share(c, parts - 1) for c in range(3)],
        mass_ref, matrix_ref, matrix_t_ref, table_ref, store,
    )


def fold(count):
    return [i // 2 if i % 2 == 0 else count - 1 - i // 2 for i in range(count)]


def exchange(pieces):
    order = fold(pieces.shape[0])
    group = [order.index(at) for at in range(len(order))]
    return lax.all_to_all(pieces, "bead", split_axis=0, concat_axis=0, axis_index_groups=[group], tiled=True)


def passed(values, step):
    count = lax.axis_size("space")
    return lax.ppermute(values, "space", [(i, (i + step) % count) for i in range(count)])


def window(values, hops):
    count = lax.axis_size("bead")
    domains = lax.axis_size("space")
    order = fold(count)
    device = {}
    for bead in range(count):
        for domain in range(domains):
            device[domain * count + order[bead]] = bead * domains + domain
    total = count * domains
    out = []
    for hop in range(-hops, hops + 1):
        if hop == 0:
            out.append(values)
        else:
            route = [(device[(at + hop) % total], device[at]) for at in range(total)]
            out.append(lax.ppermute(values, ("bead", "space"), route))
    return out


def body(positions, momenta, atom_types, neighbours, thermal_noise):
    count = lax.axis_size("bead")
    _, local, atoms = positions.shape
    beads = local * count
    domain = atoms // BLOCK
    blocks = domain // count
    share = blocks * BLOCK
    hops = -(-HALO // blocks)
    margin = hops * blocks
    edge = margin * BLOCK
    steps = thermal_noise.shape[0]
    listed = neighbours.shape[1]
    order = fold(count)

    own = lax.axis_index("space") * domain + jnp.arange(domain, dtype=jnp.int32)
    offsets = jnp.clip(neighbours - own[:, None], -margin, margin).reshape(-1)
    sent = jnp.pad(offsets[:margin * listed].astype(f32), (0, edge - margin * listed))[None, :]

    message, charge, mass = call(
        message_kernel, (positions, momenta, thermal_noise, atom_types[None, :], sent), 0,
        [(13 + 3 * steps, local, edge), (1, atoms), (1, atoms)], [], 0,
        [
            pl.BlockSpec(shape, lambda i, rank=len(shape): (0,) * rank)
            for shape in (
                (3, local, 2 * edge), (3, local, edge), (steps, 3, local, edge), (1, atoms), (1, edge)
            )
        ],
    )
    message = passed(message, -1)
    side = message[9 + 3 * steps:, 0]
    first_charge = jnp.concatenate([charge, side[:1], side[1:2]], axis=1)
    moved_mass = jnp.concatenate([mass[0, edge:], side[2]])
    moved_offsets = jnp.concatenate([offsets[margin * listed:], side[3, :margin * listed].astype(jnp.int32)])
    (rest,) = call(
        functools.partial(pack_kernel, blocks), (positions, thermal_noise, message), 0,
        [(count, (3 + 3 * steps) * blocks * local, BLOCK)], [], 0,
    )
    rest = exchange(rest)

    place = jnp.asarray(np.array(order, np.int32))[lax.axis_index("bead")]
    near_charge = lax.dynamic_slice_in_dim(first_charge, place * share, share + 2 * edge, axis=1)
    near_mass = lax.dynamic_slice_in_dim(moved_mass, place * share, share)[None, :]
    near_offsets = lax.dynamic_slice_in_dim(moved_offsets, place * blocks * listed, blocks * listed)

    matrix, tables = mode_constants(beads)
    at = np.concatenate([order.index(g) * local + np.arange(local) for g in range(count)])
    matrix = matrix[at][:, at]
    fixed = (near_mass, jnp.asarray(matrix), jnp.asarray(np.ascontiguousarray(matrix.T)), jnp.asarray(tables[:, at]))

    packed = (count, 3 * blocks * local, BLOCK)
    pairs = beads * blocks * listed * BLOCK * BLOCK
    (moment,) = call(
        functools.partial(first_kernel, count, margin, listed),
        (moved_offsets, first_charge, positions, message, momenta), 1, [packed],
        force_scratch(local, domain, margin, listed), pairs,
    )
    moment, rest = lax.optimization_barrier((moment, rest))
    coords, moment = call(
        functools.partial(modes_kernel, blocks, 3), (rest, exchange(moment)) + fixed, 0, [packed] * 2,
        [pltpu.VMEM((3, beads, share), f32)] * 3, 0,
    )
    for step in range(1, steps):
        joined = step == steps - 1
        out = call(
            functools.partial(middle_kernel, hops, blocks, listed, 3 * step + 3, joined),
            (near_offsets, near_charge) + tuple(window(coords, hops)) + (moment, rest) + fixed, 1,
            [(count, 6 * blocks * local, BLOCK)] if joined else [packed] * 2,
            force_scratch(beads, blocks, margin, listed), pairs,
        )
        if not joined:
            coords, moment = out
    both = exchange(out[0])

    def ends(low, c):
        pieces = both[low:low + hops, c * packed[1]:(c + 1) * packed[1]]
        return pieces.reshape(hops, 3, blocks, local, BLOCK).transpose(1, 3, 0, 2, 4).reshape(3, local, edge)

    message = passed(jnp.concatenate([
        ends(count - 2 * hops, 0), ends(count - hops, 0), ends(count - hops, 1),
        jnp.broadcast_to(charge[:, None, atoms - edge:], (1, local, edge)),
    ], axis=0), 1)
    last_charge = jnp.concatenate([message[9, 0], first_charge[0, :atoms + edge]])[None, :]
    return tuple(call(
        functools.partial(last_kernel, margin, listed), (offsets, last_charge, both, message), 1,
        [(3, local, atoms)] * 2, force_scratch(local, domain, margin, listed), pairs,
    ))


def solution(mesh):
    placed = (
        P(None, "bead", "space"),
        P(None, "bead", "space"),
        P("space"),
        P("space", None),
        P(None, None, "bead", "space"),
    )
    return jax.shard_map(
        body,
        mesh=mesh,
        in_specs=placed,
        out_specs=(P(None, "bead", "space"), P(None, "bead", "space")),
        check_vma=False,
    )
```

profile of v0, /device:TPU:0, one launch (start us, length us, event | category | flops | bytes accessed | tf_op | source)
XLA Modules:
  0.0 151.7 jit_solution(14509633385695085442)
XLA Ops:
  0.6 0.0 copy-start.8
  0.7 0.7 copy-done.8
  1.3 0.1 copy.17
  1.4 0.1 convert_element_type.15
  1.5 0.6 pad.4
  2.1 0.0 copy-start
  2.1 1.6 %shard_map.104 = (f32[19,4,512]{2,1,0:T(4,128)}, f32[1,4096]{1,0:T(1,128)}, f32[1,4096]{1,0:T(1,128)}) custom-call(f32[3,4,4096]{2,1,0:T(4,128)} %x_ref.5, f32[3,4,4096]{2,1,0:T(4,128)} %p_ref.3, f32[2,3,4,4096]{3,2,1,0:T(4,128)} %noise_ref.3, s32[1,4096]{1,0:T(1,128)} %bitcast.45, f32[1,512]{1,0:T(1,128)} %bitcast.46), custom_call_target="tpu_custom_call" | custom-call | flops 1024 | bytes 4194304 | tf_op jit(solution)/shard_map/pallas_call | solution.py:294
  3.7 3.9 %collective-permute-start = (f32[19,4,512]{2,1,0:T(4,128)}, f32[19,4,512]{2,1,0:T(4,128)S(1)}, u32[]{:S(2)}, u32[]{:S(2)}) collective-permute-start(f32[19,4,512]{2,1,0:T(4,128)} %get-tuple-element.9), channel_id=1, source_target_pairs={{0,3},{1,0},{2,1},{3,2},{4,7},{5,4},{6,5},{7,6},{8,11},{9,8},{10,9... | collective-permute-start | bytes 466952 | tf_op jit(solution)/shard_map/ppermute | solution.py:518
  7.6 0.1 slice.55
  7.7 0.1 copy.16
  7.8 0.1 slice.56
  7.9 3.3 %collective-permute-done.message_ref = f32[19,4,512]{2,1,0:T(4,128)S(1)} collective-permute-done((f32[19,4,512]{2,1,0:T(4,128)}, f32[19,4,512]{2,1,0:T(4,128)S(1)}, u32[]{:S(2)}, u32[]{:S(2)}) %collective-permute-start) | collective-permute-done | bytes 155680 | tf_op jit(solution)/shard_map/ppermute | solution.py:518
  11.2 0.0 copy-done
  11.2 0.0 copy-done.1
  11.3 0.9 shard_map.106
  12.1 5.0 %all-to-all-start = ((f32[8,144,128]{2,1,0:T(8,128)}), f32[8,144,128]{2,1,0:T(8,128)S(1)}, u32[]{:S(2)}, u32[]{:S(2)}) async-start(f32[8,144,128]{2,1,0:T(8,128)} %shard_map.106), calls=%async_computation | async-start | bytes 1179648 | tf_op jit(solution)/shard_map/all_to_all | solution.py:513
  17.1 0.1 pad_add_fusion.offset_ref
  17.2 0.6 copy-done.6
  17.9 0.0 copy-done.2
  17.9 0.0 copy-start.9
  17.9 0.0 copy-start.5
  17.9 30.7 %shard_map.105 = f32[8,48,128]{2,1,0:T(8,128)} custom-call(s32[160]{0:T(256)S(1)} %pad_add_fusion.offset_ref, f32[1,5120]{1,0:T(1,128)S(1)} %pad_maximum_fusion.1.charge_ref, f32[3,4,4096]{2,1,0:T(4,128)S(1)} %copy-done.1, f32[19,4,512]{2,1,0:T(4,128)S(1)} %collective-permute-done.message_ref, f32[3,4,4096]{2,1,0:T(4,128)S(1)} %copy-done.2), custom_call_target="tpu_custom_call" | custom-call | flops 209716224 | bytes 4194304 | tf_op jit(solution)/shard_map/pallas_call | solution.py:294
  48.6 0.0 all-to-all-done.rest_ref.refs_4_
  48.6 5.2 %all-to-all-start.1 = ((f32[8,48,128]{2,1,0:T(8,128)}), f32[8,48,128]{2,1,0:T(8,128)S(1)}, u32[]{:S(2)}, u32[]{:S(2)}) async-start(f32[8,48,128]{2,1,0:T(8,128)} %shard_map.105), calls=%async_computation.1 | async-start | bytes 393216 | tf_op jit(solution)/shard_map/all_to_all | solution.py:513
  53.8 0.0 copy-done.9
  53.8 0.6 dynamic_slice.12
  55.7 0.0 copy-done.7
  55.8 0.0 copy-start.4
  55.8 0.1 dynamic_slice.13.offset_ref
  55.9 0.1 fusion
  56.0 5.8 %all-to-all-done.1.p_ref = f32[8,48,128]{2,1,0:T(8,128)S(1)} async-done(((f32[8,48,128]{2,1,0:T(8,128)}), f32[8,48,128]{2,1,0:T(8,128)S(1)}, u32[]{:S(2)}, u32[]{:S(2)}) %all-to-all-start.1) | async-done | bytes 196640 | tf_op jit(solution)/shard_map/all_to_all | solution.py:513
  61.8 0.0 copy-done.5
  61.8 0.0 copy-done.3
  61.8 0.0 copy-done.4
  61.8 1.2 shard_map.107
  63.0 0.1 collective-permute-start.1
  63.1 3.0 %collective-permute-start.2 = (f32[8,48,128]{2,1,0:T(8,128)S(1)}, f32[8,48,128]{2,1,0:T(8,128)S(1)}, u32[]{:S(2)}, u32[]{:S(2)}) collective-permute-start(f32[8,48,128]{2,1,0:T(8,128)S(1)} %get-tuple-element.14.refs_1_), channel_id=1, source_target_pairs={{8,0},{16,8},{24,16},{28,24},{20,28},{12,20},{4,12},{1,4},{9,1},{1... | collective-permute-start | bytes 589832 | tf_op jit(solution)/shard_map/ppermute | solution.py:536
  66.1 3.3 %collective-permute-done.1.refs_0_ = f32[8,48,128]{2,1,0:T(8,128)S(1)} collective-permute-done((f32[8,48,128]{2,1,0:T(8,128)S(1)}, f32[8,48,128]{2,1,0:T(8,128)S(1)}, u32[]{:S(2)}, u32[]{:S(2)}) %collective-permute-start.1) | collective-permute-done | bytes 196640 | tf_op jit(solution)/shard_map/ppermute | solution.py:536
  69.4 0.7 collective-permute-done.2.refs_2_
  70.1 32.3 %shard_map.108 = f32[8,96,128]{2,1,0:T(8,128)} custom-call(s32[20]{0:T(128)S(1)} %dynamic_slice.13.offset_ref, f32[1,1536]{1,0:T(1,128)S(1)} %constant_dynamic-slice_fusion.charge_ref, f32[8,48,128]{2,1,0:T(8,128)S(1)} %collective-permute-done.1.refs_0_, f32[8,48,128]{2,1,0:T(8,128)S(1)} %get-tuple-element.14.refs_1_, ...), custom_call_target="tpu_custom_call" | custom-call | flops 209716224 | bytes 4194304 | tf_op jit(solution)/shard_map/pallas_call | solution.py:294
  102.5 3.5 %all-to-all-start.2 = ((f32[8,96,128]{2,1,0:T(8,128)}), f32[8,96,128]{2,1,0:T(8,128)S(1)}, u32[]{:S(2)}, u32[]{:S(2)}) async-start(f32[8,96,128]{2,1,0:T(8,128)} %shard_map.108), calls=%async_computation.2 | async-start | bytes 786432 | tf_op jit(solution)/shard_map/all_to_all | solution.py:513
  105.9 10.9 %all-to-all-done.2.both_ref = f32[8,96,128]{2,1,0:T(8,128)S(1)} async-done(((f32[8,96,128]{2,1,0:T(8,128)}), f32[8,96,128]{2,1,0:T(8,128)S(1)}, u32[]{:S(2)}, u32[]{:S(2)}) %all-to-all-start.2) | async-done | bytes 393248 | tf_op jit(solution)/shard_map/all_to_all | solution.py:513
  117.0 2.2 %collective-permute-start.3 = (f32[10,4,512]{2,1,0:T(4,128)S(1)}, f32[10,4,512]{2,1,0:T(4,128)S(1)}, u32[]{:S(2)}, u32[]{:S(2)}) collective-permute-start(f32[10,4,512]{2,1,0:T(4,128)S(1)} %pad_maximum_fusion), channel_id=1, source_target_pairs={{0,1},{1,2},{2,3},{3,0},{4,5},{5,6},{6,7},{7,4},{8,9},{9,10},{10,1... | collective-permute-start | bytes 245768 | tf_op jit(solution)/shard_map/ppermute | solution.py:518
  119.3 0.1 copy.15
  119.3 0.1 reshape.44.offset_ref
  119.4 0.1 maximum_reduce_fusion
  119.5 3.9 %collective-permute-done.3.message_ref = f32[10,4,512]{2,1,0:T(4,128)S(1)} collective-permute-done((f32[10,4,512]{2,1,0:T(4,128)S(1)}, f32[10,4,512]{2,1,0:T(4,128)S(1)}, u32[]{:S(2)}, u32[]{:S(2)}) %collective-permute-start.3) | collective-permute-done | bytes 81952 | tf_op jit(solution)/shard_map/ppermute | solution.py:518
  123.4 28.3 %shard_map.109 = (f32[3,4,4096]{2,1,0:T(4,128)}, f32[3,4,4096]{2,1,0:T(4,128)}) custom-call(s32[160]{0:T(256)S(1)} %reshape.44.offset_ref, f32[1,5120]{1,0:T(1,128)S(1)} %bitcast.36, f32[8,96,128]{2,1,0:T(8,128)S(1)} %all-to-all-done.2.both_ref, f32[10,4,512]{2,1,0:T(4,128)S(1)} %collective-permute-done.3.message_ref), custom_call_target="tpu_custom_call" | custom-call | flops 209716224 | bytes 4194304 | tf_op jit(solution)/shard_map/pallas_call | solution.py:294
  (27 shorter events, 0.2 us)
Async XLA Ops:
  0.6 0.7 copy-start.8
  2.1 9.1 %copy-start = (f32[2,3,4,4096]{3,2,1,0:T(4,128)S(1)}, f32[2,3,4,4096]{3,2,1,0:T(4,128)}, u32[]{:S(2)}) copy-start(f32[2,3,4,4096]{3,2,1,0:T(4,128)} %noise_ref.3) | copy-start | bytes 1179652
  2.1 9.1 %copy-start.1 = (f32[3,4,4096]{2,1,0:T(4,128)S(1)}, f32[3,4,4096]{2,1,0:T(4,128)}, u32[]{:S(2)}) copy-start(f32[3,4,4096]{2,1,0:T(4,128)} %x_ref.5) | copy-start | bytes 589828
  3.7 7.5 %collective-permute-start = (f32[19,4,512]{2,1,0:T(4,128)}, f32[19,4,512]{2,1,0:T(4,128)S(1)}, u32[]{:S(2)}, u32[]{:S(2)}) collective-permute-start(f32[19,4,512]{2,1,0:T(4,128)} %get-tuple-element.9), channel_id=1, source_target_pairs={{0,3},{1,0},{2,1},{3,2},{4,7},{5,4},{6,5},{7,6},{8,11},{9,8},{10,9... | collective-permute-start | bytes 466952 | tf_op jit(solution)/shard_map/ppermute | solution.py:518
  12.1 5.8 %copy-start.2 = (f32[3,4,4096]{2,1,0:T(4,128)S(1)}, f32[3,4,4096]{2,1,0:T(4,128)}, u32[]{:S(2)}) copy-start(f32[3,4,4096]{2,1,0:T(4,128)} %p_ref.3) | copy-start | bytes 589828
  12.1 36.5 %all-to-all-start = ((f32[8,144,128]{2,1,0:T(8,128)}), f32[8,144,128]{2,1,0:T(8,128)S(1)}, u32[]{:S(2)}, u32[]{:S(2)}) async-start(f32[8,144,128]{2,1,0:T(8,128)} %shard_map.106), calls=%async_computation | async-start | bytes 1179648 | tf_op jit(solution)/shard_map/all_to_all | solution.py:513
  17.1 0.7 copy-start.6
  17.9 35.9 %copy-start.9 = (s32[8]{0:T(128)S(1)}, s32[8]{0:T(128)}, u32[]{:S(2)}) copy-start(s32[8]{0:T(128)} %constant.42.clone) | copy-start | bytes 100
  17.9 43.9 %copy-start.5 = (f32[32,32]{1,0:T(8,128)S(1)}, f32[32,32]{1,0:T(8,128)}, u32[]{:S(2)}) copy-start(f32[32,32]{1,0:T(8,128)} %constant.44.clone.matrix_t_ref.refs_7_) | copy-start | bytes 12292
  48.6 7.2 %copy-start.7 = (f32[1,4096]{1,0:T(1,128)S(1)}, f32[1,4096]{1,0:T(1,128)}, u32[]{:S(2)}) copy-start(f32[1,4096]{1,0:T(1,128)} %get-tuple-element.13) | copy-start | bytes 49156
  48.6 13.2 %all-to-all-start.1 = ((f32[8,48,128]{2,1,0:T(8,128)}), f32[8,48,128]{2,1,0:T(8,128)S(1)}, u32[]{:S(2)}, u32[]{:S(2)}) async-start(f32[8,48,128]{2,1,0:T(8,128)} %shard_map.105), calls=%async_computation.1 | async-start | bytes 393216 | tf_op jit(solution)/shard_map/all_to_all | solution.py:513
  53.8 8.0 %copy-start.3 = (f32[5,32,128]{2,1,0:T(8,128)S(1)}, f32[5,32,128]{2,1,0:T(8,128)}, u32[]{:S(2)}) copy-start(f32[5,32,128]{2,1,0:T(8,128)} %constant.45.clone.table_ref.refs_8_) | copy-start | bytes 245764
  55.8 6.0 %copy-start.4 = (f32[32,32]{1,0:T(8,128)S(1)}, f32[32,32]{1,0:T(8,128)}, u32[]{:S(2)}) copy-start(f32[32,32]{1,0:T(8,128)} %constant.43.clone.matrix_ref.refs_6_) | copy-start | bytes 12292
  63.0 6.4 %collective-permute-start.1 = (f32[8,48,128]{2,1,0:T(8,128)S(1)}, f32[8,48,128]{2,1,0:T(8,128)S(1)}, u32[]{:S(2)}, u32[]{:S(2)}) collective-permute-start(f32[8,48,128]{2,1,0:T(8,128)S(1)} %get-tuple-element.14.refs_1_), channel_id=1, source_target_pairs={{7,0},{0,8},{8,16},{16,24},{24,28},{28,20},{20,12},{12,4},{4,1},{1... | collective-permute-start | bytes 589832 | tf_op jit(solution)/shard_map/ppermute | solution.py:536
  63.1 7.0 %collective-permute-start.2 = (f32[8,48,128]{2,1,0:T(8,128)S(1)}, f32[8,48,128]{2,1,0:T(8,128)S(1)}, u32[]{:S(2)}, u32[]{:S(2)}) collective-permute-start(f32[8,48,128]{2,1,0:T(8,128)S(1)} %get-tuple-element.14.refs_1_), channel_id=1, source_target_pairs={{8,0},{16,8},{24,16},{28,24},{20,28},{12,20},{4,12},{1,4},{9,1},{1... | collective-permute-start | bytes 589832 | tf_op jit(solution)/shard_map/ppermute | solution.py:536
  102.5 14.4 %all-to-all-start.2 = ((f32[8,96,128]{2,1,0:T(8,128)}), f32[8,96,128]{2,1,0:T(8,128)S(1)}, u32[]{:S(2)}, u32[]{:S(2)}) async-start(f32[8,96,128]{2,1,0:T(8,128)} %shard_map.108), calls=%async_computation.2 | async-start | bytes 786432 | tf_op jit(solution)/shard_map/all_to_all | solution.py:513
  117.0 6.4 %collective-permute-start.3 = (f32[10,4,512]{2,1,0:T(4,128)S(1)}, f32[10,4,512]{2,1,0:T(4,128)S(1)}, u32[]{:S(2)}, u32[]{:S(2)}) collective-permute-start(f32[10,4,512]{2,1,0:T(4,128)S(1)} %pad_maximum_fusion), channel_id=1, source_target_pairs={{0,1},{1,2},{2,3},{3,0},{4,5},{5,6},{6,7},{7,4},{8,9},{9,10},{10,1... | collective-permute-start | bytes 245768 | tf_op jit(solution)/shard_map/ppermute | solution.py:518
where the time goes:
time: 152 us
  Pallas kernels  95 us (62%)
  waiting for transfers between devices  27.9 us (18%)
  starting transfers between devices  22.9 us (15%)
  local copies, waits for them, and re-layouts  3.4 us (2%)
  between operations  2.15 us (1%)
    pallas_call x6, Pallas kernels, call(): pl.pallas_call(kernel, out_shape=[jax.ShapeDtypeStruct(shape, f32) for sh...  95 us
    all_to_all x3, waiting for transfers between devices, exchange(): lax.all_to_all(pieces, 'bead', split_axis=0, concat_axis=0, axis_index_gr...  16.7 us
    all_to_all x3, starting transfers between devices, exchange(): lax.all_to_all(pieces, 'bead', split_axis=0, concat_axis=0, axis_index_gr...  13.7 us
    ppermute x2, waiting for transfers between devices, passed(): lax.ppermute(values, 'space', [(i, (i + step) % count) for i in range(cou...  7.23 us
    ppermute x2, starting transfers between devices, passed(): lax.ppermute(values, 'space', [(i, (i + step) % count) for i in range(cou...  6.14 us
    ppermute x2, waiting for transfers between devices, window(): out.append(lax.ppermute(values, ('bead', 'space'), route))  3.98 us
    ppermute x2, starting transfers between devices, window(): out.append(lax.ppermute(values, ('bead', 'space'), route))  3.1 us
  transfers between devices with their start and end apart: 7, of which 6 were waited for; matrix products, arithmetic and copies ran while one was open for 1% of the time, Pallas kernels for 20%

commit v1 on v0

--- a/solution.py
+++ b/solution.py
@@ -26,6 +26,7 @@
 PAIR_PAD = 32
 SUM_ROWS = 16
 QUAD = 4
+PASS = 32
 FRAME = 8
 f32 = jnp.float32
 bf16 = jnp.bfloat16
@@ -96,7 +97,7 @@
 
 def add_forces(form, blocks, margin, listed, offset_ref, charge_ref, coord_ref, scratch):
     rows_ref, sums_ref, far_ref, heavy_ref, near_ref, total_ref, force_ref, *buffers = scratch
-    weight_refs = buffers
+    square_refs, weight_refs = buffers[:2], buffers[2:]
     beads = coord_ref.shape[1]
     pairs = beads // 2
     frame = min(FRAME, blocks)
@@ -190,14 +191,16 @@
         base = at_frame * width + block - at_frame * frame + margin
         return [base + offset_ref[block * listed + m] for m in range(listed)], unit - block * pairs
 
-    def weights(ats, pair, unit, m):
-        far = far_ref[ats[m], pair // (QUAD // 2)]
-        weight = weigh(jnp.dot(far, near_ref[unit], preferred_element_type=f32))
+    def parts(square):
+        weight = weigh(square)
         high = weight.astype(bf16)
         return high, (weight - high.astype(f32)).astype(bf16)
 
-    def weighted(ats, pair, m, both):
-        table = heavy_ref[ats[m], pair]
+    def squares(ats, pair, unit, m):
+        return jnp.dot(far_ref[ats[m], pair // (QUAD // 2)], near_ref[unit], preferred_element_type=f32)
+
+    def weighted(at, pair, both):
+        table = heavy_ref[at, pair]
         return jnp.dot(jnp.concatenate([table, table], axis=1), both, preferred_element_type=f32)
 
     def keep(total, slot):
@@ -206,13 +209,6 @@
             row = i * SUM_ROWS
             spot = pl.ds(pl.multiple_of((2 * slot + i) * 8, 8), 8)
             total_ref[spot, :] = total[row:row + 8, cols] + total[row + 8:row + 16, cols]
-
-    def whole_unit(unit):
-        ats, pair = places(unit)
-        keep(
-            sum(weighted(ats, pair, m, jnp.concatenate(weights(ats, pair, unit, m), axis=0)) for m in range(listed)),
-            unit,
-        )
 
     def one_unit(unit, now, other):
         before = jnp.maximum(unit - 1, 0)
@@ -221,29 +217,66 @@
         total = jnp.zeros((2 * SUM_ROWS, 2 * BLOCK), f32)
         for m in range(listed):
             spot = slice(2 * m * BLOCK, 2 * (m + 1) * BLOCK)
-            weight_refs[now][spot, :] = jnp.concatenate(weights(ats, pair, unit, m), axis=0)
-            total = total + weighted(before_ats, before_pair, m, weight_refs[other][spot, :])
+            weight_refs[now][spot, :] = jnp.concatenate(parts(squares(ats, pair, unit, m)), axis=0)
+            total = total + weighted(before_ats[m], before_pair, weight_refs[other][spot, :])
         keep(total, jnp.where(unit == 0, units, unit - 1))
 
     def two_units(step, carry):
-        if form == "whole":
-            whole_unit(2 * step)
-            whole_unit(2 * step + 1)
+        one_unit(2 * step, 0, 1)
+        one_unit(2 * step + 1, 1, 0)
+        return carry
+
+    tiles = units * listed
+
+    def tile_place(tile):
+        unit = tile // listed
+        block = unit // pairs
+        at_frame = block // frame
+        base = at_frame * width + block - at_frame * frame + margin
+        at = base + offset_ref[block * listed + tile - unit * listed]
+        return at, unit - block * pairs, unit
+
+    def tile_squares(tile, out):
+        at, pair, unit = tile_place(tile)
+        out[0:BLOCK, :] = jnp.dot(far_ref[at, pair // (QUAD // 2)], near_ref[unit], preferred_element_type=f32)
+
+    def tile_sums(tile, weight_ref, slot):
+        at, pair, _ = tile_place(tile)
+        keep(weighted(at, pair, weight_ref[0:2 * BLOCK, :]), slot)
+
+    def one_tile(tile, now, other):
+        if form == "staged":
+            tile_squares(jnp.minimum(tile + 1, tiles - 1), square_refs[other])
+            for low in range(0, BLOCK, PASS):
+                high, rest = parts(square_refs[now][low:low + PASS, :])
+                weight_refs[now][low:low + PASS, :] = high
+                weight_refs[now][BLOCK + low:BLOCK + low + PASS, :] = rest
         else:
-            one_unit(2 * step, 0, 1)
-            one_unit(2 * step + 1, 1, 0)
+            at, pair, unit = tile_place(tile)
+            square = jnp.dot(far_ref[at, pair // (QUAD // 2)], near_ref[unit], preferred_element_type=f32)
+            weight_refs[now][0:2 * BLOCK, :] = jnp.concatenate(parts(square), axis=0)
+        tile_sums(jnp.maximum(tile - 1, 0), weight_refs[other], jnp.where(tile == 0, tiles, tile - 1))
+
+    def two_tiles(step, carry):
+        one_tile(2 * step, 0, 1)
+        one_tile(2 * step + 1, 1, 0)
         return carry
 
-    lax.fori_loop(0, units // 2, two_units, 0)
-    if form != "whole":
+    if form == "late":
+        lax.fori_loop(0, units // 2, two_units, 0)
         last_ats, last_pair = places(units - 1)
         keep(
             sum(
-                weighted(last_ats, last_pair, m, weight_refs[1][2 * m * BLOCK:2 * (m + 1) * BLOCK, :])
+                weighted(last_ats[m], last_pair, weight_refs[1][2 * m * BLOCK:2 * (m + 1) * BLOCK, :])
                 for m in range(listed)
             ),
             units - 1,
         )
+    else:
+        if form == "staged":
+            tile_squares(0, square_refs[0])
+        lax.fori_loop(0, tiles // 2, two_tiles, 0)
+        tile_sums(tiles - 1, weight_refs[1], tiles - 1)
 
     def one_block(block, carry):
         at_frame = block // frame
@@ -254,10 +287,17 @@
         charge = jnp.broadcast_to(SCALE * SCALE * charge_ref[:, lanes], coords[0].shape)
 
         def summed(c):
-            return (
-                total_ref[pl.ds(block * beads * 8 + c, beads, stride=8), :]
-                + total_ref[pl.ds(block * beads * 8 + c + 4, beads, stride=8), :]
-            )
+            if form == "late":
+                return sum(total_ref[pl.ds(block * beads * 8 + c + i, beads, stride=8), :] for i in (0, 4))
+            low = block * pairs * listed * 16
+            halves = [
+                sum(
+                    total_ref[pl.ds(low + m * 16 + bead * 8 + c + i, pairs, stride=listed * 16), :]
+                    for m in range(listed) for i in (0, 4)
+                )
+                for bead in range(2)
+            ]
+            return jnp.stack(halves, axis=1).reshape(beads, BLOCK)
 
         near = summed(0)
         own = pl.ds(pl.multiple_of(block * BLOCK, BLOCK), BLOCK)
@@ -281,8 +321,10 @@
         pltpu.VMEM((tables, beads // QUAD, BLOCK, QUAD * PAIR_PAD), bf16),
         pltpu.VMEM((tables, beads // 2, 2 * SUM_ROWS, BLOCK), bf16),
         pltpu.VMEM((units, QUAD * PAIR_PAD, 2 * BLOCK), bf16),
-        pltpu.VMEM(((units + 1) * 16, BLOCK), f32),
+        pltpu.VMEM(((units * listed + 1) * 16, BLOCK), f32),
         pltpu.VMEM((3, beads, blocks * BLOCK), f32),
+        pltpu.VMEM((BLOCK, 2 * BLOCK), f32),
+        pltpu.VMEM((BLOCK, 2 * BLOCK), f32),
         pltpu.VMEM((2 * listed * BLOCK, 2 * BLOCK), bf16),
         pltpu.VMEM((2 * listed * BLOCK, 2 * BLOCK), bf16),
     ]
@@ -386,7 +428,7 @@
         coord_ref[c, :local, 0:atoms] = x_ref[c]
         for part in range(2):
             coord_ref[c, :local, atoms + part * edge:atoms + (part + 1) * edge] = message_ref[3 * part + c]
-    add_forces("whole", blocks, margin, listed, offset_ref, charge_ref, coord_ref, scratch)
+    add_forces("staged", blocks, margin, listed, offset_ref, charge_ref, coord_ref, scratch)
     force_ref = scratch[FORCE]
     for c in range(3):
         for block in range(blocks):
@@ -421,7 +463,7 @@
             at = 2 * edge + block * BLOCK
             coord_ref[c, :local, at:at + BLOCK] = taken(c, block)
         xout_ref[c] = coord_ref[c, :local, edge:edge + atoms]
-    add_forces("late", blocks, margin, listed, offset_ref, charge_ref, coord_ref, scratch)
+    add_forces("straight", blocks, margin, listed, offset_ref, charge_ref, coord_ref, scratch)
     force_ref = scratch[FORCE]
     for c in range(3):
         for block in range(blocks):

time: 152 us -> 198 us (1.30)
  Pallas kernels: 95 us -> 141 us
    pallas_call x6, Pallas kernels: 95 us -> 141 us  [call(): pl.pallas_call(kernel, out_shape=[jax.ShapeDtypeStruct(shape, f32) for sh...]
  transfers between devices with their start and end apart: 7 -> 7, of which waited for: 6 -> 6; matrix products, arithmetic and copies ran while one was open for 1% -> 1% of each run, Pallas kernels for 20% -> 22%
where the time goes in v1:
time: 198 us; the launch traced here: 197 us
  Pallas kernels  141 us (71%)
  waiting for transfers between devices  27.9 us (14%)
  starting transfers between devices  22.9 us (12%)
  local copies, waits for them, and re-layouts  3.4 us (2%)
  between operations  2.15 us (1%)
    pallas_call x6, Pallas kernels, call(): pl.pallas_call(kernel, out_shape=[jax.ShapeDtypeStruct(shape, f32) for sh...  141 us
    all_to_all x3, waiting for transfers between devices, exchange(): lax.all_to_all(pieces, 'bead', split_axis=0, concat_axis=0, axis_index_gr...  16.7 us
    all_to_all x3, starting transfers between devices, exchange(): lax.all_to_all(pieces, 'bead', split_axis=0, concat_axis=0, axis_index_gr...  13.7 us
    ppermute x2, waiting for transfers between devices, passed(): lax.ppermute(values, 'space', [(i, (i + step) % count) for i in range(cou...  7.23 us
    ppermute x2, starting transfers between devices, passed(): lax.ppermute(values, 'space', [(i, (i + step) % count) for i in range(cou...  6.14 us
    ppermute x2, waiting for transfers between devices, window(): out.append(lax.ppermute(values, ('bead', 'space'), route))  3.98 us
  transfers between devices with their start and end apart: 7, of which 6 were waited for; matrix products, arithmetic and copies ran while one was open for 1% of the time, Pallas kernels for 22%

profile of v1, /device:TPU:0, one launch (start us, length us, event | category | flops | bytes accessed | tf_op | source)
XLA Modules:
  0.0 197.5 jit_solution(8063181316361174801)
XLA Ops:
  0.6 0.0 copy-start.8
  0.7 0.7 copy-done.8
  1.3 0.1 copy.17
  1.4 0.1 convert_element_type.15
  1.5 0.6 pad.4
  2.1 0.0 copy-start
  2.1 1.6 shard_map.104
  3.7 3.9 %collective-permute-start = (f32[19,4,512]{2,1,0:T(4,128)}, f32[19,4,512]{2,1,0:T(4,128)S(1)}, u32[]{:S(2)}, u32[]{:S(2)}) collective-permute-start(f32[19,4,512]{2,1,0:T(4,128)} %get-tuple-element.9), channel_id=1, source_target_pairs={{0,3},{1,0},{2,1},{3,2},{4,7},{5,4},{6,5},{7,6},{8,11},{9,8},{10,9... | collective-permute-start | bytes 466952 | tf_op jit(solution)/shard_map/ppermute | solution.py:560
  7.6 0.1 slice.55
  7.7 0.1 copy.16
  7.8 0.1 slice.56
  7.9 3.3 %collective-permute-done.message_ref = f32[19,4,512]{2,1,0:T(4,128)S(1)} collective-permute-done((f32[19,4,512]{2,1,0:T(4,128)}, f32[19,4,512]{2,1,0:T(4,128)S(1)}, u32[]{:S(2)}, u32[]{:S(2)}) %collective-permute-start) | collective-permute-done | bytes 155680 | tf_op jit(solution)/shard_map/ppermute | solution.py:560
  11.2 0.0 copy-done
  11.2 0.0 copy-done.1
  11.3 0.9 shard_map.106
  12.1 5.0 %all-to-all-start = ((f32[8,144,128]{2,1,0:T(8,128)}), f32[8,144,128]{2,1,0:T(8,128)S(1)}, u32[]{:S(2)}, u32[]{:S(2)}) async-start(f32[8,144,128]{2,1,0:T(8,128)} %shard_map.106), calls=%async_computation | async-start | bytes 1179648 | tf_op jit(solution)/shard_map/all_to_all | solution.py:555
  17.1 0.1 pad_add_fusion.offset_ref
  17.2 0.6 copy-done.6
  17.9 0.0 copy-done.2
  17.9 0.0 copy-start.9
  17.9 0.0 copy-start.5
  17.9 43.2 %shard_map.105 = f32[8,48,128]{2,1,0:T(8,128)} custom-call(s32[160]{0:T(256)S(1)} %pad_add_fusion.offset_ref, f32[1,5120]{1,0:T(1,128)S(1)} %pad_maximum_fusion.1.charge_ref, f32[3,4,4096]{2,1,0:T(4,128)S(1)} %copy-done.1, f32[19,4,512]{2,1,0:T(4,128)S(1)} %collective-permute-done.message_ref, f32[3,4,4096]{2,1,0:T(4,128)S(1)} %copy-done.2), custom_call_target="tpu_custom_call" | custom-call | flops 209716224 | bytes 4194304 | tf_op jit(solution)/shard_map/pallas_call | solution.py:336
  61.1 0.0 all-to-all-done.rest_ref.refs_4_
  61.1 5.2 %all-to-all-start.1 = ((f32[8,48,128]{2,1,0:T(8,128)}), f32[8,48,128]{2,1,0:T(8,128)S(1)}, u32[]{:S(2)}, u32[]{:S(2)}) async-start(f32[8,48,128]{2,1,0:T(8,128)} %shard_map.105), calls=%async_computation.1 | async-start | bytes 393216 | tf_op jit(solution)/shard_map/all_to_all | solution.py:555
  66.4 0.0 copy-done.9
  66.4 0.6 dynamic_slice.12
  68.3 0.0 copy-done.7
  68.3 0.0 copy-start.4
  68.4 0.1 dynamic_slice.13.offset_ref
  68.4 0.1 fusion
  68.5 5.8 %all-to-all-done.1.p_ref = f32[8,48,128]{2,1,0:T(8,128)S(1)} async-done(((f32[8,48,128]{2,1,0:T(8,128)}), f32[8,48,128]{2,1,0:T(8,128)S(1)}, u32[]{:S(2)}, u32[]{:S(2)}) %all-to-all-start.1) | async-done | bytes 196640 | tf_op jit(solution)/shard_map/all_to_all | solution.py:555
  74.3 0.0 copy-done.5
  74.3 0.0 copy-done.3
  74.3 0.0 copy-done.4
  74.3 1.2 shard_map.107
  75.6 0.1 collective-permute-start.1
  75.6 3.0 %collective-permute-start.2 = (f32[8,48,128]{2,1,0:T(8,128)S(1)}, f32[8,48,128]{2,1,0:T(8,128)S(1)}, u32[]{:S(2)}, u32[]{:S(2)}) collective-permute-start(f32[8,48,128]{2,1,0:T(8,128)S(1)} %get-tuple-element.14.refs_1_), channel_id=1, source_target_pairs={{8,0},{16,8},{24,16},{28,24},{20,28},{12,20},{4,12},{1,4},{9,1},{1... | collective-permute-start | bytes 589832 | tf_op jit(solution)/shard_map/ppermute | solution.py:578
  78.7 3.3 %collective-permute-done.1.refs_0_ = f32[8,48,128]{2,1,0:T(8,128)S(1)} collective-permute-done((f32[8,48,128]{2,1,0:T(8,128)S(1)}, f32[8,48,128]{2,1,0:T(8,128)S(1)}, u32[]{:S(2)}, u32[]{:S(2)}) %collective-permute-start.1) | collective-permute-done | bytes 196640 | tf_op jit(solution)/shard_map/ppermute | solution.py:578
  82.0 0.7 collective-permute-done.2.refs_2_
  82.7 32.3 %shard_map.108 = f32[8,96,128]{2,1,0:T(8,128)} custom-call(s32[20]{0:T(128)S(1)} %dynamic_slice.13.offset_ref, f32[1,1536]{1,0:T(1,128)S(1)} %constant_dynamic-slice_fusion.charge_ref, f32[8,48,128]{2,1,0:T(8,128)S(1)} %collective-permute-done.1.refs_0_, f32[8,48,128]{2,1,0:T(8,128)S(1)} %get-tuple-element.14.refs_1_, ...), custom_call_target="tpu_custom_call" | custom-call | flops 209716224 | bytes 4194304 | tf_op jit(solution)/shard_map/pallas_call | solution.py:336
  115.0 3.5 %all-to-all-start.2 = ((f32[8,96,128]{2,1,0:T(8,128)}), f32[8,96,128]{2,1,0:T(8,128)S(1)}, u32[]{:S(2)}, u32[]{:S(2)}) async-start(f32[8,96,128]{2,1,0:T(8,128)} %shard_map.108), calls=%async_computation.2 | async-start | bytes 786432 | tf_op jit(solution)/shard_map/all_to_all | solution.py:555
  118.5 10.9 %all-to-all-done.2.both_ref = f32[8,96,128]{2,1,0:T(8,128)S(1)} async-done(((f32[8,96,128]{2,1,0:T(8,128)}), f32[8,96,128]{2,1,0:T(8,128)S(1)}, u32[]{:S(2)}, u32[]{:S(2)}) %all-to-all-start.2) | async-done | bytes 393248 | tf_op jit(solution)/shard_map/all_to_all | solution.py:555
  129.6 2.2 %collective-permute-start.3 = (f32[10,4,512]{2,1,0:T(4,128)S(1)}, f32[10,4,512]{2,1,0:T(4,128)S(1)}, u32[]{:S(2)}, u32[]{:S(2)}) collective-permute-start(f32[10,4,512]{2,1,0:T(4,128)S(1)} %pad_maximum_fusion), channel_id=1, source_target_pairs={{0,1},{1,2},{2,3},{3,0},{4,5},{5,6},{6,7},{7,4},{8,9},{9,10},{10,1... | collective-permute-start | bytes 245768 | tf_op jit(solution)/shard_map/ppermute | solution.py:560
  131.8 0.1 copy.15
  131.9 0.1 reshape.44.offset_ref
  132.0 0.1 maximum_reduce_fusion
  132.1 3.9 %collective-permute-done.3.message_ref = f32[10,4,512]{2,1,0:T(4,128)S(1)} collective-permute-done((f32[10,4,512]{2,1,0:T(4,128)S(1)}, f32[10,4,512]{2,1,0:T(4,128)S(1)}, u32[]{:S(2)}, u32[]{:S(2)}) %collective-permute-start.3) | collective-permute-done | bytes 81952 | tf_op jit(solution)/shard_map/ppermute | solution.py:560
  136.0 61.5 %shard_map.109 = (f32[3,4,4096]{2,1,0:T(4,128)}, f32[3,4,4096]{2,1,0:T(4,128)}) custom-call(s32[160]{0:T(256)S(1)} %reshape.44.offset_ref, f32[1,5120]{1,0:T(1,128)S(1)} %bitcast.36, f32[8,96,128]{2,1,0:T(8,128)S(1)} %all-to-all-done.2.both_ref, f32[10,4,512]{2,1,0:T(4,128)S(1)} %collective-permute-done.3.message_ref), custom_call_target="tpu_custom_call" | custom-call | flops 209716224 | bytes 4194304 | tf_op jit(solution)/shard_map/pallas_call | solution.py:336
  (27 shorter events, 0.2 us)
Async XLA Ops:
  0.6 0.7 copy-start.8
  2.1 9.1 %copy-start = (f32[2,3,4,4096]{3,2,1,0:T(4,128)S(1)}, f32[2,3,4,4096]{3,2,1,0:T(4,128)}, u32[]{:S(2)}) copy-start(f32[2,3,4,4096]{3,2,1,0:T(4,128)} %noise_ref.3) | copy-start | bytes 1179652
  2.1 9.1 %copy-start.1 = (f32[3,4,4096]{2,1,0:T(4,128)S(1)}, f32[3,4,4096]{2,1,0:T(4,128)}, u32[]{:S(2)}) copy-start(f32[3,4,4096]{2,1,0:T(4,128)} %x_ref.5) | copy-start | bytes 589828
  3.7 7.5 %collective-permute-start = (f32[19,4,512]{2,1,0:T(4,128)}, f32[19,4,512]{2,1,0:T(4,128)S(1)}, u32[]{:S(2)}, u32[]{:S(2)}) collective-permute-start(f32[19,4,512]{2,1,0:T(4,128)} %get-tuple-element.9), channel_id=1, source_target_pairs={{0,3},{1,0},{2,1},{3,2},{4,7},{5,4},{6,5},{7,6},{8,11},{9,8},{10,9... | collective-permute-start | bytes 466952 | tf_op jit(solution)/shard_map/ppermute | solution.py:560
  12.1 5.8 %copy-start.2 = (f32[3,4,4096]{2,1,0:T(4,128)S(1)}, f32[3,4,4096]{2,1,0:T(4,128)}, u32[]{:S(2)}) copy-start(f32[3,4,4096]{2,1,0:T(4,128)} %p_ref.3) | copy-start | bytes 589828
  12.1 49.0 %all-to-all-start = ((f32[8,144,128]{2,1,0:T(8,128)}), f32[8,144,128]{2,1,0:T(8,128)S(1)}, u32[]{:S(2)}, u32[]{:S(2)}) async-start(f32[8,144,128]{2,1,0:T(8,128)} %shard_map.106), calls=%async_computation | async-start | bytes 1179648 | tf_op jit(solution)/shard_map/all_to_all | solution.py:555
  17.1 0.7 copy-start.6
  17.9 48.5 %copy-start.9 = (s32[8]{0:T(128)S(1)}, s32[8]{0:T(128)}, u32[]{:S(2)}) copy-start(s32[8]{0:T(128)} %constant.42.clone) | copy-start | bytes 100
  17.9 56.4 %copy-start.5 = (f32[32,32]{1,0:T(8,128)S(1)}, f32[32,32]{1,0:T(8,128)}, u32[]{:S(2)}) copy-start(f32[32,32]{1,0:T(8,128)} %constant.44.clone.matrix_t_ref.refs_7_) | copy-start | bytes 12292
  61.1 7.1 %copy-start.7 = (f32[1,4096]{1,0:T(1,128)S(1)}, f32[1,4096]{1,0:T(1,128)}, u32[]{:S(2)}) copy-start(f32[1,4096]{1,0:T(1,128)} %get-tuple-element.13) | copy-start | bytes 49156
  61.1 13.2 %all-to-all-start.1 = ((f32[8,48,128]{2,1,0:T(8,128)}), f32[8,48,128]{2,1,0:T(8,128)S(1)}, u32[]{:S(2)}, u32[]{:S(2)}) async-start(f32[8,48,128]{2,1,0:T(8,128)} %shard_map.105), calls=%async_computation.1 | async-start | bytes 393216 | tf_op jit(solution)/shard_map/all_to_all | solution.py:555
  66.4 8.0 %copy-start.3 = (f32[5,32,128]{2,1,0:T(8,128)S(1)}, f32[5,32,128]{2,1,0:T(8,128)}, u32[]{:S(2)}) copy-start(f32[5,32,128]{2,1,0:T(8,128)} %constant.45.clone.table_ref.refs_8_) | copy-start | bytes 245764
  68.3 6.0 %copy-start.4 = (f32[32,32]{1,0:T(8,128)S(1)}, f32[32,32]{1,0:T(8,128)}, u32[]{:S(2)}) copy-start(f32[32,32]{1,0:T(8,128)} %constant.43.clone.matrix_ref.refs_6_) | copy-start | bytes 12292
  75.6 6.4 %collective-permute-start.1 = (f32[8,48,128]{2,1,0:T(8,128)S(1)}, f32[8,48,128]{2,1,0:T(8,128)S(1)}, u32[]{:S(2)}, u32[]{:S(2)}) collective-permute-start(f32[8,48,128]{2,1,0:T(8,128)S(1)} %get-tuple-element.14.refs_1_), channel_id=1, source_target_pairs={{7,0},{0,8},{8,16},{16,24},{24,28},{28,20},{20,12},{12,4},{4,1},{1... | collective-permute-start | bytes 589832 | tf_op jit(solution)/shard_map/ppermute | solution.py:578
  75.6 7.0 %collective-permute-start.2 = (f32[8,48,128]{2,1,0:T(8,128)S(1)}, f32[8,48,128]{2,1,0:T(8,128)S(1)}, u32[]{:S(2)}, u32[]{:S(2)}) collective-permute-start(f32[8,48,128]{2,1,0:T(8,128)S(1)} %get-tuple-element.14.refs_1_), channel_id=1, source_target_pairs={{8,0},{16,8},{24,16},{28,24},{20,28},{12,20},{4,12},{1,4},{9,1},{1... | collective-permute-start | bytes 589832 | tf_op jit(solution)/shard_map/ppermute | solution.py:578
  115.0 14.4 %all-to-all-start.2 = ((f32[8,96,128]{2,1,0:T(8,128)}), f32[8,96,128]{2,1,0:T(8,128)S(1)}, u32[]{:S(2)}, u32[]{:S(2)}) async-start(f32[8,96,128]{2,1,0:T(8,128)} %shard_map.108), calls=%async_computation.2 | async-start | bytes 786432 | tf_op jit(solution)/shard_map/all_to_all | solution.py:555
  129.6 6.4 %collective-permute-start.3 = (f32[10,4,512]{2,1,0:T(4,128)S(1)}, f32[10,4,512]{2,1,0:T(4,128)S(1)}, u32[]{:S(2)}, u32[]{:S(2)}) collective-permute-start(f32[10,4,512]{2,1,0:T(4,128)S(1)} %pad_maximum_fusion), channel_id=1, source_target_pairs={{0,1},{1,2},{2,3},{3,0},{4,5},{5,6},{6,7},{7,4},{8,9},{9,10},{10,1... | collective-permute-start | bytes 245768 | tf_op jit(solution)/shard_map/ppermute | solution.py:560

commit v2 on v0

--- a/solution.py
+++ b/solution.py
@@ -94,9 +94,9 @@
     return -(-beads // QUAD) * QUAD
 
 
-def add_forces(form, blocks, margin, listed, offset_ref, charge_ref, coord_ref, scratch):
+def add_forces(group, ahead, blocks, margin, listed, offset_ref, charge_ref, coord_ref, scratch):
     rows_ref, sums_ref, far_ref, heavy_ref, near_ref, total_ref, force_ref, *buffers = scratch
-    weight_refs = buffers
+    ahead_ref, *weight_refs = buffers
     beads = coord_ref.shape[1]
     pairs = beads // 2
     frame = min(FRAME, blocks)
@@ -190,14 +190,16 @@
         base = at_frame * width + block - at_frame * frame + margin
         return [base + offset_ref[block * listed + m] for m in range(listed)], unit - block * pairs
 
-    def weights(ats, pair, unit, m):
-        far = far_ref[ats[m], pair // (QUAD // 2)]
-        weight = weigh(jnp.dot(far, near_ref[unit], preferred_element_type=f32))
+    def parts(square):
+        weight = weigh(square)
         high = weight.astype(bf16)
         return high, (weight - high.astype(f32)).astype(bf16)
 
-    def weighted(ats, pair, m, both):
-        table = heavy_ref[ats[m], pair]
+    def squares(ats, pair, unit, m):
+        return jnp.dot(far_ref[ats[m], pair // (QUAD // 2)], near_ref[unit], preferred_element_type=f32)
+
+    def weighted(at, pair, both):
+        table = heavy_ref[at, pair]
         return jnp.dot(jnp.concatenate([table, table], axis=1), both, preferred_element_type=f32)
 
     def keep(total, slot):
@@ -207,43 +209,40 @@
             spot = pl.ds(pl.multiple_of((2 * slot + i) * 8, 8), 8)
             total_ref[spot, :] = total[row:row + 8, cols] + total[row + 8:row + 16, cols]
 
-    def whole_unit(unit):
+    def body(step, carry):
+        before_ats, before_pair = places(jnp.maximum(step * group - 1, 0))
+        for turn in range(group):
+            unit = step * group + turn
+            now, other = turn % 2, (turn + 1) % 2
+            ats, pair = places(unit)
+            total = jnp.zeros((2 * SUM_ROWS, 2 * BLOCK), f32)
+            for m in range(listed):
+                spot = slice(2 * m * BLOCK, 2 * (m + 1) * BLOCK)
+                square = ahead_ref[...] if ahead and turn == m == 0 else squares(ats, pair, unit, m)
+                weight_refs[now][spot, :] = jnp.concatenate(parts(square), axis=0)
+                total = total + weighted(before_ats[m], before_pair, weight_refs[other][spot, :])
+            keep(total, jnp.where(unit == 0, units, unit - 1))
+            before_ats, before_pair = ats, pair
+        if ahead:
+            look(jnp.minimum((step + 1) * group, units - 1))
+        return carry
+
+    def look(unit):
         ats, pair = places(unit)
-        keep(
-            sum(weighted(ats, pair, m, jnp.concatenate(weights(ats, pair, unit, m), axis=0)) for m in range(listed)),
-            unit,
-        )
-
-    def one_unit(unit, now, other):
-        before = jnp.maximum(unit - 1, 0)
-        ats, pair = places(unit)
-        before_ats, before_pair = places(before)
-        total = jnp.zeros((2 * SUM_ROWS, 2 * BLOCK), f32)
-        for m in range(listed):
-            spot = slice(2 * m * BLOCK, 2 * (m + 1) * BLOCK)
-            weight_refs[now][spot, :] = jnp.concatenate(weights(ats, pair, unit, m), axis=0)
-            total = total + weighted(before_ats, before_pair, m, weight_refs[other][spot, :])
-        keep(total, jnp.where(unit == 0, units, unit - 1))
-
-    def two_units(step, carry):
-        if form == "whole":
-            whole_unit(2 * step)
-            whole_unit(2 * step + 1)
-        else:
-            one_unit(2 * step, 0, 1)
-            one_unit(2 * step + 1, 1, 0)
-        return carry
-
-    lax.fori_loop(0, units // 2, two_units, 0)
-    if form != "whole":
-        last_ats, last_pair = places(units - 1)
-        keep(
-            sum(
-                weighted(last_ats, last_pair, m, weight_refs[1][2 * m * BLOCK:2 * (m + 1) * BLOCK, :])
-                for m in range(listed)
-            ),
-            units - 1,
-        )
+        ahead_ref[...] = squares(ats, pair, unit, 0)
+
+    group = math.gcd(units, group)
+    if ahead:
+        look(0)
+    lax.fori_loop(0, units // group, body, 0)
+    last_ats, last_pair = places(units - 1)
+    keep(
+        sum(
+            weighted(last_ats[m], last_pair, weight_refs[(group - 1) % 2][2 * m * BLOCK:2 * (m + 1) * BLOCK, :])
+            for m in range(listed)
+        ),
+        units - 1,
+    )
 
     def one_block(block, carry):
         at_frame = block // frame
@@ -254,10 +253,7 @@
         charge = jnp.broadcast_to(SCALE * SCALE * charge_ref[:, lanes], coords[0].shape)
 
         def summed(c):
-            return (
-                total_ref[pl.ds(block * beads * 8 + c, beads, stride=8), :]
-                + total_ref[pl.ds(block * beads * 8 + c + 4, beads, stride=8), :]
-            )
+            return sum(total_ref[pl.ds(block * beads * 8 + c + i, beads, stride=8), :] for i in (0, 4))
 
         near = summed(0)
         own = pl.ds(pl.multiple_of(block * BLOCK, BLOCK), BLOCK)
@@ -283,6 +279,7 @@
         pltpu.VMEM((units, QUAD * PAIR_PAD, 2 * BLOCK), bf16),
         pltpu.VMEM(((units + 1) * 16, BLOCK), f32),
         pltpu.VMEM((3, beads, blocks * BLOCK), f32),
+        pltpu.VMEM((BLOCK, 2 * BLOCK), f32),
         pltpu.VMEM((2 * listed * BLOCK, 2 * BLOCK), bf16),
         pltpu.VMEM((2 * listed * BLOCK, 2 * BLOCK), bf16),
     ]
@@ -386,7 +383,7 @@
         coord_ref[c, :local, 0:atoms] = x_ref[c]
         for part in range(2):
             coord_ref[c, :local, atoms + part * edge:atoms + (part + 1) * edge] = message_ref[3 * part + c]
-    add_forces("whole", blocks, margin, listed, offset_ref, charge_ref, coord_ref, scratch)
+    add_forces(4, False, blocks, margin, listed, offset_ref, charge_ref, coord_ref, scratch)
     force_ref = scratch[FORCE]
     for c in range(3):
         for block in range(blocks):
@@ -421,7 +418,7 @@
             at = 2 * edge + block * BLOCK
             coord_ref[c, :local, at:at + BLOCK] = taken(c, block)
         xout_ref[c] = coord_ref[c, :local, edge:edge + atoms]
-    add_forces("late", blocks, margin, listed, offset_ref, charge_ref, coord_ref, scratch)
+    add_forces(8, False, blocks, margin, listed, offset_ref, charge_ref, coord_ref, scratch)
     force_ref = scratch[FORCE]
     for c in range(3):
         for block in range(blocks):
@@ -480,7 +477,7 @@
     width = blocks * BLOCK
     for part in range(parts):
         unpack_beads(x_refs[part], 0, blocks, local, coord_ref, part * width)
-    add_forces("late", blocks, hops * blocks, listed, offset_ref, charge_ref, coord_ref, scratch)
+    add_forces(4, True, blocks, hops * blocks, listed, offset_ref, charge_ref, coord_ref, scratch)
     force_ref = scratch[FORCE]
     unpack_beads(p_ref, 0, blocks, local, coord_ref, 0)
     unpack_beads(noise_ref, noise_base, blocks, local, coord_ref, (parts - 1) * width)

time: 152 us -> 142 us (0.934)
  Pallas kernels: 95 us -> 84.3 us
    pallas_call x6, Pallas kernels: 95 us -> 84.3 us  [call(): pl.pallas_call(kernel, out_shape=[jax.ShapeDtypeStruct(shape, f32) for sh...]
  transfers between devices with their start and end apart: 7 -> 7, of which waited for: 6 -> 6; matrix products, arithmetic and copies ran while one was open for 1% -> 1% of each run, Pallas kernels for 20% -> 18%
where the time goes in v2:
time: 142 us; the launch traced here: 141 us
  Pallas kernels  84.3 us (59%)
  waiting for transfers between devices  27.9 us (20%)
  starting transfers between devices  22.9 us (16%)
  local copies, waits for them, and re-layouts  3.4 us (2%)
  between operations  2.15 us (2%)
    pallas_call x6, Pallas kernels, call(): pl.pallas_call(kernel, out_shape=[jax.ShapeDtypeStruct(shape, f32) for sh...  84.3 us
    all_to_all x3, waiting for transfers between devices, exchange(): lax.all_to_all(pieces, 'bead', split_axis=0, concat_axis=0, axis_index_gr...  16.7 us
    all_to_all x3, starting transfers between devices, exchange(): lax.all_to_all(pieces, 'bead', split_axis=0, concat_axis=0, axis_index_gr...  13.7 us
    ppermute x2, waiting for transfers between devices, passed(): lax.ppermute(values, 'space', [(i, (i + step) % count) for i in range(cou...  7.24 us
    ppermute x2, starting transfers between devices, passed(): lax.ppermute(values, 'space', [(i, (i + step) % count) for i in range(cou...  6.13 us
    ppermute x2, waiting for transfers between devices, window(): out.append(lax.ppermute(values, ('bead', 'space'), route))  3.97 us
    ppermute x2, starting transfers between devices, window(): out.append(lax.ppermute(values, ('bead', 'space'), route))  3.11 us
  transfers between devices with their start and end apart: 7, of which 6 were waited for; matrix products, arithmetic and copies ran while one was open for 1% of the time, Pallas kernels for 18%

profile of v2, /device:TPU:0, one launch (start us, length us, event | category | flops | bytes accessed | tf_op | source)
XLA Modules:
  0.0 141.0 jit_solution(2814947637774121794)
XLA Ops:
  0.6 0.0 copy-start.8
  0.7 0.7 copy-done.8
  1.3 0.1 copy.17
  1.4 0.1 convert_element_type.15
  1.5 0.6 pad.4
  2.1 0.0 copy-start
  2.1 1.6 %shard_map.104 = (f32[19,4,512]{2,1,0:T(4,128)}, f32[1,4096]{1,0:T(1,128)}, f32[1,4096]{1,0:T(1,128)}) custom-call(f32[3,4,4096]{2,1,0:T(4,128)} %x_ref.5, f32[3,4,4096]{2,1,0:T(4,128)} %p_ref.3, f32[2,3,4,4096]{3,2,1,0:T(4,128)} %noise_ref.3, s32[1,4096]{1,0:T(1,128)} %bitcast.45, f32[1,512]{1,0:T(1,128)} %bitcast.46), custom_call_target="tpu_custom_call" | custom-call | flops 1024 | bytes 4194304 | tf_op jit(solution)/shard_map/pallas_call | solution.py:291
  3.7 3.9 %collective-permute-start = (f32[19,4,512]{2,1,0:T(4,128)}, f32[19,4,512]{2,1,0:T(4,128)S(1)}, u32[]{:S(2)}, u32[]{:S(2)}) collective-permute-start(f32[19,4,512]{2,1,0:T(4,128)} %get-tuple-element.9), channel_id=1, source_target_pairs={{0,3},{1,0},{2,1},{3,2},{4,7},{5,4},{6,5},{7,6},{8,11},{9,8},{10,9... | collective-permute-start | bytes 466952 | tf_op jit(solution)/shard_map/ppermute | solution.py:515
  7.6 0.1 slice.55
  7.7 0.1 copy.16
  7.8 0.1 slice.56
  7.9 3.3 %collective-permute-done.message_ref = f32[19,4,512]{2,1,0:T(4,128)S(1)} collective-permute-done((f32[19,4,512]{2,1,0:T(4,128)}, f32[19,4,512]{2,1,0:T(4,128)S(1)}, u32[]{:S(2)}, u32[]{:S(2)}) %collective-permute-start) | collective-permute-done | bytes 155680 | tf_op jit(solution)/shard_map/ppermute | solution.py:515
  11.2 0.0 copy-done
  11.2 0.0 copy-done.1
  11.3 0.9 shard_map.106
  12.1 5.0 %all-to-all-start = ((f32[8,144,128]{2,1,0:T(8,128)}), f32[8,144,128]{2,1,0:T(8,128)S(1)}, u32[]{:S(2)}, u32[]{:S(2)}) async-start(f32[8,144,128]{2,1,0:T(8,128)} %shard_map.106), calls=%async_computation | async-start | bytes 1179648 | tf_op jit(solution)/shard_map/all_to_all | solution.py:510
  17.1 0.1 pad_add_fusion.offset_ref
  17.2 0.6 copy-done.6
  17.9 0.0 copy-done.2
  17.9 0.0 copy-start.9
  17.9 0.0 copy-start.5
  17.9 26.0 %shard_map.105 = f32[8,48,128]{2,1,0:T(8,128)} custom-call(s32[160]{0:T(256)S(1)} %pad_add_fusion.offset_ref, f32[1,5120]{1,0:T(1,128)S(1)} %pad_maximum_fusion.1.charge_ref, f32[3,4,4096]{2,1,0:T(4,128)S(1)} %copy-done.1, f32[19,4,512]{2,1,0:T(4,128)S(1)} %collective-permute-done.message_ref, f32[3,4,4096]{2,1,0:T(4,128)S(1)} %copy-done.2), custom_call_target="tpu_custom_call" | custom-call | flops 209716224 | bytes 4194304 | tf_op jit(solution)/shard_map/pallas_call | solution.py:291
  43.9 0.0 all-to-all-done.rest_ref.refs_4_
  43.9 5.2 %all-to-all-start.1 = ((f32[8,48,128]{2,1,0:T(8,128)}), f32[8,48,128]{2,1,0:T(8,128)S(1)}, u32[]{:S(2)}, u32[]{:S(2)}) async-start(f32[8,48,128]{2,1,0:T(8,128)} %shard_map.105), calls=%async_computation.1 | async-start | bytes 393216 | tf_op jit(solution)/shard_map/all_to_all | solution.py:510
  49.2 0.0 copy-done.9
  49.2 0.6 dynamic_slice.12
  51.1 0.0 copy-done.7
  51.1 0.0 copy-start.4
  51.1 0.1 dynamic_slice.13.offset_ref
  51.2 0.1 fusion
  51.3 5.8 %all-to-all-done.1.p_ref = f32[8,48,128]{2,1,0:T(8,128)S(1)} async-done(((f32[8,48,128]{2,1,0:T(8,128)}), f32[8,48,128]{2,1,0:T(8,128)S(1)}, u32[]{:S(2)}, u32[]{:S(2)}) %all-to-all-start.1) | async-done | bytes 196640 | tf_op jit(solution)/shard_map/all_to_all | solution.py:510
  57.1 0.0 copy-done.5
  57.1 0.0 copy-done.3
  57.1 0.0 copy-done.4
  57.1 1.2 shard_map.107
  58.4 0.1 collective-permute-start.1
  58.4 3.0 %collective-permute-start.2 = (f32[8,48,128]{2,1,0:T(8,128)S(1)}, f32[8,48,128]{2,1,0:T(8,128)S(1)}, u32[]{:S(2)}, u32[]{:S(2)}) collective-permute-start(f32[8,48,128]{2,1,0:T(8,128)S(1)} %get-tuple-element.14.refs_1_), channel_id=1, source_target_pairs={{8,0},{16,8},{24,16},{28,24},{20,28},{12,20},{4,12},{1,4},{9,1},{1... | collective-permute-start | bytes 589832 | tf_op jit(solution)/shard_map/ppermute | solution.py:533
  61.5 3.3 %collective-permute-done.1.refs_0_ = f32[8,48,128]{2,1,0:T(8,128)S(1)} collective-permute-done((f32[8,48,128]{2,1,0:T(8,128)S(1)}, f32[8,48,128]{2,1,0:T(8,128)S(1)}, u32[]{:S(2)}, u32[]{:S(2)}) %collective-permute-start.1) | collective-permute-done | bytes 196640 | tf_op jit(solution)/shard_map/ppermute | solution.py:533
  64.8 0.7 collective-permute-done.2.refs_2_
  65.4 29.9 %shard_map.108 = f32[8,96,128]{2,1,0:T(8,128)} custom-call(s32[20]{0:T(128)S(1)} %dynamic_slice.13.offset_ref, f32[1,1536]{1,0:T(1,128)S(1)} %constant_dynamic-slice_fusion.charge_ref, f32[8,48,128]{2,1,0:T(8,128)S(1)} %collective-permute-done.1.refs_0_, f32[8,48,128]{2,1,0:T(8,128)S(1)} %get-tuple-element.14.refs_1_, ...), custom_call_target="tpu_custom_call" | custom-call | flops 209716224 | bytes 4194304 | tf_op jit(solution)/shard_map/pallas_call | solution.py:291
  95.3 3.5 %all-to-all-start.2 = ((f32[8,96,128]{2,1,0:T(8,128)}), f32[8,96,128]{2,1,0:T(8,128)S(1)}, u32[]{:S(2)}, u32[]{:S(2)}) async-start(f32[8,96,128]{2,1,0:T(8,128)} %shard_map.108), calls=%async_computation.2 | async-start | bytes 786432 | tf_op jit(solution)/shard_map/all_to_all | solution.py:510
  98.8 10.9 %all-to-all-done.2.both_ref = f32[8,96,128]{2,1,0:T(8,128)S(1)} async-done(((f32[8,96,128]{2,1,0:T(8,128)}), f32[8,96,128]{2,1,0:T(8,128)S(1)}, u32[]{:S(2)}, u32[]{:S(2)}) %all-to-all-start.2) | async-done | bytes 393248 | tf_op jit(solution)/shard_map/all_to_all | solution.py:510
  109.9 2.2 %collective-permute-start.3 = (f32[10,4,512]{2,1,0:T(4,128)S(1)}, f32[10,4,512]{2,1,0:T(4,128)S(1)}, u32[]{:S(2)}, u32[]{:S(2)}) collective-permute-start(f32[10,4,512]{2,1,0:T(4,128)S(1)} %pad_maximum_fusion), channel_id=1, source_target_pairs={{0,1},{1,2},{2,3},{3,0},{4,5},{5,6},{6,7},{7,4},{8,9},{9,10},{10,1... | collective-permute-start | bytes 245768 | tf_op jit(solution)/shard_map/ppermute | solution.py:515
  112.1 0.1 copy.15
  112.2 0.1 reshape.44.offset_ref
  112.3 0.1 maximum_reduce_fusion
  112.4 3.9 %collective-permute-done.3.message_ref = f32[10,4,512]{2,1,0:T(4,128)S(1)} collective-permute-done((f32[10,4,512]{2,1,0:T(4,128)S(1)}, f32[10,4,512]{2,1,0:T(4,128)S(1)}, u32[]{:S(2)}, u32[]{:S(2)}) %collective-permute-start.3) | collective-permute-done | bytes 81952 | tf_op jit(solution)/shard_map/ppermute | solution.py:515
  116.3 24.7 %shard_map.109 = (f32[3,4,4096]{2,1,0:T(4,128)}, f32[3,4,4096]{2,1,0:T(4,128)}) custom-call(s32[160]{0:T(256)S(1)} %reshape.44.offset_ref, f32[1,5120]{1,0:T(1,128)S(1)} %bitcast.36, f32[8,96,128]{2,1,0:T(8,128)S(1)} %all-to-all-done.2.both_ref, f32[10,4,512]{2,1,0:T(4,128)S(1)} %collective-permute-done.3.message_ref), custom_call_target="tpu_custom_call" | custom-call | flops 209716224 | bytes 4194304 | tf_op jit(solution)/shard_map/pallas_call | solution.py:291
  (27 shorter events, 0.2 us)
Async XLA Ops:
  0.6 0.7 copy-start.8
  2.1 9.1 %copy-start = (f32[2,3,4,4096]{3,2,1,0:T(4,128)S(1)}, f32[2,3,4,4096]{3,2,1,0:T(4,128)}, u32[]{:S(2)}) copy-start(f32[2,3,4,4096]{3,2,1,0:T(4,128)} %noise_ref.3) | copy-start | bytes 1179652
  2.1 9.1 %copy-start.1 = (f32[3,4,4096]{2,1,0:T(4,128)S(1)}, f32[3,4,4096]{2,1,0:T(4,128)}, u32[]{:S(2)}) copy-start(f32[3,4,4096]{2,1,0:T(4,128)} %x_ref.5) | copy-start | bytes 589828
  3.7 7.5 %collective-permute-start = (f32[19,4,512]{2,1,0:T(4,128)}, f32[19,4,512]{2,1,0:T(4,128)S(1)}, u32[]{:S(2)}, u32[]{:S(2)}) collective-permute-start(f32[19,4,512]{2,1,0:T(4,128)} %get-tuple-element.9), channel_id=1, source_target_pairs={{0,3},{1,0},{2,1},{3,2},{4,7},{5,4},{6,5},{7,6},{8,11},{9,8},{10,9... | collective-permute-start | bytes 466952 | tf_op jit(solution)/shard_map/ppermute | solution.py:515
  12.1 5.8 %copy-start.2 = (f32[3,4,4096]{2,1,0:T(4,128)S(1)}, f32[3,4,4096]{2,1,0:T(4,128)}, u32[]{:S(2)}) copy-start(f32[3,4,4096]{2,1,0:T(4,128)} %p_ref.3) | copy-start | bytes 589828
  12.1 31.8 %all-to-all-start = ((f32[8,144,128]{2,1,0:T(8,128)}), f32[8,144,128]{2,1,0:T(8,128)S(1)}, u32[]{:S(2)}, u32[]{:S(2)}) async-start(f32[8,144,128]{2,1,0:T(8,128)} %shard_map.106), calls=%async_computation | async-start | bytes 1179648 | tf_op jit(solution)/shard_map/all_to_all | solution.py:510
  17.1 0.7 copy-start.6
  17.9 31.3 %copy-start.9 = (s32[8]{0:T(128)S(1)}, s32[8]{0:T(128)}, u32[]{:S(2)}) copy-start(s32[8]{0:T(128)} %constant.42.clone) | copy-start | bytes 100
  17.9 39.2 %copy-start.5 = (f32[32,32]{1,0:T(8,128)S(1)}, f32[32,32]{1,0:T(8,128)}, u32[]{:S(2)}) copy-start(f32[32,32]{1,0:T(8,128)} %constant.44.clone.matrix_t_ref.refs_7_) | copy-start | bytes 12292
  43.9 7.1 %copy-start.7 = (f32[1,4096]{1,0:T(1,128)S(1)}, f32[1,4096]{1,0:T(1,128)}, u32[]{:S(2)}) copy-start(f32[1,4096]{1,0:T(1,128)} %get-tuple-element.13) | copy-start | bytes 49156
  43.9 13.2 %all-to-all-start.1 = ((f32[8,48,128]{2,1,0:T(8,128)}), f32[8,48,128]{2,1,0:T(8,128)S(1)}, u32[]{:S(2)}, u32[]{:S(2)}) async-start(f32[8,48,128]{2,1,0:T(8,128)} %shard_map.105), calls=%async_computation.1 | async-start | bytes 393216 | tf_op jit(solution)/shard_map/all_to_all | solution.py:510
  49.1 8.0 %copy-start.3 = (f32[5,32,128]{2,1,0:T(8,128)S(1)}, f32[5,32,128]{2,1,0:T(8,128)}, u32[]{:S(2)}) copy-start(f32[5,32,128]{2,1,0:T(8,128)} %constant.45.clone.table_ref.refs_8_) | copy-start | bytes 245764
  51.1 6.0 %copy-start.4 = (f32[32,32]{1,0:T(8,128)S(1)}, f32[32,32]{1,0:T(8,128)}, u32[]{:S(2)}) copy-start(f32[32,32]{1,0:T(8,128)} %constant.43.clone.matrix_ref.refs_6_) | copy-start | bytes 12292
  58.4 6.4 %collective-permute-start.1 = (f32[8,48,128]{2,1,0:T(8,128)S(1)}, f32[8,48,128]{2,1,0:T(8,128)S(1)}, u32[]{:S(2)}, u32[]{:S(2)}) collective-permute-start(f32[8,48,128]{2,1,0:T(8,128)S(1)} %get-tuple-element.14.refs_1_), channel_id=1, source_target_pairs={{7,0},{0,8},{8,16},{16,24},{24,28},{28,20},{20,12},{12,4},{4,1},{1... | collective-permute-start | bytes 589832 | tf_op jit(solution)/shard_map/ppermute | solution.py:533
  58.4 7.0 %collective-permute-start.2 = (f32[8,48,128]{2,1,0:T(8,128)S(1)}, f32[8,48,128]{2,1,0:T(8,128)S(1)}, u32[]{:S(2)}, u32[]{:S(2)}) collective-permute-start(f32[8,48,128]{2,1,0:T(8,128)S(1)} %get-tuple-element.14.refs_1_), channel_id=1, source_target_pairs={{8,0},{16,8},{24,16},{28,24},{20,28},{12,20},{4,12},{1,4},{9,1},{1... | collective-permute-start | bytes 589832 | tf_op jit(solution)/shard_map/ppermute | solution.py:533
  95.3 14.4 %all-to-all-start.2 = ((f32[8,96,128]{2,1,0:T(8,128)}), f32[8,96,128]{2,1,0:T(8,128)S(1)}, u32[]{:S(2)}, u32[]{:S(2)}) async-start(f32[8,96,128]{2,1,0:T(8,128)} %shard_map.108), calls=%async_computation.2 | async-start | bytes 786432 | tf_op jit(solution)/shard_map/all_to_all | solution.py:510
  109.9 6.4 %collective-permute-start.3 = (f32[10,4,512]{2,1,0:T(4,128)S(1)}, f32[10,4,512]{2,1,0:T(4,128)S(1)}, u32[]{:S(2)}, u32[]{:S(2)}) collective-permute-start(f32[10,4,512]{2,1,0:T(4,128)S(1)} %pad_maximum_fusion), channel_id=1, source_target_pairs={{0,1},{1,2},{2,3},{3,0},{4,5},{5,6},{6,7},{7,4},{8,9},{9,10},{10,1... | collective-permute-start | bytes 245768 | tf_op jit(solution)/shard_map/ppermute | solution.py:515

commit v3 on v2

--- a/solution.py
+++ b/solution.py
@@ -26,6 +26,7 @@
 PAIR_PAD = 32
 SUM_ROWS = 16
 QUAD = 4
+SLOTS = 4
 FRAME = 8
 f32 = jnp.float32
 bf16 = jnp.bfloat16
@@ -94,9 +95,9 @@
     return -(-beads // QUAD) * QUAD
 
 
-def add_forces(group, ahead, blocks, margin, listed, offset_ref, charge_ref, coord_ref, scratch):
+def add_forces(group, blocks, margin, listed, offset_ref, charge_ref, coord_ref, scratch):
     rows_ref, sums_ref, far_ref, heavy_ref, near_ref, total_ref, force_ref, *buffers = scratch
-    ahead_ref, *weight_refs = buffers
+    weight_refs = buffers
     beads = coord_ref.shape[1]
     pairs = beads // 2
     frame = min(FRAME, blocks)
@@ -106,8 +107,8 @@
     lines = at_once * beads
     units = blocks * pairs
 
-    def put(ref, k, value):
-        ref[k * lines:(k + 1) * lines, :] = value
+    def put(ref, slot, k, value):
+        ref[slot, k * lines:(k + 1) * lines, :] = value
 
     def centred(block, place):
         spans = [pl.ds(pl.multiple_of((block + i) * BLOCK, BLOCK), BLOCK) for i in range(at_once)]
@@ -124,65 +125,70 @@
         )
         return coords, norm, charge
 
+    def steps(count, one):
+        slots = math.gcd(count, SLOTS)
+
+        def some(turn, carry):
+            for slot in range(slots):
+                one(turn * slots + slot, slot)
+            return carry
+
+        lax.fori_loop(0, count // slots, some, 0)
+
     nothing = jnp.zeros((lines, BLOCK), f32)
-    for k in range(PAIR_ROWS, PAIR_PAD):
-        put(rows_ref, k, nothing)
-    for k in range(12, SUM_ROWS):
-        put(sums_ref, k, nothing)
+    for slot in range(SLOTS):
+        for k in range(PAIR_ROWS, PAIR_PAD):
+            put(rows_ref, slot, k, nothing)
+        for k in range(12, SUM_ROWS):
+            put(sums_ref, slot, k, nothing)
     blank = jnp.zeros((PAIR_PAD, BLOCK), f32)
-
-    def one_frame(at_frame, carry):
-        first = at_frame * frame
-
-        def one_table(step, inner):
-            place = step * at_once
-            coords, norm, charge = centred(first + place, place)
-            for k, row in enumerate(pair_rows(coords, norm, False)):
-                put(rows_ref, k, row)
-            for c, v in enumerate([charge] + [charge * x for x in coords]):
-                for level, part in enumerate(split3(v)):
-                    put(sums_ref, level * 4 + c, part)
-            for i in range(at_once):
-                at = at_frame * width + place + i
-                for quad in range(beads // QUAD):
-                    low = i * beads + quad * QUAD
-                    four = jnp.concatenate(
-                        [rows_ref[pl.ds(low + j, PAIR_PAD, stride=lines), :] for j in range(QUAD)], axis=0
+    passes = width // at_once
+
+    def one_table(step, slot):
+        at_frame = step // passes
+        place = (step - at_frame * passes) * at_once
+        coords, norm, charge = centred(at_frame * frame + place, place)
+        for k, row in enumerate(pair_rows(coords, norm, False)):
+            put(rows_ref, slot, k, row)
+        for c, v in enumerate([charge] + [charge * x for x in coords]):
+            for level, part in enumerate(split3(v)):
+                put(sums_ref, slot, level * 4 + c, part)
+        for i in range(at_once):
+            at = at_frame * width + place + i
+            for quad in range(beads // QUAD):
+                low = i * beads + quad * QUAD
+                four = jnp.concatenate(
+                    [rows_ref[slot, pl.ds(low + j, PAIR_PAD, stride=lines), :] for j in range(QUAD)], axis=0
+                )
+                far_ref[at, quad] = jnp.transpose(four).astype(bf16)
+                for half in range(2):
+                    heavy_ref[at, 2 * quad + half] = jnp.concatenate(
+                        [
+                            sums_ref[slot, pl.ds(low + 2 * half + j, SUM_ROWS, stride=lines), :]
+                            for j in range(2)
+                        ],
+                        axis=0,
+                    ).astype(bf16)
+
+    def one_own(step, slot):
+        block = step * at_once
+        place = block - block // frame * frame + margin
+        coords, norm, _ = centred(block + margin, place)
+        for k, row in enumerate(pair_rows(coords, norm + softening * SCALE * SCALE, True)):
+            put(rows_ref, slot, k, row)
+        for i in range(at_once):
+            for pair in range(pairs):
+                columns = []
+                for j in range(2):
+                    own = rows_ref[slot, pl.ds(i * beads + 2 * pair + j, PAIR_PAD, stride=lines), :]
+                    spot = 2 * pair % QUAD + j
+                    columns.append(
+                        jnp.concatenate([own if k == spot else blank for k in range(QUAD)], axis=0)
                     )
-                    far_ref[at, quad] = jnp.transpose(four).astype(bf16)
-                    for half in range(2):
-                        heavy_ref[at, 2 * quad + half] = jnp.concatenate(
-                            [
-                                sums_ref[pl.ds(low + 2 * half + j, SUM_ROWS, stride=lines), :]
-                                for j in range(2)
-                            ],
-                            axis=0,
-                        ).astype(bf16)
-            return inner
-
-        lax.fori_loop(0, width // at_once, one_table, 0)
-
-        def one_own(step, inner):
-            block = step * at_once
-            coords, norm, _ = centred(first + margin + block, block + margin)
-            for k, row in enumerate(pair_rows(coords, norm + softening * SCALE * SCALE, True)):
-                put(rows_ref, k, row)
-            for i in range(at_once):
-                for pair in range(pairs):
-                    columns = []
-                    for j in range(2):
-                        own = rows_ref[pl.ds(i * beads + 2 * pair + j, PAIR_PAD, stride=lines), :]
-                        spot = 2 * pair % QUAD + j
-                        columns.append(
-                            jnp.concatenate([own if k == spot else blank for k in range(QUAD)], axis=0)
-                        )
-                    near_ref[(first + block + i) * pairs + pair] = jnp.concatenate(columns, axis=1).astype(bf16)
-            return inner
-
-        lax.fori_loop(0, frame // at_once, one_own, 0)
-        return carry
-
-    lax.fori_loop(0, blocks // frame, one_frame, 0)
+                near_ref[(block + i) * pairs + pair] = jnp.concatenate(columns, axis=1).astype(bf16)
+
+    steps(blocks // frame * passes, one_table)
+    steps(blocks // at_once, one_own)
 
     def places(unit):
         block = unit // pairs
@@ -218,22 +224,13 @@
             total = jnp.zeros((2 * SUM_ROWS, 2 * BLOCK), f32)
             for m in range(listed):
                 spot = slice(2 * m * BLOCK, 2 * (m + 1) * BLOCK)
-                square = ahead_ref[...] if ahead and turn == m == 0 else squares(ats, pair, unit, m)
-                weight_refs[now][spot, :] = jnp.concatenate(parts(square), axis=0)
+                weight_refs[now][spot, :] = jnp.concatenate(parts(squares(ats, pair, unit, m)), axis=0)
                 total = total + weighted(before_ats[m], before_pair, weight_refs[other][spot, :])
             keep(total, jnp.where(unit == 0, units, unit - 1))
             before_ats, before_pair = ats, pair
-        if ahead:
-            look(jnp.minimum((step + 1) * group, units - 1))
         return carry
 
-    def look(unit):
-        ats, pair = places(unit)
-        ahead_ref[...] = squares(ats, pair, unit, 0)
-
     group = math.gcd(units, group)
-    if ahead:
-        look(0)
     lax.fori_loop(0, units // group, body, 0)
     last_ats, last_pair = places(units - 1)
     keep(
@@ -244,7 +241,7 @@
         units - 1,
     )
 
-    def one_block(block, carry):
+    def one_block(block, slot):
         at_frame = block // frame
         place = block - at_frame * frame + margin
         lanes = pl.ds(pl.multiple_of((block + margin) * BLOCK, BLOCK), BLOCK)
@@ -259,9 +256,8 @@
         own = pl.ds(pl.multiple_of(block * BLOCK, BLOCK), BLOCK)
         for c in range(3):
             force_ref[c, :, own] = charge * (coords[c] * near - summed(c + 1))
-        return carry
-
-    lax.fori_loop(0, blocks, one_block, 0)
+
+    steps(blocks, one_block)
 
 
 def force_scratch(local, blocks, margin, listed):
@@ -272,14 +268,13 @@
     units = blocks * beads // 2
     return [
         pltpu.VMEM((3, beads, (blocks + 2 * margin) * BLOCK), f32),
-        pltpu.VMEM((PAIR_PAD * lines, BLOCK), f32),
-        pltpu.VMEM((SUM_ROWS * lines, BLOCK), f32),
+        pltpu.VMEM((SLOTS, PAIR_PAD * lines, BLOCK), f32),
+        pltpu.VMEM((SLOTS, SUM_ROWS * lines, BLOCK), f32),
         pltpu.VMEM((tables, beads // QUAD, BLOCK, QUAD * PAIR_PAD), bf16),
         pltpu.VMEM((tables, beads // 2, 2 * SUM_ROWS, BLOCK), bf16),
         pltpu.VMEM((units, QUAD * PAIR_PAD, 2 * BLOCK), bf16),
         pltpu.VMEM(((units + 1) * 16, BLOCK), f32),
         pltpu.VMEM((3, beads, blocks * BLOCK), f32),
-        pltpu.VMEM((BLOCK, 2 * BLOCK), f32),
         pltpu.VMEM((2 * listed * BLOCK, 2 * BLOCK), bf16),
         pltpu.VMEM((2 * listed * BLOCK, 2 * BLOCK), bf16),
     ]
@@ -383,7 +378,7 @@
         coord_ref[c, :local, 0:atoms] = x_ref[c]
         for part in range(2):
             coord_ref[c, :local, atoms + part * edge:atoms + (part + 1) * edge] = message_ref[3 * part + c]
-    add_forces(4, False, blocks, margin, listed, offset_ref, charge_ref, coord_ref, scratch)
+    add_forces(16, blocks, margin, listed, offset_ref, charge_ref, coord_ref, scratch)
     force_ref = scratch[FORCE]
     for c in range(3):
         for block in range(blocks):
@@ -418,7 +413,7 @@
             at = 2 * edge + block * BLOCK
             coord_ref[c, :local, at:at + BLOCK] = taken(c, block)
         xout_ref[c] = coord_ref[c, :local, edge:edge + atoms]
-    add_forces(8, False, blocks, margin, listed, offset_ref, charge_ref, coord_ref, scratch)
+    add_forces(8, blocks, margin, listed, offset_ref, charge_ref, coord_ref, scratch)
     force_ref = scratch[FORCE]
     for c in range(3):
         for block in range(blocks):
@@ -477,7 +472,7 @@
     width = blocks * BLOCK
     for part in range(parts):
         unpack_beads(x_refs[part], 0, blocks, local, coord_ref, part * width)
-    add_forces(4, True, blocks, hops * blocks, listed, offset_ref, charge_ref, coord_ref, scratch)
+    add_forces(8, blocks, hops * blocks, listed, offset_ref, charge_ref, coord_ref, scratch)
     force_ref = scratch[FORCE]
     unpack_beads(p_ref, 0, blocks, local, coord_ref, 0)
     unpack_beads(noise_ref, noise_base, blocks, local, coord_ref, (parts - 1) * width)

time: 142 us -> 133 us (0.937)
  Pallas kernels: 84.3 us -> 75.4 us
    pallas_call x6, Pallas kernels: 84.3 us -> 75.4 us  [call(): pl.pallas_call(kernel, out_shape=[jax.ShapeDtypeStruct(shape, f32) for sh...]
  transfers between devices with their start and end apart: 7 -> 7, of which waited for: 6 -> 6; matrix products, arithmetic and copies ran while one was open for 1% -> 1% of each run, Pallas kernels for 18% -> 16%
where the time goes in v3:
time: 133 us; the launch traced here: 132 us
  Pallas kernels  75.4 us (57%)
  waiting for transfers between devices  27.8 us (21%)
  starting transfers between devices  23.1 us (17%)
  local copies, waits for them, and re-layouts  3.4 us (3%)
  between operations  2.15 us (2%)
    pallas_call x6, Pallas kernels, call(): pl.pallas_call(kernel, out_shape=[jax.ShapeDtypeStruct(shape, f32) for sh...  75.4 us
    all_to_all x3, waiting for transfers between devices, exchange(): lax.all_to_all(pieces, 'bead', split_axis=0, concat_axis=0, axis_index_gr...  16.7 us
    all_to_all x3, starting transfers between devices, exchange(): lax.all_to_all(pieces, 'bead', split_axis=0, concat_axis=0, axis_index_gr...  13.7 us
    ppermute x2, waiting for transfers between devices, passed(): lax.ppermute(values, 'space', [(i, (i + step) % count) for i in range(cou...  7.24 us
    ppermute x2, starting transfers between devices, passed(): lax.ppermute(values, 'space', [(i, (i + step) % count) for i in range(cou...  6.14 us
    ppermute x2, waiting for transfers between devices, window(): out.append(lax.ppermute(values, ('bead', 'space'), route))  3.79 us
    ppermute x2, starting transfers between devices, window(): out.append(lax.ppermute(values, ('bead', 'space'), route))  3.29 us
  transfers between devices with their start and end apart: 7, of which 6 were waited for; matrix products, arithmetic and copies ran while one was open for 1% of the time, Pallas kernels for 16%

profile of v3, /device:TPU:0, one launch (start us, length us, event | category | flops | bytes accessed | tf_op | source)
XLA Modules:
  0.0 132.1 jit_solution(1560039624415983183)
XLA Ops:
  0.6 0.0 copy-start.8
  0.7 0.7 copy-done.8
  1.3 0.1 copy.17
  1.4 0.1 convert_element_type.15
  1.5 0.6 pad.4
  2.1 0.0 copy-start
  2.1 1.6 %shard_map.104 = (f32[19,4,512]{2,1,0:T(4,128)}, f32[1,4096]{1,0:T(1,128)}, f32[1,4096]{1,0:T(1,128)}) custom-call(f32[3,4,4096]{2,1,0:T(4,128)} %x_ref.5, f32[3,4,4096]{2,1,0:T(4,128)} %p_ref.3, f32[2,3,4,4096]{3,2,1,0:T(4,128)} %noise_ref.3, s32[1,4096]{1,0:T(1,128)} %bitcast.45, f32[1,512]{1,0:T(1,128)} %bitcast.46), custom_call_target="tpu_custom_call" | custom-call | flops 1024 | bytes 4194304 | tf_op jit(solution)/shard_map/pallas_call | solution.py:286
  3.7 3.9 %collective-permute-start = (f32[19,4,512]{2,1,0:T(4,128)}, f32[19,4,512]{2,1,0:T(4,128)S(1)}, u32[]{:S(2)}, u32[]{:S(2)}) collective-permute-start(f32[19,4,512]{2,1,0:T(4,128)} %get-tuple-element.9), channel_id=1, source_target_pairs={{0,3},{1,0},{2,1},{3,2},{4,7},{5,4},{6,5},{7,6},{8,11},{9,8},{10,9... | collective-permute-start | bytes 466952 | tf_op jit(solution)/shard_map/ppermute | solution.py:510
  7.6 0.1 slice.55
  7.7 0.1 copy.16
  7.8 0.1 slice.56
  7.9 3.3 %collective-permute-done.message_ref = f32[19,4,512]{2,1,0:T(4,128)S(1)} collective-permute-done((f32[19,4,512]{2,1,0:T(4,128)}, f32[19,4,512]{2,1,0:T(4,128)S(1)}, u32[]{:S(2)}, u32[]{:S(2)}) %collective-permute-start) | collective-permute-done | bytes 155680 | tf_op jit(solution)/shard_map/ppermute | solution.py:510
  11.2 0.0 copy-done
  11.2 0.0 copy-done.1
  11.3 0.9 shard_map.106
  12.1 5.0 %all-to-all-start = ((f32[8,144,128]{2,1,0:T(8,128)}), f32[8,144,128]{2,1,0:T(8,128)S(1)}, u32[]{:S(2)}, u32[]{:S(2)}) async-start(f32[8,144,128]{2,1,0:T(8,128)} %shard_map.106), calls=%async_computation | async-start | bytes 1179648 | tf_op jit(solution)/shard_map/all_to_all | solution.py:505
  17.1 0.1 pad_add_fusion.offset_ref
  17.2 0.6 copy-done.6
  17.9 0.0 copy-done.2
  17.9 0.0 copy-start.9
  17.9 0.0 copy-start.5
  17.9 21.5 %shard_map.105 = f32[8,48,128]{2,1,0:T(8,128)} custom-call(s32[160]{0:T(256)S(1)} %pad_add_fusion.offset_ref, f32[1,5120]{1,0:T(1,128)S(1)} %pad_maximum_fusion.1.charge_ref, f32[3,4,4096]{2,1,0:T(4,128)S(1)} %copy-done.1, f32[19,4,512]{2,1,0:T(4,128)S(1)} %collective-permute-done.message_ref, f32[3,4,4096]{2,1,0:T(4,128)S(1)} %copy-done.2), custom_call_target="tpu_custom_call" | custom-call | flops 209716224 | bytes 4194304 | tf_op jit(solution)/shard_map/pallas_call | solution.py:286
  39.4 0.0 all-to-all-done.rest_ref.refs_4_
  39.5 5.2 %all-to-all-start.1 = ((f32[8,48,128]{2,1,0:T(8,128)}), f32[8,48,128]{2,1,0:T(8,128)S(1)}, u32[]{:S(2)}, u32[]{:S(2)}) async-start(f32[8,48,128]{2,1,0:T(8,128)} %shard_map.105), calls=%async_computation.1 | async-start | bytes 393216 | tf_op jit(solution)/shard_map/all_to_all | solution.py:505
  44.7 0.0 copy-done.9
  44.7 0.6 dynamic_slice.12
  46.6 0.0 copy-done.7
  46.7 0.0 copy-start.4
  46.7 0.1 dynamic_slice.13.offset_ref
  46.8 0.1 fusion
  46.8 5.8 %all-to-all-done.1.p_ref = f32[8,48,128]{2,1,0:T(8,128)S(1)} async-done(((f32[8,48,128]{2,1,0:T(8,128)}), f32[8,48,128]{2,1,0:T(8,128)S(1)}, u32[]{:S(2)}, u32[]{:S(2)}) %all-to-all-start.1) | async-done | bytes 196640 | tf_op jit(solution)/shard_map/all_to_all | solution.py:505
  52.6 0.0 copy-done.5
  52.6 0.0 copy-done.3
  52.6 0.0 copy-done.4
  52.7 1.2 shard_map.107
  53.9 0.1 collective-permute-start.1
  54.0 3.2 %collective-permute-start.2 = (f32[8,48,128]{2,1,0:T(8,128)S(1)}, f32[8,48,128]{2,1,0:T(8,128)S(1)}, u32[]{:S(2)}, u32[]{:S(2)}) collective-permute-start(f32[8,48,128]{2,1,0:T(8,128)S(1)} %get-tuple-element.14.refs_1_), channel_id=1, source_target_pairs={{8,0},{16,8},{24,16},{28,24},{20,28},{12,20},{4,12},{1,4},{9,1},{1... | collective-permute-start | bytes 589832 | tf_op jit(solution)/shard_map/ppermute | solution.py:528
  57.2 3.1 %collective-permute-done.1.refs_0_ = f32[8,48,128]{2,1,0:T(8,128)S(1)} collective-permute-done((f32[8,48,128]{2,1,0:T(8,128)S(1)}, f32[8,48,128]{2,1,0:T(8,128)S(1)}, u32[]{:S(2)}, u32[]{:S(2)}) %collective-permute-start.1) | collective-permute-done | bytes 196640 | tf_op jit(solution)/shard_map/ppermute | solution.py:528
  60.3 0.7 collective-permute-done.2.refs_2_
  61.0 27.9 %shard_map.108 = f32[8,96,128]{2,1,0:T(8,128)} custom-call(s32[20]{0:T(128)S(1)} %dynamic_slice.13.offset_ref, f32[1,1536]{1,0:T(1,128)S(1)} %constant_dynamic-slice_fusion.charge_ref, f32[8,48,128]{2,1,0:T(8,128)S(1)} %collective-permute-done.1.refs_0_, f32[8,48,128]{2,1,0:T(8,128)S(1)} %get-tuple-element.14.refs_1_, ...), custom_call_target="tpu_custom_call" | custom-call | flops 209716224 | bytes 4194304 | tf_op jit(solution)/shard_map/pallas_call | solution.py:286
  88.9 3.5 %all-to-all-start.2 = ((f32[8,96,128]{2,1,0:T(8,128)}), f32[8,96,128]{2,1,0:T(8,128)S(1)}, u32[]{:S(2)}, u32[]{:S(2)}) async-start(f32[8,96,128]{2,1,0:T(8,128)} %shard_map.108), calls=%async_computation.2 | async-start | bytes 786432 | tf_op jit(solution)/shard_map/all_to_all | solution.py:505
  92.4 10.9 %all-to-all-done.2.both_ref = f32[8,96,128]{2,1,0:T(8,128)S(1)} async-done(((f32[8,96,128]{2,1,0:T(8,128)}), f32[8,96,128]{2,1,0:T(8,128)S(1)}, u32[]{:S(2)}, u32[]{:S(2)}) %all-to-all-start.2) | async-done | bytes 393248 | tf_op jit(solution)/shard_map/all_to_all | solution.py:505
  103.4 2.2 %collective-permute-start.3 = (f32[10,4,512]{2,1,0:T(4,128)S(1)}, f32[10,4,512]{2,1,0:T(4,128)S(1)}, u32[]{:S(2)}, u32[]{:S(2)}) collective-permute-start(f32[10,4,512]{2,1,0:T(4,128)S(1)} %pad_maximum_fusion), channel_id=1, source_target_pairs={{0,1},{1,2},{2,3},{3,0},{4,5},{5,6},{6,7},{7,4},{8,9},{9,10},{10,1... | collective-permute-start | bytes 245768 | tf_op jit(solution)/shard_map/ppermute | solution.py:510
  105.7 0.1 copy.15
  105.8 0.1 reshape.44.offset_ref
  105.9 0.1 maximum_reduce_fusion
  105.9 3.9 %collective-permute-done.3.message_ref = f32[10,4,512]{2,1,0:T(4,128)S(1)} collective-permute-done((f32[10,4,512]{2,1,0:T(4,128)S(1)}, f32[10,4,512]{2,1,0:T(4,128)S(1)}, u32[]{:S(2)}, u32[]{:S(2)}) %collective-permute-start.3) | collective-permute-done | bytes 81952 | tf_op jit(solution)/shard_map/ppermute | solution.py:510
  109.9 22.2 %shard_map.109 = (f32[3,4,4096]{2,1,0:T(4,128)}, f32[3,4,4096]{2,1,0:T(4,128)}) custom-call(s32[160]{0:T(256)S(1)} %reshape.44.offset_ref, f32[1,5120]{1,0:T(1,128)S(1)} %bitcast.36, f32[8,96,128]{2,1,0:T(8,128)S(1)} %all-to-all-done.2.both_ref, f32[10,4,512]{2,1,0:T(4,128)S(1)} %collective-permute-done.3.message_ref), custom_call_target="tpu_custom_call" | custom-call | flops 209716224 | bytes 4194304 | tf_op jit(solution)/shard_map/pallas_call | solution.py:286
  (27 shorter events, 0.2 us)
Async XLA Ops:
  0.6 0.7 copy-start.8
  2.1 9.1 %copy-start = (f32[2,3,4,4096]{3,2,1,0:T(4,128)S(1)}, f32[2,3,4,4096]{3,2,1,0:T(4,128)}, u32[]{:S(2)}) copy-start(f32[2,3,4,4096]{3,2,1,0:T(4,128)} %noise_ref.3) | copy-start | bytes 1179652
  2.1 9.1 %copy-start.1 = (f32[3,4,4096]{2,1,0:T(4,128)S(1)}, f32[3,4,4096]{2,1,0:T(4,128)}, u32[]{:S(2)}) copy-start(f32[3,4,4096]{2,1,0:T(4,128)} %x_ref.5) | copy-start | bytes 589828
  3.7 7.5 %collective-permute-start = (f32[19,4,512]{2,1,0:T(4,128)}, f32[19,4,512]{2,1,0:T(4,128)S(1)}, u32[]{:S(2)}, u32[]{:S(2)}) collective-permute-start(f32[19,4,512]{2,1,0:T(4,128)} %get-tuple-element.9), channel_id=1, source_target_pairs={{0,3},{1,0},{2,1},{3,2},{4,7},{5,4},{6,5},{7,6},{8,11},{9,8},{10,9... | collective-permute-start | bytes 466952 | tf_op jit(solution)/shard_map/ppermute | solution.py:510
  12.1 5.8 %copy-start.2 = (f32[3,4,4096]{2,1,0:T(4,128)S(1)}, f32[3,4,4096]{2,1,0:T(4,128)}, u32[]{:S(2)}) copy-start(f32[3,4,4096]{2,1,0:T(4,128)} %p_ref.3) | copy-start | bytes 589828
  12.1 27.3 %all-to-all-start = ((f32[8,144,128]{2,1,0:T(8,128)}), f32[8,144,128]{2,1,0:T(8,128)S(1)}, u32[]{:S(2)}, u32[]{:S(2)}) async-start(f32[8,144,128]{2,1,0:T(8,128)} %shard_map.106), calls=%async_computation | async-start | bytes 1179648 | tf_op jit(solution)/shard_map/all_to_all | solution.py:505
  17.1 0.7 copy-start.6
  17.9 26.8 %copy-start.9 = (s32[8]{0:T(128)S(1)}, s32[8]{0:T(128)}, u32[]{:S(2)}) copy-start(s32[8]{0:T(128)} %constant.42.clone) | copy-start | bytes 100
  17.9 34.7 %copy-start.5 = (f32[32,32]{1,0:T(8,128)S(1)}, f32[32,32]{1,0:T(8,128)}, u32[]{:S(2)}) copy-start(f32[32,32]{1,0:T(8,128)} %constant.44.clone.matrix_t_ref.refs_7_) | copy-start | bytes 12292
  39.5 7.2 %copy-start.7 = (f32[1,4096]{1,0:T(1,128)S(1)}, f32[1,4096]{1,0:T(1,128)}, u32[]{:S(2)}) copy-start(f32[1,4096]{1,0:T(1,128)} %get-tuple-element.13) | copy-start | bytes 49156
  39.5 13.2 %all-to-all-start.1 = ((f32[8,48,128]{2,1,0:T(8,128)}), f32[8,48,128]{2,1,0:T(8,128)S(1)}, u32[]{:S(2)}, u32[]{:S(2)}) async-start(f32[8,48,128]{2,1,0:T(8,128)} %shard_map.105), calls=%async_computation.1 | async-start | bytes 393216 | tf_op jit(solution)/shard_map/all_to_all | solution.py:505
  44.7 8.0 %copy-start.3 = (f32[5,32,128]{2,1,0:T(8,128)S(1)}, f32[5,32,128]{2,1,0:T(8,128)}, u32[]{:S(2)}) copy-start(f32[5,32,128]{2,1,0:T(8,128)} %constant.45.clone.table_ref.refs_8_) | copy-start | bytes 245764
  46.7 6.0 %copy-start.4 = (f32[32,32]{1,0:T(8,128)S(1)}, f32[32,32]{1,0:T(8,128)}, u32[]{:S(2)}) copy-start(f32[32,32]{1,0:T(8,128)} %constant.43.clone.matrix_ref.refs_6_) | copy-start | bytes 12292
  53.9 6.4 %collective-permute-start.1 = (f32[8,48,128]{2,1,0:T(8,128)S(1)}, f32[8,48,128]{2,1,0:T(8,128)S(1)}, u32[]{:S(2)}, u32[]{:S(2)}) collective-permute-start(f32[8,48,128]{2,1,0:T(8,128)S(1)} %get-tuple-element.14.refs_1_), channel_id=1, source_target_pairs={{7,0},{0,8},{8,16},{16,24},{24,28},{28,20},{20,12},{12,4},{4,1},{1... | collective-permute-start | bytes 589832 | tf_op jit(solution)/shard_map/ppermute | solution.py:528
  54.0 7.0 %collective-permute-start.2 = (f32[8,48,128]{2,1,0:T(8,128)S(1)}, f32[8,48,128]{2,1,0:T(8,128)S(1)}, u32[]{:S(2)}, u32[]{:S(2)}) collective-permute-start(f32[8,48,128]{2,1,0:T(8,128)S(1)} %get-tuple-element.14.refs_1_), channel_id=1, source_target_pairs={{8,0},{16,8},{24,16},{28,24},{20,28},{12,20},{4,12},{1,4},{9,1},{1... | collective-permute-start | bytes 589832 | tf_op jit(solution)/shard_map/ppermute | solution.py:528
  88.9 14.4 %all-to-all-start.2 = ((f32[8,96,128]{2,1,0:T(8,128)}), f32[8,96,128]{2,1,0:T(8,128)S(1)}, u32[]{:S(2)}, u32[]{:S(2)}) async-start(f32[8,96,128]{2,1,0:T(8,128)} %shard_map.108), calls=%async_computation.2 | async-start | bytes 786432 | tf_op jit(solution)/shard_map/all_to_all | solution.py:505
  103.4 6.4 %collective-permute-start.3 = (f32[10,4,512]{2,1,0:T(4,128)S(1)}, f32[10,4,512]{2,1,0:T(4,128)S(1)}, u32[]{:S(2)}, u32[]{:S(2)}) collective-permute-start(f32[10,4,512]{2,1,0:T(4,128)S(1)} %pad_maximum_fusion), channel_id=1, source_target_pairs={{0,1},{1,2},{2,3},{3,0},{4,5},{5,6},{6,7},{7,4},{8,9},{9,10},{10,1... | collective-permute-start | bytes 245768 | tf_op jit(solution)/shard_map/ppermute | solution.py:510

commit v4 on v3

--- a/solution.py
+++ b/solution.py
@@ -160,7 +160,7 @@
                 four = jnp.concatenate(
                     [rows_ref[slot, pl.ds(low + j, PAIR_PAD, stride=lines), :] for j in range(QUAD)], axis=0
                 )
-                far_ref[at, quad] = jnp.transpose(four).astype(bf16)
+                far_ref[at, quad] = jnp.transpose(four.astype(bf16))
                 for half in range(2):
                     heavy_ref[at, 2 * quad + half] = jnp.concatenate(
                         [
@@ -327,8 +327,7 @@
         coord_ref[...] = jnp.zeros(coord_ref.shape, f32)
 
 
-def message_kernel(x_ref, p_ref, noise_ref, types_ref, offsets_ref, message_ref, charge_ref, mass_ref):
-    steps = noise_ref.shape[0]
+def message_kernel(x_ref, p_ref, types_ref, offsets_ref, message_ref, charge_ref, mass_ref):
     _, local, edge = message_ref.shape
     types = types_ref[...]
     charge = jnp.zeros(types.shape, f32)
@@ -342,83 +341,117 @@
         message_ref[c] = x_ref[c, :, :edge]
         message_ref[3 + c] = x_ref[c, :, edge:2 * edge]
         message_ref[6 + c] = p_ref[c, :, :edge]
-        for step in range(steps):
-            message_ref[9 + 3 * step + c] = noise_ref[step, c, :, :edge]
-    at = 9 + 3 * steps
     for i, row in enumerate([charge[:, :edge], charge[:, edge:2 * edge], mass[:, :edge], offsets_ref[...]]):
-        message_ref[at + i] = jnp.broadcast_to(row, (local, edge))
-
-
-def pack_kernel(blocks, x_ref, noise_ref, message_ref, out_ref):
-    steps = noise_ref.shape[0]
-    _, local, edge = message_ref.shape
-    atoms = x_ref.shape[2]
+        message_ref[9 + i] = jnp.broadcast_to(row, (local, edge))
+
+
+def pack_kernel(blocks, x_ref, noise_ref, out_ref):
+    steps, _, local, atoms = noise_ref.shape
     for c in range(3 + 3 * steps):
         for block in range(atoms // BLOCK):
-            at = edge + block * BLOCK
-            if at >= atoms:
-                value = message_ref[c if c < 3 else 6 + c, :, at - atoms:at - atoms + BLOCK]
-            elif c < 3:
-                value = x_ref[c, :, at:at + BLOCK]
-            else:
-                value = noise_ref[c // 3 - 1, c % 3, :, at:at + BLOCK]
+            lanes = slice(block * BLOCK, (block + 1) * BLOCK)
+            value = x_ref[c, :, lanes] if c < 3 else noise_ref[c // 3 - 1, c % 3, :, lanes]
             row = row_of(c, block % blocks, blocks, local)
             out_ref[block // blocks, row:row + local, :] = value
 
 
-def first_kernel(
-    shares, margin, listed, offset_ref, charge_ref, x_ref, message_ref, p_ref, pout_ref, coord_ref, *scratch
+def front_kernel(each, margin, listed, offset_ref, charge_ref, x_ref, p_ref, pout_ref, coord_ref, *scratch):
+    _, local, _ = x_ref.shape
+    blocks = pout_ref.shape[0] * each
+    clear(coord_ref, local)
+    for c in range(3):
+        coord_ref[c, :local, :] = x_ref[c, :, :(blocks + 2 * margin) * BLOCK]
+    add_forces(16, blocks, margin, listed, offset_ref, charge_ref, coord_ref, scratch)
+    force_ref = scratch[FORCE]
+    for c in range(3):
+        for block in range(blocks):
+            lanes = slice(block * BLOCK, (block + 1) * BLOCK)
+            moment = p_ref[c, :, (block + margin) * BLOCK:(block + margin + 1) * BLOCK]
+            row = row_of(c, block % each, each, local)
+            pout_ref[block // each, row:row + local, :] = moment + half_step * force_ref[c, :local, lanes]
+
+
+def back_kernel(
+    each, margin, listed, offset_ref, charge_ref, x_ref, message_ref, p_ref, front_ref, pout_ref, coord_ref, *scratch
 ):
     _, local, atoms = x_ref.shape
-    blocks = atoms // BLOCK
-    each = blocks // shares
     edge = margin * BLOCK
+    done = front_ref.shape[0]
+    first = done * each
+    blocks = (pout_ref.shape[0] - done) * each
+    own = atoms - first * BLOCK
     clear(coord_ref, local)
     for c in range(3):
-        coord_ref[c, :local, 0:atoms] = x_ref[c]
+        coord_ref[c, :local, :own] = x_ref[c, :, first * BLOCK:]
         for part in range(2):
-            coord_ref[c, :local, atoms + part * edge:atoms + (part + 1) * edge] = message_ref[3 * part + c]
-    add_forces(16, blocks, margin, listed, offset_ref, charge_ref, coord_ref, scratch)
+            coord_ref[c, :local, own + part * edge:own + (part + 1) * edge] = message_ref[3 * part + c]
+    add_forces(8, blocks, margin, listed, offset_ref, charge_ref, coord_ref, scratch)
     force_ref = scratch[FORCE]
+    pout_ref[:done] = front_ref[...]
     for c in range(3):
         for block in range(blocks):
             lanes = slice(block * BLOCK, (block + 1) * BLOCK)
-            at = block * BLOCK + edge
+            at = (first + block) * BLOCK + edge
             if at < atoms:
                 moment = p_ref[c, :, at:at + BLOCK]
             else:
                 moment = message_ref[6 + c, :, at - atoms:at - atoms + BLOCK]
             row = row_of(c, block % each, each, local)
-            pout_ref[block // each, row:row + local, :] = moment + half_step * force_ref[c, :local, lanes]
-
-
-def last_kernel(
-    margin, listed, offset_ref, charge_ref, both_ref, message_ref, xout_ref, pout_ref, coord_ref, *scratch
+            pout_ref[done + block // each, row:row + local, :] = moment + half_step * force_ref[c, :local, lanes]
+
+
+def from_packed(ref, c, block, each, local):
+    row = row_of(c, block % each, each, local)
+    return ref[block // each, row:row + local, :]
+
+
+def upper_kernel(each, margin, listed, offset_ref, charge_ref, both_ref, pout_ref, coord_ref, *scratch):
+    _, local, atoms = pout_ref.shape
+    blocks = atoms // BLOCK
+    domain = both_ref.shape[0] * each
+    skipped = domain - blocks - 2 * margin
+    clear(coord_ref, local)
+    for c in range(3):
+        for block in range(skipped, domain):
+            at = (block - skipped) * BLOCK
+            coord_ref[c, :local, at:at + BLOCK] = from_packed(both_ref, c, block, each, local)
+    add_forces(16, blocks, margin, listed, offset_ref, charge_ref, coord_ref, scratch)
+    force_ref = scratch[FORCE]
+    for c in range(3):
+        for block in range(blocks):
+            lanes = slice(block * BLOCK, (block + 1) * BLOCK)
+            moment = from_packed(both_ref, 3 + c, domain - blocks + block - margin, each, local)
+            pout_ref[c, :, lanes] = moment + half_step * force_ref[c, :local, lanes]
+
+
+def lower_kernel(
+    each, margin, listed, offset_ref, charge_ref, both_ref, message_ref, upper_ref, xout_ref, pout_ref, coord_ref, *scratch
 ):
-    shares = both_ref.shape[0]
     _, local, atoms = xout_ref.shape
-    blocks = atoms // BLOCK
-    each = blocks // shares
     edge = margin * BLOCK
-
-    def taken(c, block):
-        row = row_of(c, block % each, each, local)
-        return both_ref[block // each, row:row + local, :]
-
+    lower = atoms - upper_ref.shape[2]
+    blocks = lower // BLOCK
     clear(coord_ref, local)
     for c in range(3):
         for part in range(2):
             coord_ref[c, :local, part * edge:(part + 1) * edge] = message_ref[3 * part + c]
         for block in range(blocks):
             at = 2 * edge + block * BLOCK
-            coord_ref[c, :local, at:at + BLOCK] = taken(c, block)
-        xout_ref[c] = coord_ref[c, :local, edge:edge + atoms]
+            coord_ref[c, :local, at:at + BLOCK] = from_packed(both_ref, c, block, each, local)
+        xout_ref[c, :, :edge] = message_ref[3 + c]
+        for block in range(margin, atoms // BLOCK):
+            lanes = slice(block * BLOCK, (block + 1) * BLOCK)
+            xout_ref[c, :, lanes] = from_packed(both_ref, c, block - margin, each, local)
+        pout_ref[c, :, lower:] = upper_ref[c]
     add_forces(8, blocks, margin, listed, offset_ref, charge_ref, coord_ref, scratch)
     force_ref = scratch[FORCE]
     for c in range(3):
         for block in range(blocks):
             lanes = slice(block * BLOCK, (block + 1) * BLOCK)
-            moment = message_ref[6 + c, :, lanes] if block < margin else taken(3 + c, block - margin)
+            if block < margin:
+                moment = message_ref[6 + c, :, lanes]
+            else:
+                moment = from_packed(both_ref, 3 + c, block - margin, each, local)
             pout_ref[c, :, lanes] = moment + half_step * force_ref[c, :local, lanes]
 
 
@@ -472,7 +505,7 @@
     width = blocks * BLOCK
     for part in range(parts):
         unpack_beads(x_refs[part], 0, blocks, local, coord_ref, part * width)
-    add_forces(8, blocks, hops * blocks, listed, offset_ref, charge_ref, coord_ref, scratch)
+    add_forces(16, blocks, hops * blocks, listed, offset_ref, charge_ref, coord_ref, scratch)
     force_ref = scratch[FORCE]
     unpack_beads(p_ref, 0, blocks, local, coord_ref, 0)
     unpack_beads(noise_ref, noise_base, blocks, local, coord_ref, (parts - 1) * width)
@@ -510,7 +543,7 @@
     return lax.ppermute(values, "space", [(i, (i + step) % count) for i in range(count)])
 
 
-def window(values, hops):
+def round_ring(values, hop):
     count = lax.axis_size("bead")
     domains = lax.axis_size("space")
     order = fold(count)
@@ -519,14 +552,11 @@
         for domain in range(domains):
             device[domain * count + order[bead]] = bead * domains + domain
     total = count * domains
-    out = []
-    for hop in range(-hops, hops + 1):
-        if hop == 0:
-            out.append(values)
-        else:
-            route = [(device[(at + hop) % total], device[at]) for at in range(total)]
-            out.append(lax.ppermute(values, ("bead", "space"), route))
-    return out
+    return lax.ppermute(values, ("bead", "space"), [(device[(at + hop) % total], device[at]) for at in range(total)])
+
+
+def window(values, hops):
+    return [round_ring(values, hop) if hop else values for hop in range(-hops, hops + 1)]
 
 
 def body(positions, momenta, atom_types, neighbours, thermal_noise):
@@ -547,26 +577,25 @@
     offsets = jnp.clip(neighbours - own[:, None], -margin, margin).reshape(-1)
     sent = jnp.pad(offsets[:margin * listed].astype(f32), (0, edge - margin * listed))[None, :]
 
+    (rest,) = call(
+        functools.partial(pack_kernel, blocks), (positions, thermal_noise), 0,
+        [(count, (3 + 3 * steps) * blocks * local, BLOCK)], [], 0,
+    )
+    rest = exchange(rest)
+
     message, charge, mass = call(
-        message_kernel, (positions, momenta, thermal_noise, atom_types[None, :], sent), 0,
-        [(13 + 3 * steps, local, edge), (1, atoms), (1, atoms)], [], 0,
+        message_kernel, (positions, momenta, atom_types[None, :], sent), 0,
+        [(13, local, edge), (1, atoms), (1, atoms)], [], 0,
         [
             pl.BlockSpec(shape, lambda i, rank=len(shape): (0,) * rank)
-            for shape in (
-                (3, local, 2 * edge), (3, local, edge), (steps, 3, local, edge), (1, atoms), (1, edge)
-            )
+            for shape in ((3, local, 2 * edge), (3, local, edge), (1, atoms), (1, edge))
         ],
     )
     message = passed(message, -1)
-    side = message[9 + 3 * steps:, 0]
+    side = message[9:, 0]
     first_charge = jnp.concatenate([charge, side[:1], side[1:2]], axis=1)
     moved_mass = jnp.concatenate([mass[0, edge:], side[2]])
     moved_offsets = jnp.concatenate([offsets[margin * listed:], side[3, :margin * listed].astype(jnp.int32)])
-    (rest,) = call(
-        functools.partial(pack_kernel, blocks), (positions, thermal_noise, message), 0,
-        [(count, (3 + 3 * steps) * blocks * local, BLOCK)], [], 0,
-    )
-    rest = exchange(rest)
 
     place = jnp.asarray(np.array(order, np.int32))[lax.axis_index("bead")]
     near_charge = lax.dynamic_slice_in_dim(first_charge, place * share, share + 2 * edge, axis=1)
@@ -580,10 +609,20 @@
 
     packed = (count, 3 * blocks * local, BLOCK)
     pairs = beads * blocks * listed * BLOCK * BLOCK
+    frame = min(FRAME, domain)
+    most = domain - frame
+    window_atoms = (most + 2 * margin) * BLOCK
     (moment,) = call(
-        functools.partial(first_kernel, count, margin, listed),
-        (moved_offsets, first_charge, positions, message, momenta), 1, [packed],
-        force_scratch(local, domain, margin, listed), pairs,
+        functools.partial(front_kernel, blocks, margin, listed),
+        (offsets[margin * listed:(margin + most) * listed], charge[:, :window_atoms], positions, momenta), 1,
+        [(most // blocks,) + packed[1:]], force_scratch(local, most, margin, listed), pairs * most // domain,
+    )
+    moment, rest = lax.optimization_barrier((moment, rest))
+    rest = round_ring(rest, hops)
+    (moment,) = call(
+        functools.partial(back_kernel, blocks, margin, listed),
+        (moved_offsets[most * listed:], first_charge[:, most * BLOCK:], positions, message, momenta, moment), 1,
+        [packed], force_scratch(local, frame, margin, listed), pairs * frame // domain,
     )
     moment, rest = lax.optimization_barrier((moment, rest))
     coords, moment = call(
@@ -610,10 +649,16 @@
         ends(count - 2 * hops, 0), ends(count - hops, 0), ends(count - hops, 1),
         jnp.broadcast_to(charge[:, None, atoms - edge:], (1, local, edge)),
     ], axis=0), 1)
-    last_charge = jnp.concatenate([message[9, 0], first_charge[0, :atoms + edge]])[None, :]
+    (upper,) = call(
+        functools.partial(upper_kernel, blocks, margin, listed),
+        (offsets[frame * listed:], first_charge[:, frame * BLOCK - edge:atoms + edge], both), 1,
+        [(3, local, most * BLOCK)], force_scratch(local, most, margin, listed), pairs * most // domain,
+    )
+    last_charge = jnp.concatenate([message[9, :1], first_charge[:, :frame * BLOCK + edge]], axis=1)
     return tuple(call(
-        functools.partial(last_kernel, margin, listed), (offsets, last_charge, both, message), 1,
-        [(3, local, atoms)] * 2, force_scratch(local, domain, margin, listed), pairs,
+        functools.partial(lower_kernel, blocks, margin, listed),
+        (offsets[:frame * listed], last_charge, both, message, upper), 1,
+        [(3, local, atoms)] * 2, force_scratch(local, frame, margin, listed), pairs * frame // domain,
     ))
 
 

time: 133 us -> 129 us (0.970)
  waiting for transfers between devices: 27.8 us -> 24.4 us
  starting transfers between devices: 23.1 us -> 19.9 us
  local copies, waits for them, and re-layouts: 3.4 us -> 5.66 us
    ppermute x2, waiting for transfers between devices: 7.24 us -> 0.01 us  [passed(): lax.ppermute(values, 'space', [(i, (i + step) % count) for i in range(cou...]
    ppermute x2 -> x3, waiting for transfers between devices: 3.79 us -> 8.06 us  [round_ring(): lax.ppermute(values, ('bead', 'space'), [(device[(at + hop) % total], dev...]
    ppermute x2, starting transfers between devices: 6.14 us -> 2.73 us  [passed(): lax.ppermute(values, 'space', [(i, (i + step) % count) for i in range(cou...]
    unnamed x21 -> x23, local copies, waits for them, and re-layouts: 1.33 us -> 3.11 us
    pallas_call x6 -> x8, Pallas kernels: 75.4 us -> 75.9 us  [call(): pl.pallas_call(kernel, out_shape=[jax.ShapeDtypeStruct(shape, f32) for sh...]
    ppermute x2 -> x3, starting transfers between devices: 3.29 us -> 3.12 us  [round_ring(): lax.ppermute(values, ('bead', 'space'), [(device[(at + hop) % total], dev...]
  transfers between devices with their start and end apart: 7 -> 8, of which waited for: 6 -> 4; matrix products, arithmetic and copies ran while one was open for 1% -> 2% of each run, Pallas kernels for 16% -> 31%
where the time goes in v4:
time: 129 us; the launch traced here: 128 us
  Pallas kernels  75.9 us (59%)
  waiting for transfers between devices  24.4 us (19%)
  starting transfers between devices  19.9 us (15%)
  local copies, waits for them, and re-layouts  5.66 us (4%)
  between operations  2.24 us (2%)
    pallas_call x8, Pallas kernels, call(): pl.pallas_call(kernel, out_shape=[jax.ShapeDtypeStruct(shape, f32) for sh...  75.9 us
    all_to_all x3, waiting for transfers between devices, exchange(): lax.all_to_all(pieces, 'bead', split_axis=0, concat_axis=0, axis_index_gr...  16.4 us
    all_to_all x3, starting transfers between devices, exchange(): lax.all_to_all(pieces, 'bead', split_axis=0, concat_axis=0, axis_index_gr...  14.1 us
    ppermute x3, waiting for transfers between devices, round_ring(): lax.ppermute(values, ('bead', 'space'), [(device[(at + hop) % total], dev...  8.06 us
    ppermute x3, starting transfers between devices, round_ring(): lax.ppermute(values, ('bead', 'space'), [(device[(at + hop) % total], dev...  3.12 us
    unnamed x23, local copies, waits for them, and re-layouts  3.11 us
    ppermute x2, starting transfers between devices, passed(): lax.ppermute(values, 'space', [(i, (i + step) % count) for i in range(cou...  2.73 us
  transfers between devices with their start and end apart: 8, of which 4 were waited for; matrix products, arithmetic and copies ran while one was open for 2% of the time, Pallas kernels for 31%

profile of v4, /device:TPU:0, one launch (start us, length us, event | category | flops | bytes accessed | tf_op | source)
XLA Modules:
  0.0 128.4 jit_solution(12116648119779209361)
XLA Ops:
  0.6 0.0 copy-start
  0.6 0.9 copy-done
  1.6 1.0 copy-done.2
  2.6 0.9 shard_map.106
  3.4 6.3 %all-to-all-start = ((f32[8,144,128]{2,1,0:T(8,128)}), f32[8,144,128]{2,1,0:T(8,128)S(1)}, u32[]{:S(2)}, u32[]{:S(2)}) async-start(f32[8,144,128]{2,1,0:T(8,128)} %shard_map.106), calls=%async_computation | async-start | bytes 1179648 | tf_op jit(solution)/shard_map/all_to_all | solution.py:538
  9.8 0.7 copy-done.9
  10.4 0.1 copy.20
  10.5 0.1 convert_element_type.15
  10.6 0.6 pad.4
  11.2 1.5 %shard_map.104 = (f32[13,4,512]{2,1,0:T(4,128)}, f32[1,4096]{1,0:T(1,128)}, f32[1,4096]{1,0:T(1,128)}) custom-call(f32[3,4,4096]{2,1,0:T(4,128)} %x_ref.7, f32[3,4,4096]{2,1,0:T(4,128)} %p_ref.5, s32[1,4096]{1,0:T(1,128)} %bitcast.46, f32[1,512]{1,0:T(1,128)} %bitcast.47), custom_call_target="tpu_custom_call" | custom-call | flops 1024 | bytes 4194304 | tf_op jit(solution)/shard_map/pallas_call | solution.py:286
  12.8 2.4 %collective-permute-start = (f32[13,4,512]{2,1,0:T(4,128)}, f32[13,4,512]{2,1,0:T(4,128)S(1)}, u32[]{:S(2)}, u32[]{:S(2)}) collective-permute-start(f32[13,4,512]{2,1,0:T(4,128)} %get-tuple-element.11), channel_id=1, source_target_pairs={{0,3},{1,0},{2,1},{3,2},{4,7},{5,4},{6,5},{7,6},{8,11},{9,8},{10,9... | collective-permute-start | bytes 319496 | tf_op jit(solution)/shard_map/ppermute | solution.py:543
  15.2 0.1 fusion.4
  15.3 0.1 slice.86
  15.4 0.1 copy.21
  15.4 0.1 slice.98.offset_ref
  15.5 0.0 copy-start.4
  15.5 0.1 copy.19
  15.6 0.1 slice.87
  15.8 0.5 copy-done.4
  16.3 15.8 %shard_map.105.front_ref = f32[6,48,128]{2,1,0:T(8,128)S(1)} custom-call(s32[120]{0:T(128)S(1)} %slice.98.offset_ref, f32[1,4096]{1,0:T(1,128)S(1)} %copy-done.4, f32[3,4,4096]{2,1,0:T(4,128)S(1)} %copy-done.1, f32[3,4,4096]{2,1,0:T(4,128)S(1)} %copy-done.3), custom_call_target="tpu_custom_call" | custom-call | flops 157287424 | bytes 4194304 | tf_op jit(solution)/shard_map/pallas_call | solution.py:286
  32.1 0.0 collective-permute-done.message_ref
  32.1 0.0 all-to-all-done
  32.1 0.4 collective-permute-start.1
  32.6 0.1 pad_add_fusion
  32.7 0.1 slice.95.offset_ref
  32.8 6.6 %shard_map.107 = f32[8,48,128]{2,1,0:T(8,128)} custom-call(s32[40]{0:T(128)S(1)} %slice.95.offset_ref, f32[1,2048]{1,0:T(1,128)S(1)} %slice.114.charge_ref, f32[3,4,4096]{2,1,0:T(4,128)S(1)} %copy-done.1, f32[13,4,512]{2,1,0:T(4,128)S(1)} %collective-permute-done.message_ref, f32[3,4,4096]{2,1,0:T(4,128)S(1)} %copy-done.3, ...), custom_call_target="tpu_custom_call" | custom-call | flops 52429824 | bytes 4194304 | tf_op jit(solution)/shard_map/pallas_call | solution.py:286
  39.4 2.7 %collective-permute-done.1.rest_ref.refs_4_ = f32[8,144,128]{2,1,0:T(8,128)S(1)} collective-permute-done((f32[8,144,128]{2,1,0:T(8,128)S(1)}, f32[8,144,128]{2,1,0:T(8,128)S(1)}, u32[]{:S(2)}, u32[]{:S(2)}) %collective-permute-start.1) | collective-permute-done | bytes 589856 | tf_op jit(solution)/shard_map/ppermute | solution.py:555
  42.1 4.3 %all-to-all-start.1 = ((f32[8,48,128]{2,1,0:T(8,128)}), f32[8,48,128]{2,1,0:T(8,128)S(1)}, u32[]{:S(2)}, u32[]{:S(2)}) async-start(f32[8,48,128]{2,1,0:T(8,128)} %shard_map.107), calls=%async_computation.1 | async-start | bytes 393216 | tf_op jit(solution)/shard_map/all_to_all | solution.py:538
  46.4 0.6 dynamic_slice.12
  48.4 0.0 copy-start.6
  48.4 0.1 dynamic_slice.13.offset_ref
  48.5 0.1 fusion
  48.5 5.8 %all-to-all-done.1.p_ref = f32[8,48,128]{2,1,0:T(8,128)S(1)} async-done(((f32[8,48,128]{2,1,0:T(8,128)}), f32[8,48,128]{2,1,0:T(8,128)S(1)}, u32[]{:S(2)}, u32[]{:S(2)}) %all-to-all-start.1) | async-done | bytes 196640 | tf_op jit(solution)/shard_map/all_to_all | solution.py:538
  54.4 1.2 shard_map.108
  55.6 0.1 collective-permute-start.2
  55.7 2.6 %collective-permute-start.3 = (f32[8,48,128]{2,1,0:T(8,128)S(1)}, f32[8,48,128]{2,1,0:T(8,128)S(1)}, u32[]{:S(2)}, u32[]{:S(2)}) collective-permute-start(f32[8,48,128]{2,1,0:T(8,128)S(1)} %get-tuple-element.18.refs_1_), channel_id=1, source_target_pairs={{8,0},{16,8},{24,16},{28,24},{20,28},{12,20},{4,12},{1,4},{9,1},{1... | collective-permute-start | bytes 589832 | tf_op jit(solution)/shard_map/ppermute | solution.py:555
  58.3 5.4 %collective-permute-done.2.refs_0_ = f32[8,48,128]{2,1,0:T(8,128)S(1)} collective-permute-done((f32[8,48,128]{2,1,0:T(8,128)S(1)}, f32[8,48,128]{2,1,0:T(8,128)S(1)}, u32[]{:S(2)}, u32[]{:S(2)}) %collective-permute-start.2) | collective-permute-done | bytes 196640 | tf_op jit(solution)/shard_map/ppermute | solution.py:555
  63.7 0.0 collective-permute-done.3.refs_2_
  63.7 27.3 %shard_map.109 = f32[8,96,128]{2,1,0:T(8,128)} custom-call(s32[20]{0:T(128)S(1)} %dynamic_slice.13.offset_ref, f32[1,1536]{1,0:T(1,128)S(1)} %constant_dynamic-slice_fusion.charge_ref, f32[8,48,128]{2,1,0:T(8,128)S(1)} %collective-permute-done.2.refs_0_, f32[8,48,128]{2,1,0:T(8,128)S(1)} %get-tuple-element.18.refs_1_, ...), custom_call_target="tpu_custom_call" | custom-call | flops 209716224 | bytes 4194304 | tf_op jit(solution)/shard_map/pallas_call | solution.py:286
  91.0 3.5 %all-to-all-start.2 = ((f32[8,96,128]{2,1,0:T(8,128)}), f32[8,96,128]{2,1,0:T(8,128)S(1)}, u32[]{:S(2)}, u32[]{:S(2)}) async-start(f32[8,96,128]{2,1,0:T(8,128)} %shard_map.109), calls=%async_computation.2 | async-start | bytes 786432 | tf_op jit(solution)/shard_map/all_to_all | solution.py:538
  94.5 0.1 copy.25
  94.6 0.1 slice.108.offset_ref
  94.7 0.1 copy.18
  94.7 0.1 slice.85.offset_ref
  94.8 10.6 %all-to-all-done.2.both_ref = f32[8,96,128]{2,1,0:T(8,128)S(1)} async-done(((f32[8,96,128]{2,1,0:T(8,128)}), f32[8,96,128]{2,1,0:T(8,128)S(1)}, u32[]{:S(2)}, u32[]{:S(2)}) %all-to-all-start.2) | async-done | bytes 393248 | tf_op jit(solution)/shard_map/all_to_all | solution.py:538
  105.5 0.3 collective-permute-start.4
  105.8 15.8 %shard_map.110.upper_ref = f32[3,4,3072]{2,1,0:T(4,128)S(1)} custom-call(s32[120]{0:T(128)S(1)} %slice.108.offset_ref, f32[1,4096]{1,0:T(1,128)S(1)} %pad_maximum_fusion.2.charge_ref, f32[8,96,128]{2,1,0:T(8,128)S(1)} %all-to-all-done.2.both_ref), custom_call_target="tpu_custom_call" | custom-call | flops 157287424 | bytes 4194304 | tf_op jit(solution)/shard_map/pallas_call | solution.py:286
  121.7 6.7 %shard_map.111 = (f32[3,4,4096]{2,1,0:T(4,128)}, f32[3,4,4096]{2,1,0:T(4,128)}) custom-call(s32[40]{0:T(128)S(1)} %slice.85.offset_ref, f32[1,2048]{1,0:T(1,128)S(1)} %pad_maximum_fusion.3.charge_ref, f32[8,96,128]{2,1,0:T(8,128)S(1)} %all-to-all-done.2.both_ref, f32[10,4,512]{2,1,0:T(4,128)S(1)} %collective-permute-done.4.message_ref, ...), custom_call_target="tpu_custom_call" | custom-call | flops 52429824 | bytes 4194304 | tf_op jit(solution)/shard_map/pallas_call | solution.py:286
  (41 shorter events, 0.3 us)
Async XLA Ops:
  0.6 0.9 copy-start
  1.6 1.0 copy-start.2
  3.4 28.7 %all-to-all-start = ((f32[8,144,128]{2,1,0:T(8,128)}), f32[8,144,128]{2,1,0:T(8,128)S(1)}, u32[]{:S(2)}, u32[]{:S(2)}) async-start(f32[8,144,128]{2,1,0:T(8,128)} %shard_map.106), calls=%async_computation | async-start | bytes 1179648 | tf_op jit(solution)/shard_map/all_to_all | solution.py:538
  9.7 0.7 copy-start.9
  11.2 4.5 %copy-start.1 = (f32[3,4,4096]{2,1,0:T(4,128)S(1)}, f32[3,4,4096]{2,1,0:T(4,128)}, u32[]{:S(2)}) copy-start(f32[3,4,4096]{2,1,0:T(4,128)} %x_ref.7) | copy-start | bytes 589828
  11.2 4.5 %copy-start.3 = (f32[3,4,4096]{2,1,0:T(4,128)S(1)}, f32[3,4,4096]{2,1,0:T(4,128)}, u32[]{:S(2)}) copy-start(f32[3,4,4096]{2,1,0:T(4,128)} %p_ref.5) | copy-start | bytes 589828
  12.8 19.3 %collective-permute-start = (f32[13,4,512]{2,1,0:T(4,128)}, f32[13,4,512]{2,1,0:T(4,128)S(1)}, u32[]{:S(2)}, u32[]{:S(2)}) collective-permute-start(f32[13,4,512]{2,1,0:T(4,128)} %get-tuple-element.11), channel_id=1, source_target_pairs={{0,3},{1,0},{2,1},{3,2},{4,7},{5,4},{6,5},{7,6},{8,11},{9,8},{10,9... | collective-permute-start | bytes 319496 | tf_op jit(solution)/shard_map/ppermute | solution.py:543
  15.5 0.7 copy-start.4
  32.1 9.9 %collective-permute-start.1 = (f32[8,144,128]{2,1,0:T(8,128)S(1)}, f32[8,144,128]{2,1,0:T(8,128)S(1)}, u32[]{:S(2)}, u32[]{:S(2)}) collective-permute-start(f32[8,144,128]{2,1,0:T(8,128)S(1)} %all-to-all-done), channel_id=1, source_target_pairs={{8,0},{16,8},{24,16},{28,24},{20,28},{12,20},{4,12},{1,4},{9,1},{1... | collective-permute-start | bytes 1769480 | tf_op jit(solution)/shard_map/ppermute | solution.py:555
  32.8 13.6 %copy-start.10 = (s32[8]{0:T(128)S(1)}, s32[8]{0:T(128)}, u32[]{:S(2)}) copy-start(s32[8]{0:T(128)} %constant.42.clone) | copy-start | bytes 100
  32.8 21.6 %copy-start.7 = (f32[32,32]{1,0:T(8,128)S(1)}, f32[32,32]{1,0:T(8,128)}, u32[]{:S(2)}) copy-start(f32[32,32]{1,0:T(8,128)} %constant.44.clone.matrix_t_ref.refs_7_) | copy-start | bytes 12292
  42.1 6.2 %copy-start.8 = (f32[1,4096]{1,0:T(1,128)S(1)}, f32[1,4096]{1,0:T(1,128)}, u32[]{:S(2)}) copy-start(f32[1,4096]{1,0:T(1,128)} %get-tuple-element.17) | copy-start | bytes 49156
  42.1 12.3 %all-to-all-start.1 = ((f32[8,48,128]{2,1,0:T(8,128)}), f32[8,48,128]{2,1,0:T(8,128)S(1)}, u32[]{:S(2)}, u32[]{:S(2)}) async-start(f32[8,48,128]{2,1,0:T(8,128)} %shard_map.107), calls=%async_computation.1 | async-start | bytes 393216 | tf_op jit(solution)/shard_map/all_to_all | solution.py:538
  46.4 8.0 %copy-start.5 = (f32[5,32,128]{2,1,0:T(8,128)S(1)}, f32[5,32,128]{2,1,0:T(8,128)}, u32[]{:S(2)}) copy-start(f32[5,32,128]{2,1,0:T(8,128)} %constant.45.clone.table_ref.refs_8_) | copy-start | bytes 245764
  48.4 6.0 %copy-start.6 = (f32[32,32]{1,0:T(8,128)S(1)}, f32[32,32]{1,0:T(8,128)}, u32[]{:S(2)}) copy-start(f32[32,32]{1,0:T(8,128)} %constant.43.clone.matrix_ref.refs_6_) | copy-start | bytes 12292
  55.6 8.1 %collective-permute-start.2 = (f32[8,48,128]{2,1,0:T(8,128)S(1)}, f32[8,48,128]{2,1,0:T(8,128)S(1)}, u32[]{:S(2)}, u32[]{:S(2)}) collective-permute-start(f32[8,48,128]{2,1,0:T(8,128)S(1)} %get-tuple-element.18.refs_1_), channel_id=1, source_target_pairs={{7,0},{0,8},{8,16},{16,24},{24,28},{28,20},{20,12},{12,4},{4,1},{1... | collective-permute-start | bytes 589832 | tf_op jit(solution)/shard_map/ppermute | solution.py:555
  55.7 8.0 %collective-permute-start.3 = (f32[8,48,128]{2,1,0:T(8,128)S(1)}, f32[8,48,128]{2,1,0:T(8,128)S(1)}, u32[]{:S(2)}, u32[]{:S(2)}) collective-permute-start(f32[8,48,128]{2,1,0:T(8,128)S(1)} %get-tuple-element.18.refs_1_), channel_id=1, source_target_pairs={{8,0},{16,8},{24,16},{28,24},{20,28},{12,20},{4,12},{1,4},{9,1},{1... | collective-permute-start | bytes 589832 | tf_op jit(solution)/shard_map/ppermute | solution.py:555
  91.0 14.4 %all-to-all-start.2 = ((f32[8,96,128]{2,1,0:T(8,128)}), f32[8,96,128]{2,1,0:T(8,128)S(1)}, u32[]{:S(2)}, u32[]{:S(2)}) async-start(f32[8,96,128]{2,1,0:T(8,128)} %shard_map.109), calls=%async_computation.2 | async-start | bytes 786432 | tf_op jit(solution)/shard_map/all_to_all | solution.py:538
  105.5 16.1 %collective-permute-start.4 = (f32[10,4,512]{2,1,0:T(4,128)S(1)}, f32[10,4,512]{2,1,0:T(4,128)S(1)}, u32[]{:S(2)}, u32[]{:S(2)}) collective-permute-start(f32[10,4,512]{2,1,0:T(4,128)S(1)} %pad_maximum_fusion), channel_id=1, source_target_pairs={{0,1},{1,2},{2,3},{3,0},{4,5},{5,6},{6,7},{7,4},{8,9},{9,10},{10,1... | collective-permute-start | bytes 245768 | tf_op jit(solution)/shard_map/ppermute | solution.py:543

commit v5 on v4

--- a/solution.py
+++ b/solution.py
@@ -91,11 +91,20 @@
     return decay * ((inverse * inverse) * (inverse + math.log(2.0)))
 
 
+def offsets_of(where_ref, lists_ref, skip, origin, margin):
+    first = where_ref[0] + origin
+
+    def offset_at(block, m):
+        return jnp.clip(lists_ref[skip + block, m] - (first + block), -margin, margin)
+
+    return offset_at
+
+
 def whole_quads(beads):
     return -(-beads // QUAD) * QUAD
 
 
-def add_forces(group, blocks, margin, listed, offset_ref, charge_ref, coord_ref, scratch):
+def add_forces(group, blocks, margin, listed, offset_at, charge_ref, coord_ref, scratch):
     rows_ref, sums_ref, far_ref, heavy_ref, near_ref, total_ref, force_ref, *buffers = scratch
     weight_refs = buffers
     beads = coord_ref.shape[1]
@@ -194,7 +203,7 @@
         block = unit // pairs
         at_frame = block // frame
         base = at_frame * width + block - at_frame * frame + margin
-        return [base + offset_ref[block * listed + m] for m in range(listed)], unit - block * pairs
+        return [base + offset_at(block, m) for m in range(listed)], unit - block * pairs
 
     def parts(square):
         weight = weigh(square)
@@ -327,8 +336,11 @@
         coord_ref[...] = jnp.zeros(coord_ref.shape, f32)
 
 
-def message_kernel(x_ref, p_ref, types_ref, offsets_ref, message_ref, charge_ref, mass_ref):
-    _, local, edge = message_ref.shape
+def prepare_kernel(
+    blocks, x_ref, edge_ref, noise_ref, types_ref, lists_ref, rest_ref, message_ref, charge_ref, mass_ref
+):
+    steps, _, local, atoms = noise_ref.shape
+    edge = message_ref.shape[2]
     types = types_ref[...]
     charge = jnp.zeros(types.shape, f32)
     mass = jnp.zeros(types.shape, f32)
@@ -340,28 +352,31 @@
     for c in range(3):
         message_ref[c] = x_ref[c, :, :edge]
         message_ref[3 + c] = x_ref[c, :, edge:2 * edge]
-        message_ref[6 + c] = p_ref[c, :, :edge]
-    for i, row in enumerate([charge[:, :edge], charge[:, edge:2 * edge], mass[:, :edge], offsets_ref[...]]):
+        message_ref[6 + c] = edge_ref[c]
+    for i, row in enumerate([charge[:, :edge], charge[:, edge:2 * edge], mass[:, :edge]]):
         message_ref[9 + i] = jnp.broadcast_to(row, (local, edge))
-
-
-def pack_kernel(blocks, x_ref, noise_ref, out_ref):
-    steps, _, local, atoms = noise_ref.shape
+    message_ref[12] = jnp.zeros((local, edge), f32)
+    for block in range(edge // BLOCK):
+        at = block * BLOCK
+        message_ref[12, 0:1, at:at + lists_ref.shape[1]] = lists_ref[block:block + 1, :].astype(f32)
     for c in range(3 + 3 * steps):
         for block in range(atoms // BLOCK):
             lanes = slice(block * BLOCK, (block + 1) * BLOCK)
             value = x_ref[c, :, lanes] if c < 3 else noise_ref[c // 3 - 1, c % 3, :, lanes]
             row = row_of(c, block % blocks, blocks, local)
-            out_ref[block // blocks, row:row + local, :] = value
-
-
-def front_kernel(each, margin, listed, offset_ref, charge_ref, x_ref, p_ref, pout_ref, coord_ref, *scratch):
+            rest_ref[block // blocks, row:row + local, :] = value
+
+
+def front_kernel(
+    each, margin, listed, where_ref, lists_ref, charge_ref, x_ref, p_ref, pout_ref, coord_ref, *scratch
+):
     _, local, _ = x_ref.shape
     blocks = pout_ref.shape[0] * each
     clear(coord_ref, local)
     for c in range(3):
         coord_ref[c, :local, :] = x_ref[c, :, :(blocks + 2 * margin) * BLOCK]
-    add_forces(16, blocks, margin, listed, offset_ref, charge_ref, coord_ref, scratch)
+    offset_at = offsets_of(where_ref, lists_ref, margin, margin, margin)
+    add_forces(16, blocks, margin, listed, offset_at, charge_ref, coord_ref, scratch)
     force_ref = scratch[FORCE]
     for c in range(3):
         for block in range(blocks):
@@ -372,22 +387,25 @@
 
 
 def back_kernel(
-    each, margin, listed, offset_ref, charge_ref, x_ref, message_ref, p_ref, front_ref, pout_ref, coord_ref, *scratch
+    each, margin, listed, where_ref, lists_ref, charge_ref, x_ref, message_ref, p_ref, front_ref, *refs
 ):
+    count = lists_ref.shape[0] // each
+    pout_refs, (stage_ref, coord_ref, *scratch) = refs[:count], refs[count:]
     _, local, atoms = x_ref.shape
     edge = margin * BLOCK
     done = front_ref.shape[0]
     first = done * each
-    blocks = (pout_ref.shape[0] - done) * each
+    blocks = (count - done) * each
     own = atoms - first * BLOCK
     clear(coord_ref, local)
     for c in range(3):
         coord_ref[c, :local, :own] = x_ref[c, :, first * BLOCK:]
         for part in range(2):
             coord_ref[c, :local, own + part * edge:own + (part + 1) * edge] = message_ref[3 * part + c]
-    add_forces(8, blocks, margin, listed, offset_ref, charge_ref, coord_ref, scratch)
+    offset_at = offsets_of(where_ref, lists_ref, first, first + margin, margin)
+    add_forces(16, blocks, margin, listed, offset_at, charge_ref, coord_ref, scratch)
     force_ref = scratch[FORCE]
-    pout_ref[:done] = front_ref[...]
+    stage_ref[:done] = front_ref[...]
     for c in range(3):
         for block in range(blocks):
             lanes = slice(block * BLOCK, (block + 1) * BLOCK)
@@ -397,7 +415,20 @@
             else:
                 moment = message_ref[6 + c, :, at - atoms:at - atoms + BLOCK]
             row = row_of(c, block % each, each, local)
-            pout_ref[done + block // each, row:row + local, :] = moment + half_step * force_ref[c, :local, lanes]
+            stage_ref[done + block // each, row:row + local, :] = moment + half_step * force_ref[c, :local, lanes]
+    hand_out(stage_ref, pout_refs, where_ref[1])
+
+
+def hand_out(stage_ref, out_refs, place):
+    count = len(out_refs)
+    for away in range(count):
+        out_refs[away][...] = stage_ref[lax.rem(place + away, count)]
+
+
+def take_in(refs, stage_ref, place):
+    count = len(refs)
+    for away in range(count):
+        stage_ref[lax.rem(place - away + count, count)] = refs[away][...]
 
 
 def from_packed(ref, c, block, each, local):
@@ -405,7 +436,7 @@
     return ref[block // each, row:row + local, :]
 
 
-def upper_kernel(each, margin, listed, offset_ref, charge_ref, both_ref, pout_ref, coord_ref, *scratch):
+def upper_kernel(each, margin, listed, where_ref, lists_ref, charge_ref, both_ref, pout_ref, coord_ref, *scratch):
     _, local, atoms = pout_ref.shape
     blocks = atoms // BLOCK
     domain = both_ref.shape[0] * each
@@ -415,7 +446,8 @@
         for block in range(skipped, domain):
             at = (block - skipped) * BLOCK
             coord_ref[c, :local, at:at + BLOCK] = from_packed(both_ref, c, block, each, local)
-    add_forces(16, blocks, margin, listed, offset_ref, charge_ref, coord_ref, scratch)
+    offset_at = offsets_of(where_ref, lists_ref, domain - blocks, domain - blocks, margin)
+    add_forces(16, blocks, margin, listed, offset_at, charge_ref, coord_ref, scratch)
     force_ref = scratch[FORCE]
     for c in range(3):
         for block in range(blocks):
@@ -425,7 +457,8 @@
 
 
 def lower_kernel(
-    each, margin, listed, offset_ref, charge_ref, both_ref, message_ref, upper_ref, xout_ref, pout_ref, coord_ref, *scratch
+    each, margin, listed, where_ref, lists_ref, charge_ref, both_ref, message_ref, upper_ref, xout_ref, pout_ref, coord_ref,
+    *scratch,
 ):
     _, local, atoms = xout_ref.shape
     edge = margin * BLOCK
@@ -443,7 +476,8 @@
             lanes = slice(block * BLOCK, (block + 1) * BLOCK)
             xout_ref[c, :, lanes] = from_packed(both_ref, c, block - margin, each, local)
         pout_ref[c, :, lower:] = upper_ref[c]
-    add_forces(8, blocks, margin, listed, offset_ref, charge_ref, coord_ref, scratch)
+    offset_at = offsets_of(where_ref, lists_ref, 0, 0, margin)
+    add_forces(16, blocks, margin, listed, offset_at, charge_ref, coord_ref, scratch)
     force_ref = scratch[FORCE]
     for c in range(3):
         for block in range(blocks):
@@ -475,13 +509,13 @@
         )
 
 
-def modes_kernel(
-    blocks, noise_base, rest_ref, p_ref, mass_ref, matrix_ref, matrix_t_ref, table_ref,
-    xout_ref, pout_ref, coord_ref, moment_ref, noise_ref,
-):
-    local = p_ref.shape[1] // (3 * blocks)
+def modes_kernel(blocks, noise_base, count, where_ref, rest_ref, *refs):
+    p_refs, refs = refs[:count], refs[count:]
+    mass_ref, matrix_ref, matrix_t_ref, table_ref, xout_ref, pout_ref, stage_ref, coord_ref, moment_ref, noise_ref = refs
+    local = stage_ref.shape[1] // (3 * blocks)
+    take_in(p_refs, stage_ref, where_ref[1])
     unpack_beads(rest_ref, 0, blocks, local, coord_ref, 0)
-    unpack_beads(p_ref, 0, blocks, local, moment_ref, 0)
+    unpack_beads(stage_ref, 0, blocks, local, moment_ref, 0)
     unpack_beads(rest_ref, noise_base, blocks, local, noise_ref, 0)
 
     def store(c, x, p):
@@ -494,7 +528,7 @@
     )
 
 
-def middle_kernel(hops, blocks, listed, noise_base, joined, offset_ref, charge_ref, *refs):
+def middle_kernel(hops, blocks, listed, noise_base, joined, where_ref, lists_ref, charge_ref, *refs):
     parts = 2 * hops + 1
     x_refs = refs[:parts]
     p_ref, noise_ref, mass_ref, matrix_ref, matrix_t_ref, table_ref = refs[parts:parts + 6]
@@ -505,7 +539,8 @@
     width = blocks * BLOCK
     for part in range(parts):
         unpack_beads(x_refs[part], 0, blocks, local, coord_ref, part * width)
-    add_forces(16, blocks, hops * blocks, listed, offset_ref, charge_ref, coord_ref, scratch)
+    offset_at = offsets_of(where_ref, lists_ref, 0, 0, hops * blocks)
+    add_forces(16, blocks, hops * blocks, listed, offset_at, charge_ref, coord_ref, scratch)
     force_ref = scratch[FORCE]
     unpack_beads(p_ref, 0, blocks, local, coord_ref, 0)
     unpack_beads(noise_ref, noise_base, blocks, local, coord_ref, (parts - 1) * width)
@@ -536,6 +571,16 @@
     order = fold(pieces.shape[0])
     group = [order.index(at) for at in range(len(order))]
     return lax.all_to_all(pieces, "bead", split_axis=0, concat_axis=0, axis_index_groups=[group], tiled=True)
+
+
+def exchange_steps(pieces):
+    count = len(pieces)
+    order = fold(count)
+    return [
+        lax.ppermute(piece, "bead", [(order.index(i), order.index((i + away) % count)) for i in range(count)])
+        if away else piece
+        for away, piece in enumerate(pieces)
+    ]
 
 
 def passed(values, step):
@@ -573,67 +618,65 @@
     listed = neighbours.shape[1]
     order = fold(count)
 
-    own = lax.axis_index("space") * domain + jnp.arange(domain, dtype=jnp.int32)
-    offsets = jnp.clip(neighbours - own[:, None], -margin, margin).reshape(-1)
-    sent = jnp.pad(offsets[:margin * listed].astype(f32), (0, edge - margin * listed))[None, :]
-
-    (rest,) = call(
-        functools.partial(pack_kernel, blocks), (positions, thermal_noise), 0,
-        [(count, (3 + 3 * steps) * blocks * local, BLOCK)], [], 0,
-    )
+    packed = (count, 3 * blocks * local, BLOCK)
+    whole = [positions.shape, (3, local, edge), thermal_noise.shape, (1, atoms), neighbours.shape]
+    rest, message, charge, mass = call(
+        functools.partial(prepare_kernel, blocks),
+        (positions, momenta, thermal_noise, atom_types[None, :], neighbours), 0,
+        [(count, (1 + steps) * packed[1], BLOCK), (13, local, edge), (1, atoms), (1, atoms)], [], 0,
+        [pl.BlockSpec(shape, lambda i, rank=len(shape): (0,) * rank) for shape in whole],
+    )
+    message = passed(message, -1)
     rest = exchange(rest)
-
-    message, charge, mass = call(
-        message_kernel, (positions, momenta, atom_types[None, :], sent), 0,
-        [(13, local, edge), (1, atoms), (1, atoms)], [], 0,
-        [
-            pl.BlockSpec(shape, lambda i, rank=len(shape): (0,) * rank)
-            for shape in ((3, local, 2 * edge), (3, local, edge), (1, atoms), (1, edge))
-        ],
-    )
-    message = passed(message, -1)
     side = message[9:, 0]
     first_charge = jnp.concatenate([charge, side[:1], side[1:2]], axis=1)
     moved_mass = jnp.concatenate([mass[0, edge:], side[2]])
-    moved_offsets = jnp.concatenate([offsets[margin * listed:], side[3, :margin * listed].astype(jnp.int32)])
+    domains = lax.axis_size("space")
+    at_space = lax.axis_index("space")
+    foreign = side[3].reshape(margin, BLOCK)[:, :listed].astype(jnp.int32)
+    foreign = foreign + jnp.where(at_space == domains - 1, domains * domain, 0)
+    moved_lists = jnp.concatenate([neighbours[margin:], foreign], axis=0)
 
     place = jnp.asarray(np.array(order, np.int32))[lax.axis_index("bead")]
     near_charge = lax.dynamic_slice_in_dim(first_charge, place * share, share + 2 * edge, axis=1)
     near_mass = lax.dynamic_slice_in_dim(moved_mass, place * share, share)[None, :]
-    near_offsets = lax.dynamic_slice_in_dim(moved_offsets, place * blocks * listed, blocks * listed)
+    near_lists = lax.dynamic_slice_in_dim(moved_lists, place * blocks, blocks)
+    first_block = at_space * domain
+    where = jnp.stack([first_block, place]).astype(jnp.int32)
+    near_where = jnp.stack([first_block + margin + place * blocks, place]).astype(jnp.int32)
 
     matrix, tables = mode_constants(beads)
     at = np.concatenate([order.index(g) * local + np.arange(local) for g in range(count)])
     matrix = matrix[at][:, at]
     fixed = (near_mass, jnp.asarray(matrix), jnp.asarray(np.ascontiguousarray(matrix.T)), jnp.asarray(tables[:, at]))
 
-    packed = (count, 3 * blocks * local, BLOCK)
     pairs = beads * blocks * listed * BLOCK * BLOCK
-    frame = min(FRAME, domain)
-    most = domain - frame
+    frame = min(FRAME, domain // 2)
+    most = domain - 2 * frame
     window_atoms = (most + 2 * margin) * BLOCK
     (moment,) = call(
         functools.partial(front_kernel, blocks, margin, listed),
-        (offsets[margin * listed:(margin + most) * listed], charge[:, :window_atoms], positions, momenta), 1,
+        (where, neighbours, charge[:, :window_atoms], positions, momenta), 2,
         [(most // blocks,) + packed[1:]], force_scratch(local, most, margin, listed), pairs * most // domain,
     )
     moment, rest = lax.optimization_barrier((moment, rest))
     rest = round_ring(rest, hops)
-    (moment,) = call(
+    moments = call(
         functools.partial(back_kernel, blocks, margin, listed),
-        (moved_offsets[most * listed:], first_charge[:, most * BLOCK:], positions, message, momenta, moment), 1,
-        [packed], force_scratch(local, frame, margin, listed), pairs * frame // domain,
-    )
-    moment, rest = lax.optimization_barrier((moment, rest))
+        (where, moved_lists, first_charge[:, most * BLOCK:], positions, message, momenta, moment), 2,
+        [packed[1:]] * count, [pltpu.VMEM(packed, f32)] + force_scratch(local, domain - most, margin, listed),
+        pairs * (domain - most) // domain,
+    )
     coords, moment = call(
-        functools.partial(modes_kernel, blocks, 3), (rest, exchange(moment)) + fixed, 0, [packed] * 2,
-        [pltpu.VMEM((3, beads, share), f32)] * 3, 0,
+        functools.partial(modes_kernel, blocks, 3, count),
+        (where, rest) + tuple(exchange_steps(moments)) + fixed, 1, [packed] * 2,
+        [pltpu.VMEM(packed, f32)] + [pltpu.VMEM((3, beads, share), f32)] * 3, 0,
     )
     for step in range(1, steps):
         joined = step == steps - 1
         out = call(
             functools.partial(middle_kernel, hops, blocks, listed, 3 * step + 3, joined),
-            (near_offsets, near_charge) + tuple(window(coords, hops)) + (moment, rest) + fixed, 1,
+            (near_where, near_lists, near_charge) + tuple(window(coords, hops)) + (moment, rest) + fixed, 2,
             [(count, 6 * blocks * local, BLOCK)] if joined else [packed] * 2,
             force_scratch(beads, blocks, margin, listed), pairs,
         )
@@ -651,14 +694,14 @@
     ], axis=0), 1)
     (upper,) = call(
         functools.partial(upper_kernel, blocks, margin, listed),
-        (offsets[frame * listed:], first_charge[:, frame * BLOCK - edge:atoms + edge], both), 1,
+        (where, neighbours, first_charge[:, 2 * frame * BLOCK - edge:atoms + edge], both), 2,
         [(3, local, most * BLOCK)], force_scratch(local, most, margin, listed), pairs * most // domain,
     )
-    last_charge = jnp.concatenate([message[9, :1], first_charge[:, :frame * BLOCK + edge]], axis=1)
+    last_charge = jnp.concatenate([message[9, :1], first_charge[:, :2 * frame * BLOCK + edge]], axis=1)
     return tuple(call(
         functools.partial(lower_kernel, blocks, margin, listed),
-        (offsets[:frame * listed], last_charge, both, message, upper), 1,
-        [(3, local, atoms)] * 2, force_scratch(local, frame, margin, listed), pairs * frame // domain,
+        (where, neighbours, last_charge, both, message, upper), 2,
+        [(3, local, atoms)] * 2, force_scratch(local, domain - most, margin, listed), pairs * (domain - most) // domain,
     ))
 
 

time: 129 us -> 130 us (level)
  starting transfers between devices: 19.9 us -> 24.9 us
  waiting for transfers between devices: 24.4 us -> 19.8 us
  other arithmetic: 0.25 us -> 1.64 us
    ppermute x0 -> x7, starting transfers between devices: none -> 8.8 us  [exchange_steps(): lax.ppermute(piece, 'bead', [(order.index(i), order.index((i + away) % co...]
    all_to_all x3 -> x2, starting transfers between devices: 14.1 us -> 8.46 us  [exchange(): lax.all_to_all(pieces, 'bead', split_axis=0, concat_axis=0, axis_index_gr...]
    all_to_all x3 -> x2, waiting for transfers between devices: 16.4 us -> 10.9 us  [exchange(): lax.all_to_all(pieces, 'bead', split_axis=0, concat_axis=0, axis_index_gr...]
    ppermute x0 -> x7, waiting for transfers between devices: none -> 3.75 us  [exchange_steps(): lax.ppermute(piece, 'bead', [(order.index(i), order.index((i + away) % co...]
    ppermute x3, waiting for transfers between devices: 8.06 us -> 5.11 us  [round_ring(): lax.ppermute(values, ('bead', 'space'), [(device[(at + hop) % total], dev...]
    ppermute x2, starting transfers between devices: 2.73 us -> 4.81 us  [passed(): lax.ppermute(values, 'space', [(i, (i + step) % count) for i in range(cou...]
    another operation x0 -> x2, other arithmetic: none -> 1.41 us  [the longest x1 0.7 us: body(): jnp.stack([first_block + margin + place * blocks, place]).astype(jnp.int32)]
    pallas_call x8 -> x7, Pallas kernels: 75.9 us -> 76.5 us  [call(): pl.pallas_call(kernel, out_shape=[jax.ShapeDtypeStruct(shape, f32) for sh...]
  transfers between devices with their start and end apart: 8 -> 14, of which waited for: 4 -> 5; matrix products, arithmetic and copies ran while one was open for 2% -> 2% of each run, Pallas kernels for 31% -> 26%
where the time goes in v5:
time: 130 us; the launch traced here: 129 us
  Pallas kernels  76.5 us (59%)
  starting transfers between devices  24.9 us (19%)
  waiting for transfers between devices  19.8 us (15%)
  local copies, waits for them, and re-layouts  4.5 us (3%)
  between operations  2.15 us (2%)
  other arithmetic  1.64 us (1%)
    pallas_call x7, Pallas kernels, call(): pl.pallas_call(kernel, out_shape=[jax.ShapeDtypeStruct(shape, f32) for sh...  76.5 us
    all_to_all x2, waiting for transfers between devices, exchange(): lax.all_to_all(pieces, 'bead', split_axis=0, concat_axis=0, axis_index_gr...  10.9 us
    ppermute x7, starting transfers between devices, exchange_steps(): lax.ppermute(piece, 'bead', [(order.index(i), order.index((i + away) % co...  8.8 us
    all_to_all x2, starting transfers between devices, exchange(): lax.all_to_all(pieces, 'bead', split_axis=0, concat_axis=0, axis_index_gr...  8.46 us
    ppermute x3, waiting for transfers between devices, round_ring(): lax.ppermute(values, ('bead', 'space'), [(device[(at + hop) % total], dev...  5.11 us
    ppermute x2, starting transfers between devices, passed(): lax.ppermute(values, 'space', [(i, (i + step) % count) for i in range(cou...  4.81 us
    ppermute x7, waiting for transfers between devices, exchange_steps(): lax.ppermute(piece, 'bead', [(order.index(i), order.index((i + away) % co...  3.75 us
    unnamed x22, local copies, waits for them, and re-layouts  3.52 us
  transfers between devices with their start and end apart: 14, of which 5 were waited for; matrix products, arithmetic and copies ran while one was open for 2% of the time, Pallas kernels for 26%

profile of v5, /device:TPU:0, one launch (start us, length us, event | category | flops | bytes accessed | tf_op | source)
XLA Modules:
  0.0 129.5 jit_solution(5446239849497781401)
XLA Ops:
  0.6 1.4 %copy.28.lists_ref = s32[32,5]{1,0:T(8,128)} copy(s32[32,5]{0,1:T(8,128)} %param.12) | data formatting | bytes 1280 | tf_op args[3]
  2.0 2.0 %shard_map.104 = (f32[8,144,128]{2,1,0:T(8,128)}, f32[13,4,512]{2,1,0:T(4,128)}, f32[1,4096]{1,0:T(1,128)}, f32[1,4096]{1,0:T(1,128)}) custom-call(f32[3,4,4096]{2,1,0:T(4,128)} %x_ref.5, f32[3,4,4096]{2,1,0:T(4,128)} %p_ref.3, f32[2,3,4,4096]{3,2,1,0:T(4,128)} %noise_ref.1, s32[1,4096]{1,0:T(1,128)} %bitcast.42, s32[32,5]{1,0:T(8,128)} %copy.28.lists_ref), custom_call_target="tpu_custom_call" | custom-call | flops 1024 | bytes 4194304 | tf_op jit(solution)/shard_map/pallas_call | solution.py:295
  4.0 3.9 %collective-permute-start = (f32[13,4,512]{2,1,0:T(4,128)}, f32[13,4,512]{2,1,0:T(4,128)S(1)}, u32[]{:S(2)}, u32[]{:S(2)}) collective-permute-start(f32[13,4,512]{2,1,0:T(4,128)} %get-tuple-element.18), channel_id=1, source_target_pairs={{0,3},{1,0},{2,1},{3,2},{4,7},{5,4},{6,5},{7,6},{8,11},{9,8},{10,9... | collective-permute-start | bytes 319496 | tf_op jit(solution)/shard_map/ppermute | solution.py:588
  7.9 5.0 %all-to-all-start = ((f32[8,144,128]{2,1,0:T(8,128)}), f32[8,144,128]{2,1,0:T(8,128)S(1)}, u32[]{:S(2)}, u32[]{:S(2)}) async-start(f32[8,144,128]{2,1,0:T(8,128)} %get-tuple-element.20), calls=%async_computation | async-start | bytes 1179648 | tf_op jit(solution)/shard_map/all_to_all | solution.py:573
  12.9 0.7 copy-done.8
  13.7 0.0 copy-start.9
  13.7 0.6 copy-done.9
  14.4 0.6 dynamic_slice.12
  15.0 0.7 pad_add_fusion.1.where_ref
  15.7 0.1 slice.62
  17.1 0.7 pad_add_fusion.2.where_ref
  17.8 0.0 collective-permute-done.message_ref
  17.8 0.0 copy-start.3
  17.9 0.7 copy-done.3
  18.5 11.1 %shard_map.105.front_ref = f32[4,48,128]{2,1,0:T(8,128)S(1)} custom-call(s32[2]{0:T(128)S(1)} %pad_add_fusion.1.where_ref, s32[32,5]{1,0:T(8,128)S(1)} %copy-done.3, f32[1,3072]{1,0:T(1,128)S(1)} %get-tuple-element.42.charge_ref, f32[3,4,4096]{2,1,0:T(4,128)S(1)} %copy-done, f32[3,4,4096]{2,1,0:T(4,128)S(1)} %copy-done.1), custom_call_target="tpu_custom_call" | custom-call | flops 104858624 | bytes 4194304 | tf_op jit(solution)/shard_map/pallas_call | solution.py:295
  29.7 0.0 all-to-all-done
  29.7 0.7 collective-permute-start.1
  30.4 0.1 copy.29
  30.5 0.1 pad_add_fusion
  30.6 0.1 copy.21.lists_ref
  30.7 11.2 %shard_map.106 = (f32[48,128]{1,0:T(8,128)S(1)}, f32[48,128]{1,0:T(8,128)S(1)}, f32[48,128]{1,0:T(8,128)S(1)}, f32[48,128]{1,0:T(8,128)S(1)}, f32[48,128]{1,0:T(...) custom-call(s32[2]{0:T(128)S(1)} %pad_add_fusion.1.where_ref, ...), custom_call_target="tpu_custom_call" | custom-call | flops 104858624 | bytes 4194304 | tf_op jit(solution)/shard_map/pallas_call | solution.py:295
  41.9 1.4 %collective-permute-start.2 = (f32[48,128]{1,0:T(8,128)S(1)}, f32[48,128]{1,0:T(8,128)S(1)}, u32[]{:S(2)}, u32[]{:S(2)}) collective-permute-start(f32[48,128]{1,0:T(8,128)S(1)} %get-tuple-element.24), channel_id=1, source_target_pairs={{0,8},{8,16},{16,24},{24,28},{28,20},{20,12},{12,4},{4,0},{1,9},{9... | collective-permute-start | bytes 73736 | tf_op jit(solution)/shard_map/ppermute | solution.py:580
  43.3 2.9 %collective-permute-start.3 = (f32[48,128]{1,0:T(8,128)S(1)}, f32[48,128]{1,0:T(8,128)S(1)}, u32[]{:S(2)}, u32[]{:S(2)}) collective-permute-start(f32[48,128]{1,0:T(8,128)S(1)} %get-tuple-element.25), channel_id=1, source_target_pairs={{0,16},{8,24},{16,28},{24,20},{28,12},{20,4},{12,0},{4,8},{1,17},{... | collective-permute-start | bytes 73736 | tf_op jit(solution)/shard_map/ppermute | solution.py:580
  46.2 0.7 collective-permute-start.4
  46.9 1.7 %collective-permute-start.5 = (f32[48,128]{1,0:T(8,128)S(1)}, f32[48,128]{1,0:T(8,128)S(1)}, u32[]{:S(2)}, u32[]{:S(2)}) collective-permute-start(f32[48,128]{1,0:T(8,128)S(1)} %get-tuple-element.27), channel_id=1, source_target_pairs={{0,28},{8,20},{16,12},{24,4},{28,0},{20,8},{12,16},{4,24},{1,29},{... | collective-permute-start | bytes 73736 | tf_op jit(solution)/shard_map/ppermute | solution.py:580
  48.6 0.0 collective-permute-done.2.refs_1_
  48.6 0.4 collective-permute-start.6
  49.0 0.0 collective-permute-done.3.refs_2_
  49.0 1.8 %collective-permute-start.7 = (f32[48,128]{1,0:T(8,128)S(1)}, f32[48,128]{1,0:T(8,128)S(1)}, u32[]{:S(2)}, u32[]{:S(2)}) collective-permute-start(f32[48,128]{1,0:T(8,128)S(1)} %get-tuple-element.29), channel_id=1, source_target_pairs={{0,12},{8,4},{16,0},{24,8},{28,16},{20,24},{12,28},{4,20},{1,13},{... | collective-permute-start | bytes 73736 | tf_op jit(solution)/shard_map/ppermute | solution.py:580
  50.7 0.0 collective-permute-done.4.refs_3_
  50.7 0.0 collective-permute-start.8
  50.7 0.1 fusion
  50.8 1.2 collective-permute-done.5.refs_4_
  52.0 2.2 %collective-permute-done.6.refs_5_ = f32[48,128]{1,0:T(8,128)S(1)} collective-permute-done((f32[48,128]{1,0:T(8,128)S(1)}, f32[48,128]{1,0:T(8,128)S(1)}, u32[]{:S(2)}, u32[]{:S(2)}) %collective-permute-start.6) | collective-permute-done | bytes 24608 | tf_op jit(solution)/shard_map/ppermute | solution.py:580
  54.2 0.3 collective-permute-done.8.refs_7_
  54.5 0.0 collective-permute-done.1.rest_ref.refs_4_
  54.6 1.8 %shard_map.107 = (f32[8,48,128]{2,1,0:T(8,128)S(1)}, f32[8,48,128]{2,1,0:T(8,128)S(1)}) custom-call(s32[2]{0:T(128)S(1)} %pad_add_fusion.1.where_ref, f32[8,144,128]{2,1,0:T(8,128)S(1)} %collective-permute-done.1.rest_ref.refs_4_, f32[48,128]{1,0:T(8,128)S(1)} %get-tuple-element.23.refs_0_, f32[48,128]{1,0:T(8,128)S(1)} %collective-permute-done.2.refs_1_, ...), custom_call_target="tpu_custom_call" | custom-call | flops 1024 | bytes 4194304 | tf_op jit(solution)/shard_map/pallas_call | solution.py:295
  56.4 0.1 collective-permute-start.10
  56.4 2.0 %collective-permute-start.9 = (f32[8,48,128]{2,1,0:T(8,128)S(1)}, f32[8,48,128]{2,1,0:T(8,128)S(1)}, u32[]{:S(2)}, u32[]{:S(2)}) collective-permute-start(f32[8,48,128]{2,1,0:T(8,128)S(1)} %get-tuple-element.32.refs_1_), channel_id=1, source_target_pairs={{7,0},{0,8},{8,16},{16,24},{24,28},{28,20},{20,12},{12,4},{4,1},{1... | collective-permute-start | bytes 589832 | tf_op jit(solution)/shard_map/ppermute | solution.py:600
  58.4 5.1 %collective-permute-done.10.refs_2_ = f32[8,48,128]{2,1,0:T(8,128)S(1)} collective-permute-done((f32[8,48,128]{2,1,0:T(8,128)S(1)}, f32[8,48,128]{2,1,0:T(8,128)S(1)}, u32[]{:S(2)}, u32[]{:S(2)}) %collective-permute-start.10) | collective-permute-done | bytes 196640 | tf_op jit(solution)/shard_map/ppermute | solution.py:600
  63.6 0.0 collective-permute-done.9.refs_0_
  63.6 27.4 %shard_map.108 = f32[8,96,128]{2,1,0:T(8,128)} custom-call(s32[2]{0:T(128)S(1)} %pad_add_fusion.2.where_ref, s32[4,5]{1,0:T(4,128)S(1)} %constant_dynamic-slice_fusion.1.lists_ref, f32[1,1536]{1,0:T(1,128)S(1)} %constant_dynamic-slice_fusion.charge_ref, f32[8,48,128]{2,1,0:T(8,128)S(1)} %collective-permute-done.9.refs_0_, ...), custom_call_target="tpu_custom_call" | custom-call | flops 209716224 | bytes 4194304 | tf_op jit(solution)/shard_map/pallas_call | solution.py:295
  90.9 3.5 %all-to-all-start.1 = ((f32[8,96,128]{2,1,0:T(8,128)}), f32[8,96,128]{2,1,0:T(8,128)S(1)}, u32[]{:S(2)}, u32[]{:S(2)}) async-start(f32[8,96,128]{2,1,0:T(8,128)} %shard_map.108), calls=%async_computation.1 | async-start | bytes 786432 | tf_op jit(solution)/shard_map/all_to_all | solution.py:573
  94.4 10.9 %all-to-all-done.1.both_ref = f32[8,96,128]{2,1,0:T(8,128)S(1)} async-done(((f32[8,96,128]{2,1,0:T(8,128)}), f32[8,96,128]{2,1,0:T(8,128)S(1)}, u32[]{:S(2)}, u32[]{:S(2)}) %all-to-all-start.1) | async-done | bytes 393248 | tf_op jit(solution)/shard_map/all_to_all | solution.py:573
  105.5 0.9 collective-permute-start.11
  106.4 11.1 %shard_map.109.upper_ref = f32[3,4,2048]{2,1,0:T(4,128)S(1)} custom-call(s32[2]{0:T(128)S(1)} %pad_add_fusion.1.where_ref, s32[32,5]{1,0:T(8,128)S(1)} %copy-done.3, f32[1,3072]{1,0:T(1,128)S(1)} %get-tuple-element.41.charge_ref, f32[8,96,128]{2,1,0:T(8,128)S(1)} %all-to-all-done.1.both_ref), custom_call_target="tpu_custom_call" | custom-call | flops 104858624 | bytes 4194304 | tf_op jit(solution)/shard_map/pallas_call | solution.py:295
  117.6 0.0 collective-permute-done.11.message_ref
  117.6 11.9 %shard_map.110 = (f32[3,4,4096]{2,1,0:T(4,128)}, f32[3,4,4096]{2,1,0:T(4,128)}) custom-call(s32[2]{0:T(128)S(1)} %pad_add_fusion.1.where_ref, s32[32,5]{1,0:T(8,128)S(1)} %copy-done.3, f32[1,3072]{1,0:T(1,128)S(1)} %pad_maximum_fusion.3.charge_ref, f32[8,96,128]{2,1,0:T(8,128)S(1)} %all-to-all-done.1.both_ref, ...), custom_call_target="tpu_custom_call" | custom-call | flops 104858624 | bytes 4194304 | tf_op jit(solution)/shard_map/pallas_call | solution.py:295
  (37 shorter events, 0.3 us)
Async XLA Ops:
  4.0 13.8 %collective-permute-start = (f32[13,4,512]{2,1,0:T(4,128)}, f32[13,4,512]{2,1,0:T(4,128)S(1)}, u32[]{:S(2)}, u32[]{:S(2)}) collective-permute-start(f32[13,4,512]{2,1,0:T(4,128)} %get-tuple-element.18), channel_id=1, source_target_pairs={{0,3},{1,0},{2,1},{3,2},{4,7},{5,4},{6,5},{7,6},{8,11},{9,8},{10,9... | collective-permute-start | bytes 319496 | tf_op jit(solution)/shard_map/ppermute | solution.py:588
  7.9 9.9 %copy-start = (f32[3,4,4096]{2,1,0:T(4,128)S(1)}, f32[3,4,4096]{2,1,0:T(4,128)}, u32[]{:S(2)}) copy-start(f32[3,4,4096]{2,1,0:T(4,128)} %x_ref.5) | copy-start | bytes 589828
  7.9 9.9 %copy-start.1 = (f32[3,4,4096]{2,1,0:T(4,128)S(1)}, f32[3,4,4096]{2,1,0:T(4,128)}, u32[]{:S(2)}) copy-start(f32[3,4,4096]{2,1,0:T(4,128)} %p_ref.3) | copy-start | bytes 589828
  7.9 21.8 %all-to-all-start = ((f32[8,144,128]{2,1,0:T(8,128)}), f32[8,144,128]{2,1,0:T(8,128)S(1)}, u32[]{:S(2)}, u32[]{:S(2)}) async-start(f32[8,144,128]{2,1,0:T(8,128)} %get-tuple-element.20), calls=%async_computation | async-start | bytes 1179648 | tf_op jit(solution)/shard_map/all_to_all | solution.py:573
  12.9 0.7 copy-start.8
  13.7 0.7 copy-start.9
  14.4 1.4 %copy-start.7 = (s32[32,5]{0,1:T(8,128)S(1)}, s32[32,5]{0,1:T(8,128)}, u32[]{:S(2)}) copy-start(s32[32,5]{0,1:T(8,128)} %param.12) | copy-start | bytes 1924
  17.1 0.7 copy-start.6
  17.8 0.7 copy-start.3
  29.7 24.8 %collective-permute-start.1 = (f32[8,144,128]{2,1,0:T(8,128)S(1)}, f32[8,144,128]{2,1,0:T(8,128)S(1)}, u32[]{:S(2)}, u32[]{:S(2)}) collective-permute-start(f32[8,144,128]{2,1,0:T(8,128)S(1)} %all-to-all-done), channel_id=1, source_target_pairs={{8,0},{16,8},{24,16},{28,24},{20,28},{12,20},{4,12},{1,4},{9,1},{1... | collective-permute-start | bytes 1769480 | tf_op jit(solution)/shard_map/ppermute | solution.py:600
  30.7 23.8 %copy-start.2 = (f32[5,32,128]{2,1,0:T(8,128)S(1)}, f32[5,32,128]{2,1,0:T(8,128)}, u32[]{:S(2)}) copy-start(f32[5,32,128]{2,1,0:T(8,128)} %constant.41.clone.refs_11_.refs_8_) | copy-start | bytes 245764
  41.9 6.7 %collective-permute-start.2 = (f32[48,128]{1,0:T(8,128)S(1)}, f32[48,128]{1,0:T(8,128)S(1)}, u32[]{:S(2)}, u32[]{:S(2)}) collective-permute-start(f32[48,128]{1,0:T(8,128)S(1)} %get-tuple-element.24), channel_id=1, source_target_pairs={{0,8},{8,16},{16,24},{24,28},{28,20},{20,12},{12,4},{4,0},{1,9},{9... | collective-permute-start | bytes 73736 | tf_op jit(solution)/shard_map/ppermute | solution.py:580
  43.3 5.7 %collective-permute-start.3 = (f32[48,128]{1,0:T(8,128)S(1)}, f32[48,128]{1,0:T(8,128)S(1)}, u32[]{:S(2)}, u32[]{:S(2)}) collective-permute-start(f32[48,128]{1,0:T(8,128)S(1)} %get-tuple-element.25), channel_id=1, source_target_pairs={{0,16},{8,24},{16,28},{24,20},{28,12},{20,4},{12,0},{4,8},{1,17},{... | collective-permute-start | bytes 73736 | tf_op jit(solution)/shard_map/ppermute | solution.py:580
  46.2 4.5 %collective-permute-start.4 = (f32[48,128]{1,0:T(8,128)S(1)}, f32[48,128]{1,0:T(8,128)S(1)}, u32[]{:S(2)}, u32[]{:S(2)}) collective-permute-start(f32[48,128]{1,0:T(8,128)S(1)} %get-tuple-element.26), channel_id=1, source_target_pairs={{0,24},{8,28},{16,20},{24,12},{28,4},{20,0},{12,8},{4,16},{1,25},{... | collective-permute-start | bytes 73736 | tf_op jit(solution)/shard_map/ppermute | solution.py:580
  46.9 5.2 %collective-permute-start.5 = (f32[48,128]{1,0:T(8,128)S(1)}, f32[48,128]{1,0:T(8,128)S(1)}, u32[]{:S(2)}, u32[]{:S(2)}) collective-permute-start(f32[48,128]{1,0:T(8,128)S(1)} %get-tuple-element.27), channel_id=1, source_target_pairs={{0,28},{8,20},{16,12},{24,4},{28,0},{20,8},{12,16},{4,24},{1,29},{... | collective-permute-start | bytes 73736 | tf_op jit(solution)/shard_map/ppermute | solution.py:580
  48.6 6.0 %copy-start.5 = (f32[32,32]{1,0:T(8,128)S(1)}, f32[32,32]{1,0:T(8,128)}, u32[]{:S(2)}) copy-start(f32[32,32]{1,0:T(8,128)} %constant.40.clone.refs_10_.refs_7_) | copy-start | bytes 12292
  48.6 6.0 %copy-start.4 = (f32[32,32]{1,0:T(8,128)S(1)}, f32[32,32]{1,0:T(8,128)}, u32[]{:S(2)}) copy-start(f32[32,32]{1,0:T(8,128)} %constant.39.clone.refs_9_.refs_6_) | copy-start | bytes 12292
  48.6 5.6 %collective-permute-start.6 = (f32[48,128]{1,0:T(8,128)S(1)}, f32[48,128]{1,0:T(8,128)S(1)}, u32[]{:S(2)}, u32[]{:S(2)}) collective-permute-start(f32[48,128]{1,0:T(8,128)S(1)} %get-tuple-element.28), channel_id=1, source_target_pairs={{0,20},{8,12},{16,4},{24,0},{28,8},{20,16},{12,24},{4,28},{1,21},{... | collective-permute-start | bytes 73736 | tf_op jit(solution)/shard_map/ppermute | solution.py:580
  49.0 5.3 %collective-permute-start.7 = (f32[48,128]{1,0:T(8,128)S(1)}, f32[48,128]{1,0:T(8,128)S(1)}, u32[]{:S(2)}, u32[]{:S(2)}) collective-permute-start(f32[48,128]{1,0:T(8,128)S(1)} %get-tuple-element.29), channel_id=1, source_target_pairs={{0,12},{8,4},{16,0},{24,8},{28,16},{20,24},{12,28},{4,20},{1,13},{... | collective-permute-start | bytes 73736 | tf_op jit(solution)/shard_map/ppermute | solution.py:580
  50.7 3.8 %collective-permute-start.8 = (f32[48,128]{1,0:T(8,128)S(1)}, f32[48,128]{1,0:T(8,128)S(1)}, u32[]{:S(2)}, u32[]{:S(2)}) collective-permute-start(f32[48,128]{1,0:T(8,128)S(1)} %get-tuple-element.30), channel_id=1, source_target_pairs={{0,4},{8,0},{16,8},{24,16},{28,24},{20,28},{12,20},{4,12},{1,5},{9... | collective-permute-start | bytes 73736 | tf_op jit(solution)/shard_map/ppermute | solution.py:580
  56.4 7.2 %collective-permute-start.10 = (f32[8,48,128]{2,1,0:T(8,128)S(1)}, f32[8,48,128]{2,1,0:T(8,128)S(1)}, u32[]{:S(2)}, u32[]{:S(2)}) collective-permute-start(f32[8,48,128]{2,1,0:T(8,128)S(1)} %get-tuple-element.32.refs_1_), channel_id=1, source_target_pairs={{8,0},{16,8},{24,16},{28,24},{20,28},{12,20},{4,12},{1,4},{9,1},{1... | collective-permute-start | bytes 589832 | tf_op jit(solution)/shard_map/ppermute | solution.py:600
  56.4 7.1 %collective-permute-start.9 = (f32[8,48,128]{2,1,0:T(8,128)S(1)}, f32[8,48,128]{2,1,0:T(8,128)S(1)}, u32[]{:S(2)}, u32[]{:S(2)}) collective-permute-start(f32[8,48,128]{2,1,0:T(8,128)S(1)} %get-tuple-element.32.refs_1_), channel_id=1, source_target_pairs={{7,0},{0,8},{8,16},{16,24},{24,28},{28,20},{20,12},{12,4},{4,1},{1... | collective-permute-start | bytes 589832 | tf_op jit(solution)/shard_map/ppermute | solution.py:600
  90.9 14.4 %all-to-all-start.1 = ((f32[8,96,128]{2,1,0:T(8,128)}), f32[8,96,128]{2,1,0:T(8,128)S(1)}, u32[]{:S(2)}, u32[]{:S(2)}) async-start(f32[8,96,128]{2,1,0:T(8,128)} %shard_map.108), calls=%async_computation.1 | async-start | bytes 786432 | tf_op jit(solution)/shard_map/all_to_all | solution.py:573
  105.5 12.1 %collective-permute-start.11 = (f32[10,4,512]{2,1,0:T(4,128)S(1)}, f32[10,4,512]{2,1,0:T(4,128)S(1)}, u32[]{:S(2)}, u32[]{:S(2)}) collective-permute-start(f32[10,4,512]{2,1,0:T(4,128)S(1)} %pad_maximum_fusion), channel_id=1, source_target_pairs={{0,1},{1,2},{2,3},{3,0},{4,5},{5,6},{6,7},{7,4},{8,9},{9,10},{10,1... | collective-permute-start | bytes 245768 | tf_op jit(solution)/shard_map/ppermute | solution.py:588

commit v6 on v4

--- a/solution.py
+++ b/solution.py
@@ -91,11 +91,37 @@
     return decay * ((inverse * inverse) * (inverse + math.log(2.0)))
 
 
+def own_place(count):
+    bead = lax.axis_index("bead")
+    half = lax.div(bead, 2)
+    return jnp.where(lax.rem(bead, 2) == 0, half, count - 1 - half)
+
+
+def offsets_of(lists_ref, skip, origin, margin):
+    first = lax.axis_index("space") * lists_ref.shape[1] + origin
+
+    def offset_at(block, m):
+        return jnp.clip(lists_ref[m, skip + block] - (first + block), -margin, margin)
+
+    return offset_at
+
+
+def charges(types):
+    charge = jnp.zeros(types.shape, f32)
+    for kind in range(4):
+        charge = jnp.where(types == kind, CHARGES[kind], charge)
+    return charge
+
+
+def odd_tiles(lines):
+    return lines + 8 * (1 - lines // 8 % 2)
+
+
 def whole_quads(beads):
     return -(-beads // QUAD) * QUAD
 
 
-def add_forces(group, blocks, margin, listed, offset_ref, charge_ref, coord_ref, scratch):
+def add_forces(group, blocks, margin, listed, offset_at, charge_ref, coord_ref, scratch, charge_from=0):
     rows_ref, sums_ref, far_ref, heavy_ref, near_ref, total_ref, force_ref, *buffers = scratch
     weight_refs = buffers
     beads = coord_ref.shape[1]
@@ -105,10 +131,14 @@
     middle = margin + (frame - 1) / 2.0
     at_once = max(1, 8 // beads)
     lines = at_once * beads
+    apart = odd_tiles(lines)
     units = blocks * pairs
 
+    def charge_at(block):
+        return charge_ref[:, pl.ds(pl.multiple_of((charge_from + block) * BLOCK, BLOCK), BLOCK)]
+
     def put(ref, slot, k, value):
-        ref[slot, k * lines:(k + 1) * lines, :] = value
+        ref[slot, k * apart:k * apart + lines, :] = value
 
     def centred(block, place):
         spans = [pl.ds(pl.multiple_of((block + i) * BLOCK, BLOCK), BLOCK) for i in range(at_once)]
@@ -121,7 +151,7 @@
         coords[0] = coords[0] + shift
         norm = coords[0] * coords[0] + coords[1] * coords[1] + coords[2] * coords[2]
         charge = jnp.concatenate(
-            [jnp.broadcast_to(charge_ref[:, lanes], (beads, BLOCK)) for lanes in spans], axis=0
+            [jnp.broadcast_to(charge_at(block + i), (beads, BLOCK)) for i in range(at_once)], axis=0
         )
         return coords, norm, charge
 
@@ -158,13 +188,13 @@
             for quad in range(beads // QUAD):
                 low = i * beads + quad * QUAD
                 four = jnp.concatenate(
-                    [rows_ref[slot, pl.ds(low + j, PAIR_PAD, stride=lines), :] for j in range(QUAD)], axis=0
+                    [rows_ref[slot, pl.ds(low + j, PAIR_PAD, stride=apart), :] for j in range(QUAD)], axis=0
                 )
                 far_ref[at, quad] = jnp.transpose(four.astype(bf16))
                 for half in range(2):
                     heavy_ref[at, 2 * quad + half] = jnp.concatenate(
                         [
-                            sums_ref[slot, pl.ds(low + 2 * half + j, SUM_ROWS, stride=lines), :]
+                            sums_ref[slot, pl.ds(low + 2 * half + j, SUM_ROWS, stride=apart), :]
                             for j in range(2)
                         ],
                         axis=0,
@@ -180,7 +210,7 @@
             for pair in range(pairs):
                 columns = []
                 for j in range(2):
-                    own = rows_ref[slot, pl.ds(i * beads + 2 * pair + j, PAIR_PAD, stride=lines), :]
+                    own = rows_ref[slot, pl.ds(i * beads + 2 * pair + j, PAIR_PAD, stride=apart), :]
                     spot = 2 * pair % QUAD + j
                     columns.append(
                         jnp.concatenate([own if k == spot else blank for k in range(QUAD)], axis=0)
@@ -194,7 +224,7 @@
         block = unit // pairs
         at_frame = block // frame
         base = at_frame * width + block - at_frame * frame + margin
-        return [base + offset_ref[block * listed + m] for m in range(listed)], unit - block * pairs
+        return [base + offset_at(block, m) for m in range(listed)], unit - block * pairs
 
     def parts(square):
         weight = weigh(square)
@@ -247,7 +277,7 @@
         lanes = pl.ds(pl.multiple_of((block + margin) * BLOCK, BLOCK), BLOCK)
         coords = [(coord_ref[c, :, lanes] - 1.0) * SCALE for c in range(3)]
         coords[0] = coords[0] + SCALE * (place.astype(f32) - middle)
-        charge = jnp.broadcast_to(SCALE * SCALE * charge_ref[:, lanes], coords[0].shape)
+        charge = jnp.broadcast_to(SCALE * SCALE * charge_at(block + margin), coords[0].shape)
 
         def summed(c):
             return sum(total_ref[pl.ds(block * beads * 8 + c + i, beads, stride=8), :] for i in (0, 4))
@@ -268,8 +298,8 @@
     units = blocks * beads // 2
     return [
         pltpu.VMEM((3, beads, (blocks + 2 * margin) * BLOCK), f32),
-        pltpu.VMEM((SLOTS, PAIR_PAD * lines, BLOCK), f32),
-        pltpu.VMEM((SLOTS, SUM_ROWS * lines, BLOCK), f32),
+        pltpu.VMEM((SLOTS, PAIR_PAD * odd_tiles(lines), BLOCK), f32),
+        pltpu.VMEM((SLOTS, SUM_ROWS * odd_tiles(lines), BLOCK), f32),
         pltpu.VMEM((tables, beads // QUAD, BLOCK, QUAD * PAIR_PAD), bf16),
         pltpu.VMEM((tables, beads // 2, 2 * SUM_ROWS, BLOCK), bf16),
         pltpu.VMEM((units, QUAD * PAIR_PAD, 2 * BLOCK), bf16),
@@ -327,41 +357,47 @@
         coord_ref[...] = jnp.zeros(coord_ref.shape, f32)
 
 
-def message_kernel(x_ref, p_ref, types_ref, offsets_ref, message_ref, charge_ref, mass_ref):
-    _, local, edge = message_ref.shape
+def prepare_kernel(
+    blocks, x_ref, edge_ref, noise_ref, types_ref, lists_ref, rest_ref, message_ref, charge_ref, mass_ref
+):
+    steps, _, local, atoms = noise_ref.shape
+    edge = message_ref.shape[2]
     types = types_ref[...]
-    charge = jnp.zeros(types.shape, f32)
+    charge = charges(types)
     mass = jnp.zeros(types.shape, f32)
     for kind in range(4):
-        charge = jnp.where(types == kind, CHARGES[kind], charge)
         mass = jnp.where(types == kind, MASSES[kind], mass)
     charge_ref[...] = charge
     mass_ref[...] = mass
     for c in range(3):
         message_ref[c] = x_ref[c, :, :edge]
         message_ref[3 + c] = x_ref[c, :, edge:2 * edge]
-        message_ref[6 + c] = p_ref[c, :, :edge]
-    for i, row in enumerate([charge[:, :edge], charge[:, edge:2 * edge], mass[:, :edge], offsets_ref[...]]):
+        message_ref[6 + c] = edge_ref[c]
+    for i, row in enumerate([charge[:, :edge], charge[:, edge:2 * edge], mass[:, :edge]]):
         message_ref[9 + i] = jnp.broadcast_to(row, (local, edge))
-
-
-def pack_kernel(blocks, x_ref, noise_ref, out_ref):
-    steps, _, local, atoms = noise_ref.shape
+    message_ref[12] = jnp.zeros((local, edge), f32)
+    for m in range(lists_ref.shape[0]):
+        at = m * (edge // 8)
+        message_ref[12, 0:1, at:at + edge // BLOCK] = lists_ref[m:m + 1, :edge // BLOCK].astype(f32)
     for c in range(3 + 3 * steps):
         for block in range(atoms // BLOCK):
             lanes = slice(block * BLOCK, (block + 1) * BLOCK)
             value = x_ref[c, :, lanes] if c < 3 else noise_ref[c // 3 - 1, c % 3, :, lanes]
             row = row_of(c, block % blocks, blocks, local)
-            out_ref[block // blocks, row:row + local, :] = value
-
-
-def front_kernel(each, margin, listed, offset_ref, charge_ref, x_ref, p_ref, pout_ref, coord_ref, *scratch):
+            rest_ref[block // blocks, row:row + local, :] = value
+
+
+def front_kernel(
+    each, margin, listed, lists_ref, types_ref, x_ref, p_ref, pout_ref, charge_ref, coord_ref, *scratch
+):
     _, local, _ = x_ref.shape
     blocks = pout_ref.shape[0] * each
+    charge_ref[...] = charges(types_ref[...])
     clear(coord_ref, local)
     for c in range(3):
         coord_ref[c, :local, :] = x_ref[c, :, :(blocks + 2 * margin) * BLOCK]
-    add_forces(16, blocks, margin, listed, offset_ref, charge_ref, coord_ref, scratch)
+    offset_at = offsets_of(lists_ref, margin, margin, margin)
+    add_forces(16, blocks, margin, listed, offset_at, charge_ref, coord_ref, scratch)
     force_ref = scratch[FORCE]
     for c in range(3):
         for block in range(blocks):
@@ -372,7 +408,7 @@
 
 
 def back_kernel(
-    each, margin, listed, offset_ref, charge_ref, x_ref, message_ref, p_ref, front_ref, pout_ref, coord_ref, *scratch
+    each, margin, listed, lists_ref, charge_ref, x_ref, message_ref, p_ref, front_ref, pout_ref, coord_ref, *scratch
 ):
     _, local, atoms = x_ref.shape
     edge = margin * BLOCK
@@ -385,7 +421,8 @@
         coord_ref[c, :local, :own] = x_ref[c, :, first * BLOCK:]
         for part in range(2):
             coord_ref[c, :local, own + part * edge:own + (part + 1) * edge] = message_ref[3 * part + c]
-    add_forces(8, blocks, margin, listed, offset_ref, charge_ref, coord_ref, scratch)
+    offset_at = offsets_of(lists_ref, first, first + margin, margin)
+    add_forces(16, blocks, margin, listed, offset_at, charge_ref, coord_ref, scratch, first)
     force_ref = scratch[FORCE]
     pout_ref[:done] = front_ref[...]
     for c in range(3):
@@ -405,7 +442,7 @@
     return ref[block // each, row:row + local, :]
 
 
-def upper_kernel(each, margin, listed, offset_ref, charge_ref, both_ref, pout_ref, coord_ref, *scratch):
+def upper_kernel(each, margin, listed, lists_ref, charge_ref, both_ref, pout_ref, coord_ref, *scratch):
     _, local, atoms = pout_ref.shape
     blocks = atoms // BLOCK
     domain = both_ref.shape[0] * each
@@ -415,7 +452,8 @@
         for block in range(skipped, domain):
             at = (block - skipped) * BLOCK
             coord_ref[c, :local, at:at + BLOCK] = from_packed(both_ref, c, block, each, local)
-    add_forces(16, blocks, margin, listed, offset_ref, charge_ref, coord_ref, scratch)
+    offset_at = offsets_of(lists_ref, domain - blocks, domain - blocks, margin)
+    add_forces(16, blocks, margin, listed, offset_at, charge_ref, coord_ref, scratch, skipped + margin)
     force_ref = scratch[FORCE]
     for c in range(3):
         for block in range(blocks):
@@ -425,7 +463,8 @@
 
 
 def lower_kernel(
-    each, margin, listed, offset_ref, charge_ref, both_ref, message_ref, upper_ref, xout_ref, pout_ref, coord_ref, *scratch
+    each, margin, listed, lists_ref, charge_ref, both_ref, message_ref, upper_ref, xout_ref, pout_ref, coord_ref,
+    *scratch,
 ):
     _, local, atoms = xout_ref.shape
     edge = margin * BLOCK
@@ -443,7 +482,8 @@
             lanes = slice(block * BLOCK, (block + 1) * BLOCK)
             xout_ref[c, :, lanes] = from_packed(both_ref, c, block - margin, each, local)
         pout_ref[c, :, lower:] = upper_ref[c]
-    add_forces(8, blocks, margin, listed, offset_ref, charge_ref, coord_ref, scratch)
+    offset_at = offsets_of(lists_ref, 0, 0, margin)
+    add_forces(16, blocks, margin, listed, offset_at, charge_ref, coord_ref, scratch)
     force_ref = scratch[FORCE]
     for c in range(3):
         for block in range(blocks):
@@ -460,7 +500,8 @@
     cosine, ratio, stiffness, damping, kick = [
         jnp.concatenate([table_ref[i]] * (width // BLOCK), axis=1) for i in range(5)
     ]
-    mass = jnp.broadcast_to(mass_ref[...], (beads, width))
+    first = pl.multiple_of(own_place(mass_ref.shape[1] // width) * width, BLOCK)
+    mass = jnp.broadcast_to(mass_ref[:, pl.ds(first, width)], (beads, width))
     spread = kick * jnp.sqrt(thermal * mass)
     drift = ratio / mass
     stiff = stiffness * mass
@@ -494,7 +535,7 @@
     )
 
 
-def middle_kernel(hops, blocks, listed, noise_base, joined, offset_ref, charge_ref, *refs):
+def middle_kernel(hops, blocks, listed, noise_base, joined, lists_ref, charge_ref, *refs):
     parts = 2 * hops + 1
     x_refs = refs[:parts]
     p_ref, noise_ref, mass_ref, matrix_ref, matrix_t_ref, table_ref = refs[parts:parts + 6]
@@ -505,7 +546,10 @@
     width = blocks * BLOCK
     for part in range(parts):
         unpack_beads(x_refs[part], 0, blocks, local, coord_ref, part * width)
-    add_forces(16, blocks, hops * blocks, listed, offset_ref, charge_ref, coord_ref, scratch)
+    margin = hops * blocks
+    first = own_place(p_ref.shape[0]) * blocks
+    offset_at = offsets_of(lists_ref, first, first + margin, margin)
+    add_forces(16, blocks, margin, listed, offset_at, charge_ref, coord_ref, scratch, first)
     force_ref = scratch[FORCE]
     unpack_beads(p_ref, 0, blocks, local, coord_ref, 0)
     unpack_beads(noise_ref, noise_base, blocks, local, coord_ref, (parts - 1) * width)
@@ -572,57 +616,46 @@
     steps = thermal_noise.shape[0]
     listed = neighbours.shape[1]
     order = fold(count)
-
-    own = lax.axis_index("space") * domain + jnp.arange(domain, dtype=jnp.int32)
-    offsets = jnp.clip(neighbours - own[:, None], -margin, margin).reshape(-1)
-    sent = jnp.pad(offsets[:margin * listed].astype(f32), (0, edge - margin * listed))[None, :]
-
-    (rest,) = call(
-        functools.partial(pack_kernel, blocks), (positions, thermal_noise), 0,
-        [(count, (3 + 3 * steps) * blocks * local, BLOCK)], [], 0,
-    )
+    lists = neighbours.T
+    types = atom_types[None, :]
+
+    packed = (count, 3 * blocks * local, BLOCK)
+    whole = [positions.shape, (3, local, edge), thermal_noise.shape, types.shape, lists.shape]
+    rest, message, charge, mass = call(
+        functools.partial(prepare_kernel, blocks),
+        (positions, momenta, thermal_noise, types, lists), 0,
+        [(count, (1 + steps) * packed[1], BLOCK), (13, local, edge), (1, atoms), (1, atoms)], [], 0,
+        [pl.BlockSpec(shape, lambda i, rank=len(shape): (0,) * rank) for shape in whole],
+    )
+    message = passed(message, -1)
     rest = exchange(rest)
-
-    message, charge, mass = call(
-        message_kernel, (positions, momenta, atom_types[None, :], sent), 0,
-        [(13, local, edge), (1, atoms), (1, atoms)], [], 0,
-        [
-            pl.BlockSpec(shape, lambda i, rank=len(shape): (0,) * rank)
-            for shape in ((3, local, 2 * edge), (3, local, edge), (1, atoms), (1, edge))
-        ],
-    )
-    message = passed(message, -1)
     side = message[9:, 0]
     first_charge = jnp.concatenate([charge, side[:1], side[1:2]], axis=1)
-    moved_mass = jnp.concatenate([mass[0, edge:], side[2]])
-    moved_offsets = jnp.concatenate([offsets[margin * listed:], side[3, :margin * listed].astype(jnp.int32)])
-
-    place = jnp.asarray(np.array(order, np.int32))[lax.axis_index("bead")]
-    near_charge = lax.dynamic_slice_in_dim(first_charge, place * share, share + 2 * edge, axis=1)
-    near_mass = lax.dynamic_slice_in_dim(moved_mass, place * share, share)[None, :]
-    near_offsets = lax.dynamic_slice_in_dim(moved_offsets, place * blocks * listed, blocks * listed)
+    moved_mass = jnp.concatenate([mass[:, edge:], side[2:3]], axis=1)
+    domains = lax.axis_size("space")
+    foreign = side[3].reshape(8, edge // 8)[:listed, :margin].astype(jnp.int32)
+    foreign = foreign + jnp.where(lax.axis_index("space") == domains - 1, domains * domain, 0)
+    moved_lists = jnp.concatenate([lists[:, margin:], foreign], axis=1)
 
     matrix, tables = mode_constants(beads)
     at = np.concatenate([order.index(g) * local + np.arange(local) for g in range(count)])
     matrix = matrix[at][:, at]
-    fixed = (near_mass, jnp.asarray(matrix), jnp.asarray(np.ascontiguousarray(matrix.T)), jnp.asarray(tables[:, at]))
-
-    packed = (count, 3 * blocks * local, BLOCK)
+    fixed = (moved_mass, jnp.asarray(matrix), jnp.asarray(np.ascontiguousarray(matrix.T)), jnp.asarray(tables[:, at]))
+
     pairs = beads * blocks * listed * BLOCK * BLOCK
-    frame = min(FRAME, domain)
-    most = domain - frame
-    window_atoms = (most + 2 * margin) * BLOCK
+    frame = min(FRAME, domain // 2)
+    most = domain - 2 * frame
     (moment,) = call(
-        functools.partial(front_kernel, blocks, margin, listed),
-        (offsets[margin * listed:(margin + most) * listed], charge[:, :window_atoms], positions, momenta), 1,
-        [(most // blocks,) + packed[1:]], force_scratch(local, most, margin, listed), pairs * most // domain,
+        functools.partial(front_kernel, blocks, margin, listed), (lists, types, positions, momenta), 1,
+        [(most // blocks,) + packed[1:]],
+        [pltpu.VMEM(types.shape, f32)] + force_scratch(local, most, margin, listed), pairs * most // domain,
     )
     moment, rest = lax.optimization_barrier((moment, rest))
     rest = round_ring(rest, hops)
     (moment,) = call(
         functools.partial(back_kernel, blocks, margin, listed),
-        (moved_offsets[most * listed:], first_charge[:, most * BLOCK:], positions, message, momenta, moment), 1,
-        [packed], force_scratch(local, frame, margin, listed), pairs * frame // domain,
+        (moved_lists, first_charge, positions, message, momenta, moment), 1,
+        [packed], force_scratch(local, domain - most, margin, listed), pairs * (domain - most) // domain,
     )
     moment, rest = lax.optimization_barrier((moment, rest))
     coords, moment = call(
@@ -633,7 +666,7 @@
         joined = step == steps - 1
         out = call(
             functools.partial(middle_kernel, hops, blocks, listed, 3 * step + 3, joined),
-            (near_offsets, near_charge) + tuple(window(coords, hops)) + (moment, rest) + fixed, 1,
+            (moved_lists, first_charge) + tuple(window(coords, hops)) + (moment, rest) + fixed, 1,
             [(count, 6 * blocks * local, BLOCK)] if joined else [packed] * 2,
             force_scratch(beads, blocks, margin, listed), pairs,
         )
@@ -651,14 +684,14 @@
     ], axis=0), 1)
     (upper,) = call(
         functools.partial(upper_kernel, blocks, margin, listed),
-        (offsets[frame * listed:], first_charge[:, frame * BLOCK - edge:atoms + edge], both), 1,
+        (lists, first_charge, both), 1,
         [(3, local, most * BLOCK)], force_scratch(local, most, margin, listed), pairs * most // domain,
     )
-    last_charge = jnp.concatenate([message[9, :1], first_charge[:, :frame * BLOCK + edge]], axis=1)
+    last_charge = jnp.concatenate([message[9, :1], first_charge[:, :2 * frame * BLOCK + edge]], axis=1)
     return tuple(call(
         functools.partial(lower_kernel, blocks, margin, listed),
-        (offsets[:frame * listed], last_charge, both, message, upper), 1,
-        [(3, local, atoms)] * 2, force_scratch(local, frame, margin, listed), pairs * frame // domain,
+        (lists, last_charge, both, message, upper), 1,
+        [(3, local, atoms)] * 2, force_scratch(local, domain - most, margin, listed), pairs * (domain - most) // domain,
     ))
 
 

time: 129 us -> 121 us (0.938)
  local copies, waits for them, and re-layouts: 5.66 us -> 1.03 us
  Pallas kernels: 75.9 us -> 72.5 us
  starting transfers between devices: 19.9 us -> 21.9 us
  between operations: 2.24 us -> 0.84 us
    pallas_call x8 -> x7, Pallas kernels: 75.9 us -> 72.5 us  [call(): pl.pallas_call(kernel, out_shape=[jax.ShapeDtypeStruct(shape, f32) for sh...]
    ppermute x3, waiting for transfers between devices: 8.06 us -> 4.69 us  [round_ring(): lax.ppermute(values, ('bead', 'space'), [(device[(at + hop) % total], dev...]
    ppermute x3, starting transfers between devices: 3.12 us -> 5.66 us  [round_ring(): lax.ppermute(values, ('bead', 'space'), [(device[(at + hop) % total], dev...]
    unnamed x23 -> x20, local copies, waits for them, and re-layouts: 3.11 us -> 0.74 us
    all_to_all x3, waiting for transfers between devices: 16.4 us -> 18.7 us  [exchange(): lax.all_to_all(pieces, 'bead', split_axis=0, concat_axis=0, axis_index_gr...]
  transfers between devices with their start and end apart: 8 -> 8, of which waited for: 4 -> 3; matrix products, arithmetic and copies ran while one was open for 2% -> 0% of each run, Pallas kernels for 31% -> 28%
where the time goes in v6:
time: 121 us; the launch traced here: 120 us
  Pallas kernels  72.5 us (60%)
  waiting for transfers between devices  23.4 us (19%)
  starting transfers between devices  21.9 us (18%)
    pallas_call x7, Pallas kernels, call(): pl.pallas_call(kernel, out_shape=[jax.ShapeDtypeStruct(shape, f32) for sh...  72.5 us
    all_to_all x3, waiting for transfers between devices, exchange(): lax.all_to_all(pieces, 'bead', split_axis=0, concat_axis=0, axis_index_gr...  18.7 us
    all_to_all x3, starting transfers between devices, exchange(): lax.all_to_all(pieces, 'bead', split_axis=0, concat_axis=0, axis_index_gr...  13.4 us
    ppermute x3, starting transfers between devices, round_ring(): lax.ppermute(values, ('bead', 'space'), [(device[(at + hop) % total], dev...  5.66 us
    ppermute x3, waiting for transfers between devices, round_ring(): lax.ppermute(values, ('bead', 'space'), [(device[(at + hop) % total], dev...  4.69 us
    ppermute x2, starting transfers between devices, passed(): lax.ppermute(values, 'space', [(i, (i + step) % count) for i in range(cou...  2.79 us
  transfers between devices with their start and end apart: 8, of which 3 were waited for; matrix products, arithmetic and copies ran while one was open for 0% of the time, Pallas kernels for 28%

profile of v6, /device:TPU:0, one launch (start us, length us, event | category | flops | bytes accessed | tf_op | source)
XLA Modules:
  0.0 119.9 jit_solution(7171141567111123569)
XLA Ops:
  0.6 2.0 %shard_map.95 = (f32[8,144,128]{2,1,0:T(8,128)}, f32[13,4,512]{2,1,0:T(4,128)}, f32[1,4096]{1,0:T(1,128)}, f32[1,4096]{1,0:T(1,128)}) custom-call(f32[3,4,4096]{2,1,0:T(4,128)} %x_ref.5, f32[3,4,4096]{2,1,0:T(4,128)} %p_ref.3, f32[2,3,4,4096]{3,2,1,0:T(4,128)} %noise_ref.1, s32[1,4096]{1,0:T(1,128)} %bitcast.34, s32[5,32]{1,0:T(8,128)} %bitcast.29), custom_call_target="tpu_custom_call" | custom-call | flops 1024 | bytes 4194304 | tf_op jit(solution)/shard_map/pallas_call | solution.py:316
  2.7 0.0 copy-start.9
  2.7 0.0 copy-start.5
  2.7 0.0 copy-start
  2.7 0.0 copy-start.1
  2.7 6.5 %all-to-all-start = ((f32[8,144,128]{2,1,0:T(8,128)}), f32[8,144,128]{2,1,0:T(8,128)S(1)}, u32[]{:S(2)}, u32[]{:S(2)}) async-start(f32[8,144,128]{2,1,0:T(8,128)} %get-tuple-element.14), calls=%async_computation | async-start | bytes 1179648 | tf_op jit(solution)/shard_map/all_to_all | solution.py:582
  9.1 0.0 copy-start.8
  9.2 0.0 copy-done.9
  9.2 2.5 %collective-permute-start = (f32[13,4,512]{2,1,0:T(4,128)S(1)}, f32[13,4,512]{2,1,0:T(4,128)S(1)}, u32[]{:S(2)}, u32[]{:S(2)}) collective-permute-start(f32[13,4,512]{2,1,0:T(4,128)S(1)} %copy-done.9), channel_id=1, source_target_pairs={{0,3},{1,0},{2,1},{3,2},{4,7},{5,4},{6,5},{7,6},{8,11},{9,8},{10,9... | collective-permute-start | bytes 319496 | tf_op jit(solution)/shard_map/ppermute | solution.py:587
  11.7 0.0 copy-done.5
  11.7 0.1 slice.54
  11.7 0.0 copy-done.8
  11.7 0.0 copy-start.6
  11.7 0.0 copy-done
  11.7 0.0 copy-done.1
  11.8 0.7 copy-done.6
  12.5 11.1 %shard_map.96.front_ref = f32[4,48,128]{2,1,0:T(8,128)S(1)} custom-call(s32[5,32]{1,0:T(8,128)S(1)} %bitcast.31, s32[1,4096]{1,0:T(1,128)S(1)} %bitcast.35, f32[3,4,4096]{2,1,0:T(4,128)S(1)} %copy-done, f32[3,4,4096]{2,1,0:T(4,128)S(1)} %copy-done.1), custom_call_target="tpu_custom_call" | custom-call | flops 104858624 | bytes 4194304 | tf_op jit(solution)/shard_map/pallas_call | solution.py:316
  23.6 0.0 collective-permute-done.message_ref
  23.6 0.0 copy-start.7
  23.6 0.1 reshape_squeeze.3
  23.7 0.0 all-to-all-done
  23.7 3.0 %collective-permute-start.1 = (f32[8,144,128]{2,1,0:T(8,128)S(1)}, f32[8,144,128]{2,1,0:T(8,128)S(1)}, u32[]{:S(2)}, u32[]{:S(2)}) collective-permute-start(f32[8,144,128]{2,1,0:T(8,128)S(1)} %all-to-all-done), channel_id=1, source_target_pairs={{8,0},{16,8},{24,16},{28,24},{20,28},{12,20},{4,12},{1,4},{9,1},{1... | collective-permute-start | bytes 1769480 | tf_op jit(solution)/shard_map/ppermute | solution.py:599
  26.7 0.1 pad_add_fusion.lists_ref
  26.8 0.0 copy-done.7
  26.8 11.8 %shard_map.97 = f32[8,48,128]{2,1,0:T(8,128)} custom-call(s32[5,32]{1,0:T(8,128)S(1)} %pad_add_fusion.lists_ref, f32[1,5120]{1,0:T(1,128)S(1)} %pad_maximum_fusion.1.charge_ref, f32[3,4,4096]{2,1,0:T(4,128)S(1)} %copy-done, f32[13,4,512]{2,1,0:T(4,128)S(1)} %collective-permute-done.message_ref, f32[3,4,4096]{2,1,0:T(4,128)S(1)} %copy-done.1, ...), custom_call_target="tpu_custom_call" | custom-call | flops 104858624 | bytes 4194304 | tf_op jit(solution)/shard_map/pallas_call | solution.py:316
  38.6 0.0 collective-permute-done.1.rest_ref.refs_4_
  38.6 0.0 copy-start.2
  38.6 3.5 %all-to-all-start.1 = ((f32[8,48,128]{2,1,0:T(8,128)}), f32[8,48,128]{2,1,0:T(8,128)S(1)}, u32[]{:S(2)}, u32[]{:S(2)}) async-start(f32[8,48,128]{2,1,0:T(8,128)} %shard_map.97), calls=%async_computation.1 | async-start | bytes 393216 | tf_op jit(solution)/shard_map/all_to_all | solution.py:582
  42.1 0.0 copy-start.3
  42.1 0.0 copy-start.4
  42.2 7.8 %all-to-all-done.1.p_ref = f32[8,48,128]{2,1,0:T(8,128)S(1)} async-done(((f32[8,48,128]{2,1,0:T(8,128)}), f32[8,48,128]{2,1,0:T(8,128)S(1)}, u32[]{:S(2)}, u32[]{:S(2)}) %all-to-all-start.1) | async-done | bytes 196640 | tf_op jit(solution)/shard_map/all_to_all | solution.py:582
  50.0 0.0 copy-done.2
  50.0 0.0 copy-done.3
  50.0 0.0 copy-done.4
  50.0 1.2 %shard_map.98 = (f32[8,48,128]{2,1,0:T(8,128)S(1)}, f32[8,48,128]{2,1,0:T(8,128)S(1)}) custom-call(f32[8,144,128]{2,1,0:T(8,128)S(1)} %collective-permute-done.1.rest_ref.refs_4_, f32[8,48,128]{2,1,0:T(8,128)S(1)} %all-to-all-done.1.p_ref, f32[1,4096]{1,0:T(1,128)S(1)} %pad_maximum_fusion.2.mass_ref.refs_5_, f32[32,32]{1,0:T(8,128)S(1)} %copy-done.3, ...), custom_call_target="tpu_custom_call" | custom-call | flops 1024 | bytes 4194304 | tf_op jit(solution)/shard_map/pallas_call | solution.py:316
  51.3 0.1 collective-permute-start.2
  51.3 2.6 %collective-permute-start.3 = (f32[8,48,128]{2,1,0:T(8,128)S(1)}, f32[8,48,128]{2,1,0:T(8,128)S(1)}, u32[]{:S(2)}, u32[]{:S(2)}) collective-permute-start(f32[8,48,128]{2,1,0:T(8,128)S(1)} %get-tuple-element.20.refs_1_), channel_id=1, source_target_pairs={{8,0},{16,8},{24,16},{28,24},{20,28},{12,20},{4,12},{1,4},{9,1},{1... | collective-permute-start | bytes 589832 | tf_op jit(solution)/shard_map/ppermute | solution.py:599
  54.0 4.7 %collective-permute-done.2.refs_0_ = f32[8,48,128]{2,1,0:T(8,128)S(1)} collective-permute-done((f32[8,48,128]{2,1,0:T(8,128)S(1)}, f32[8,48,128]{2,1,0:T(8,128)S(1)}, u32[]{:S(2)}, u32[]{:S(2)}) %collective-permute-start.2) | collective-permute-done | bytes 196640 | tf_op jit(solution)/shard_map/ppermute | solution.py:599
  58.6 0.0 collective-permute-done.3.refs_2_
  58.6 23.3 %shard_map.99 = f32[8,96,128]{2,1,0:T(8,128)} custom-call(s32[5,32]{1,0:T(8,128)S(1)} %pad_add_fusion.lists_ref, f32[1,5120]{1,0:T(1,128)S(1)} %pad_maximum_fusion.1.charge_ref, f32[8,48,128]{2,1,0:T(8,128)S(1)} %collective-permute-done.2.refs_0_, f32[8,48,128]{2,1,0:T(8,128)S(1)} %get-tuple-element.20.refs_1_, ...), custom_call_target="tpu_custom_call" | custom-call | flops 209716224 | bytes 4194304 | tf_op jit(solution)/shard_map/pallas_call | solution.py:316
  82.0 3.5 %all-to-all-start.2 = ((f32[8,96,128]{2,1,0:T(8,128)}), f32[8,96,128]{2,1,0:T(8,128)S(1)}, u32[]{:S(2)}, u32[]{:S(2)}) async-start(f32[8,96,128]{2,1,0:T(8,128)} %shard_map.99), calls=%async_computation.2 | async-start | bytes 786432 | tf_op jit(solution)/shard_map/all_to_all | solution.py:582
  85.4 10.9 %all-to-all-done.2.both_ref = f32[8,96,128]{2,1,0:T(8,128)S(1)} async-done(((f32[8,96,128]{2,1,0:T(8,128)}), f32[8,96,128]{2,1,0:T(8,128)S(1)}, u32[]{:S(2)}, u32[]{:S(2)}) %all-to-all-start.2) | async-done | bytes 393248 | tf_op jit(solution)/shard_map/all_to_all | solution.py:582
  96.5 0.3 collective-permute-start.4
  96.8 11.1 %shard_map.100.upper_ref = f32[3,4,2048]{2,1,0:T(4,128)S(1)} custom-call(s32[5,32]{1,0:T(8,128)S(1)} %bitcast.32, f32[1,5120]{1,0:T(1,128)S(1)} %pad_maximum_fusion.1.charge_ref, f32[8,96,128]{2,1,0:T(8,128)S(1)} %all-to-all-done.2.both_ref), custom_call_target="tpu_custom_call" | custom-call | flops 104858624 | bytes 4194304 | tf_op jit(solution)/shard_map/pallas_call | solution.py:316
  108.0 0.0 collective-permute-done.4.message_ref
  108.0 11.9 %shard_map.101 = (f32[3,4,4096]{2,1,0:T(4,128)}, f32[3,4,4096]{2,1,0:T(4,128)}) custom-call(s32[5,32]{1,0:T(8,128)S(1)} %bitcast.33, f32[1,3072]{1,0:T(1,128)S(1)} %pad_maximum_fusion.3.charge_ref, f32[8,96,128]{2,1,0:T(8,128)S(1)} %all-to-all-done.2.both_ref, f32[10,4,512]{2,1,0:T(4,128)S(1)} %collective-permute-done.4.message_ref, ...), custom_call_target="tpu_custom_call" | custom-call | flops 104858624 | bytes 4194304 | tf_op jit(solution)/shard_map/pallas_call | solution.py:316
  (18 shorter events, 0.2 us)
Async XLA Ops:
  2.7 6.5 %copy-start.9 = (f32[13,4,512]{2,1,0:T(4,128)S(1)}, f32[13,4,512]{2,1,0:T(4,128)}, u32[]{:S(2)}) copy-start(f32[13,4,512]{2,1,0:T(4,128)} %get-tuple-element.12) | copy-start | bytes 319492
  2.7 9.0 %copy-start.5 = (s32[32,5]{0,1:T(8,128)S(1)}, s32[32,5]{0,1:T(8,128)}, u32[]{:S(2)}) copy-start(s32[32,5]{0,1:T(8,128)} %param.11) | copy-start | bytes 1924
  2.7 9.1 %copy-start = (f32[3,4,4096]{2,1,0:T(4,128)S(1)}, f32[3,4,4096]{2,1,0:T(4,128)}, u32[]{:S(2)}) copy-start(f32[3,4,4096]{2,1,0:T(4,128)} %x_ref.5) | copy-start | bytes 589828
  2.7 9.1 %copy-start.1 = (f32[3,4,4096]{2,1,0:T(4,128)S(1)}, f32[3,4,4096]{2,1,0:T(4,128)}, u32[]{:S(2)}) copy-start(f32[3,4,4096]{2,1,0:T(4,128)} %p_ref.3) | copy-start | bytes 589828
  2.7 21.0 %all-to-all-start = ((f32[8,144,128]{2,1,0:T(8,128)}), f32[8,144,128]{2,1,0:T(8,128)S(1)}, u32[]{:S(2)}, u32[]{:S(2)}) async-start(f32[8,144,128]{2,1,0:T(8,128)} %get-tuple-element.14), calls=%async_computation | async-start | bytes 1179648 | tf_op jit(solution)/shard_map/all_to_all | solution.py:582
  9.1 2.6 %copy-start.8 = (f32[1,4096]{1,0:T(1,128)S(1)}, f32[1,4096]{1,0:T(1,128)}, u32[]{:S(2)}) copy-start(f32[1,4096]{1,0:T(1,128)} %get-tuple-element.19) | copy-start | bytes 49156
  9.2 14.4 %collective-permute-start = (f32[13,4,512]{2,1,0:T(4,128)S(1)}, f32[13,4,512]{2,1,0:T(4,128)S(1)}, u32[]{:S(2)}, u32[]{:S(2)}) collective-permute-start(f32[13,4,512]{2,1,0:T(4,128)S(1)} %copy-done.9), channel_id=1, source_target_pairs={{0,3},{1,0},{2,1},{3,2},{4,7},{5,4},{6,5},{7,6},{8,11},{9,8},{10,9... | collective-permute-start | bytes 319496 | tf_op jit(solution)/shard_map/ppermute | solution.py:587
  11.7 0.7 copy-start.6
  23.6 3.1 %copy-start.7 = (f32[1,4096]{1,0:T(1,128)S(1)}, f32[1,4096]{1,0:T(1,128)}, u32[]{:S(2)}) copy-start(f32[1,4096]{1,0:T(1,128)} %get-tuple-element.13) | copy-start | bytes 49156
  23.7 14.9 %collective-permute-start.1 = (f32[8,144,128]{2,1,0:T(8,128)S(1)}, f32[8,144,128]{2,1,0:T(8,128)S(1)}, u32[]{:S(2)}, u32[]{:S(2)}) collective-permute-start(f32[8,144,128]{2,1,0:T(8,128)S(1)} %all-to-all-done), channel_id=1, source_target_pairs={{8,0},{16,8},{24,16},{28,24},{20,28},{12,20},{4,12},{1,4},{9,1},{1... | collective-permute-start | bytes 1769480 | tf_op jit(solution)/shard_map/ppermute | solution.py:599
  38.6 11.4 %copy-start.2 = (f32[5,32,128]{2,1,0:T(8,128)S(1)}, f32[5,32,128]{2,1,0:T(8,128)}, u32[]{:S(2)}) copy-start(f32[5,32,128]{2,1,0:T(8,128)} %constant.18.clone.table_ref.refs_8_) | copy-start | bytes 245764
  38.6 11.4 %all-to-all-start.1 = ((f32[8,48,128]{2,1,0:T(8,128)}), f32[8,48,128]{2,1,0:T(8,128)S(1)}, u32[]{:S(2)}, u32[]{:S(2)}) async-start(f32[8,48,128]{2,1,0:T(8,128)} %shard_map.97), calls=%async_computation.1 | async-start | bytes 393216 | tf_op jit(solution)/shard_map/all_to_all | solution.py:582
  42.1 7.9 %copy-start.3 = (f32[32,32]{1,0:T(8,128)S(1)}, f32[32,32]{1,0:T(8,128)}, u32[]{:S(2)}) copy-start(f32[32,32]{1,0:T(8,128)} %constant.16.clone.matrix_ref.refs_6_) | copy-start | bytes 12292
  42.1 7.9 %copy-start.4 = (f32[32,32]{1,0:T(8,128)S(1)}, f32[32,32]{1,0:T(8,128)}, u32[]{:S(2)}) copy-start(f32[32,32]{1,0:T(8,128)} %constant.17.clone.matrix_t_ref.refs_7_) | copy-start | bytes 12292
  51.3 7.4 %collective-permute-start.2 = (f32[8,48,128]{2,1,0:T(8,128)S(1)}, f32[8,48,128]{2,1,0:T(8,128)S(1)}, u32[]{:S(2)}, u32[]{:S(2)}) collective-permute-start(f32[8,48,128]{2,1,0:T(8,128)S(1)} %get-tuple-element.20.refs_1_), channel_id=1, source_target_pairs={{7,0},{0,8},{8,16},{16,24},{24,28},{28,20},{20,12},{12,4},{4,1},{1... | collective-permute-start | bytes 589832 | tf_op jit(solution)/shard_map/ppermute | solution.py:599
  51.3 7.3 %collective-permute-start.3 = (f32[8,48,128]{2,1,0:T(8,128)S(1)}, f32[8,48,128]{2,1,0:T(8,128)S(1)}, u32[]{:S(2)}, u32[]{:S(2)}) collective-permute-start(f32[8,48,128]{2,1,0:T(8,128)S(1)} %get-tuple-element.20.refs_1_), channel_id=1, source_target_pairs={{8,0},{16,8},{24,16},{28,24},{20,28},{12,20},{4,12},{1,4},{9,1},{1... | collective-permute-start | bytes 589832 | tf_op jit(solution)/shard_map/ppermute | solution.py:599
  82.0 14.4 %all-to-all-start.2 = ((f32[8,96,128]{2,1,0:T(8,128)}), f32[8,96,128]{2,1,0:T(8,128)S(1)}, u32[]{:S(2)}, u32[]{:S(2)}) async-start(f32[8,96,128]{2,1,0:T(8,128)} %shard_map.99), calls=%async_computation.2 | async-start | bytes 786432 | tf_op jit(solution)/shard_map/all_to_all | solution.py:582
  96.5 11.4 %collective-permute-start.4 = (f32[10,4,512]{2,1,0:T(4,128)S(1)}, f32[10,4,512]{2,1,0:T(4,128)S(1)}, u32[]{:S(2)}, u32[]{:S(2)}) collective-permute-start(f32[10,4,512]{2,1,0:T(4,128)S(1)} %pad_maximum_fusion), channel_id=1, source_target_pairs={{0,1},{1,2},{2,3},{3,0},{4,5},{5,6},{6,7},{7,4},{8,9},{9,10},{10,1... | collective-permute-start | bytes 245768 | tf_op jit(solution)/shard_map/ppermute | solution.py:587

commit v7 on v6

--- a/solution.py
+++ b/solution.py
@@ -26,8 +26,8 @@
 PAIR_PAD = 32
 SUM_ROWS = 16
 QUAD = 4
-SLOTS = 4
-FRAME = 8
+SLOTS = 8
+FRAME = 16
 f32 = jnp.float32
 bf16 = jnp.bfloat16
 
@@ -156,7 +156,7 @@
         return coords, norm, charge
 
     def steps(count, one):
-        slots = math.gcd(count, SLOTS)
+        slots = max(n for n in range(1, SLOTS + 1) if count % n == 0)
 
         def some(turn, carry):
             for slot in range(slots):
@@ -171,7 +171,7 @@
             put(rows_ref, slot, k, nothing)
         for k in range(12, SUM_ROWS):
             put(sums_ref, slot, k, nothing)
-    blank = jnp.zeros((PAIR_PAD, BLOCK), f32)
+    blank = jnp.zeros((PAIR_PAD, BLOCK), bf16)
     passes = width // at_once
 
     def one_table(step, slot):
@@ -207,15 +207,10 @@
         for k, row in enumerate(pair_rows(coords, norm + softening * SCALE * SCALE, True)):
             put(rows_ref, slot, k, row)
         for i in range(at_once):
-            for pair in range(pairs):
-                columns = []
-                for j in range(2):
-                    own = rows_ref[slot, pl.ds(i * beads + 2 * pair + j, PAIR_PAD, stride=apart), :]
-                    spot = 2 * pair % QUAD + j
-                    columns.append(
-                        jnp.concatenate([own if k == spot else blank for k in range(QUAD)], axis=0)
-                    )
-                near_ref[(block + i) * pairs + pair] = jnp.concatenate(columns, axis=1).astype(bf16)
+            for bead in range(beads):
+                near_ref[(block + i) * beads + bead] = rows_ref[
+                    slot, pl.ds(i * beads + bead, PAIR_PAD, stride=apart), :
+                ].astype(bf16)
 
     steps(blocks // frame * passes, one_table)
     steps(blocks // at_once, one_own)
@@ -231,8 +226,15 @@
         high = weight.astype(bf16)
         return high, (weight - high.astype(f32)).astype(bf16)
 
-    def squares(ats, pair, unit, m):
-        return jnp.dot(far_ref[ats[m], pair // (QUAD // 2)], near_ref[unit], preferred_element_type=f32)
+    def squares(ats, pair, near, m):
+        return jnp.dot(far_ref[ats[m], pair // (QUAD // 2)], near, preferred_element_type=f32)
+
+    def own_columns(unit, half):
+        columns = [
+            jnp.concatenate([near_ref[2 * unit + j] if k == 2 * half + j else blank for k in range(QUAD)], axis=0)
+            for j in range(2)
+        ]
+        return jnp.concatenate(columns, axis=1)
 
     def weighted(at, pair, both):
         table = heavy_ref[at, pair]
@@ -251,10 +253,11 @@
             unit = step * group + turn
             now, other = turn % 2, (turn + 1) % 2
             ats, pair = places(unit)
+            near = own_columns(unit, turn % 2)
             total = jnp.zeros((2 * SUM_ROWS, 2 * BLOCK), f32)
             for m in range(listed):
                 spot = slice(2 * m * BLOCK, 2 * (m + 1) * BLOCK)
-                weight_refs[now][spot, :] = jnp.concatenate(parts(squares(ats, pair, unit, m)), axis=0)
+                weight_refs[now][spot, :] = jnp.concatenate(parts(squares(ats, pair, near, m)), axis=0)
                 total = total + weighted(before_ats[m], before_pair, weight_refs[other][spot, :])
             keep(total, jnp.where(unit == 0, units, unit - 1))
             before_ats, before_pair = ats, pair
@@ -302,7 +305,7 @@
         pltpu.VMEM((SLOTS, SUM_ROWS * odd_tiles(lines), BLOCK), f32),
         pltpu.VMEM((tables, beads // QUAD, BLOCK, QUAD * PAIR_PAD), bf16),
         pltpu.VMEM((tables, beads // 2, 2 * SUM_ROWS, BLOCK), bf16),
-        pltpu.VMEM((units, QUAD * PAIR_PAD, 2 * BLOCK), bf16),
+        pltpu.VMEM((2 * units, PAIR_PAD, BLOCK), bf16),
         pltpu.VMEM(((units + 1) * 16, BLOCK), f32),
         pltpu.VMEM((3, beads, blocks * BLOCK), f32),
         pltpu.VMEM((2 * listed * BLOCK, 2 * BLOCK), bf16),
@@ -643,8 +646,8 @@
     fixed = (moved_mass, jnp.asarray(matrix), jnp.asarray(np.ascontiguousarray(matrix.T)), jnp.asarray(tables[:, at]))
 
     pairs = beads * blocks * listed * BLOCK * BLOCK
-    frame = min(FRAME, domain // 2)
-    most = domain - 2 * frame
+    half = domain // 2
+    most = domain - half
     (moment,) = call(
         functools.partial(front_kernel, blocks, margin, listed), (lists, types, positions, momenta), 1,
         [(most // blocks,) + packed[1:]],
@@ -687,7 +690,7 @@
         (lists, first_charge, both), 1,
         [(3, local, most * BLOCK)], force_scratch(local, most, margin, listed), pairs * most // domain,
     )
-    last_charge = jnp.concatenate([message[9, :1], first_charge[:, :2 * frame * BLOCK + edge]], axis=1)
+    last_charge = jnp.concatenate([message[9, :1], first_charge[:, :half * BLOCK + edge]], axis=1)
     return tuple(call(
         functools.partial(lower_kernel, blocks, margin, listed),
         (lists, last_charge, both, message, upper), 1,

time: 121 us -> 119 us (0.983)
  Pallas kernels: 72.5 us -> 70.3 us
    pallas_call x7, Pallas kernels: 72.5 us -> 70.3 us  [call(): pl.pallas_call(kernel, out_shape=[jax.ShapeDtypeStruct(shape, f32) for sh...]
  transfers between devices with their start and end apart: 8 -> 8, of which waited for: 3 -> 4; matrix products, arithmetic and copies ran while one was open for 0% -> 0% of each run, Pallas kernels for 28% -> 28%
where the time goes in v7:
time: 119 us; the launch traced here: 118 us
  Pallas kernels  70.3 us (59%)
  waiting for transfers between devices  23.3 us (20%)
  starting transfers between devices  22.5 us (19%)
    pallas_call x7, Pallas kernels, call(): pl.pallas_call(kernel, out_shape=[jax.ShapeDtypeStruct(shape, f32) for sh...  70.3 us
    all_to_all x3, waiting for transfers between devices, exchange(): lax.all_to_all(pieces, 'bead', split_axis=0, concat_axis=0, axis_index_gr...  18.6 us
    all_to_all x3, starting transfers between devices, exchange(): lax.all_to_all(pieces, 'bead', split_axis=0, concat_axis=0, axis_index_gr...  13.6 us
    ppermute x3, starting transfers between devices, round_ring(): lax.ppermute(values, ('bead', 'space'), [(device[(at + hop) % total], dev...  6.05 us
    ppermute x3, waiting for transfers between devices, round_ring(): lax.ppermute(values, ('bead', 'space'), [(device[(at + hop) % total], dev...  4.7 us
    ppermute x2, starting transfers between devices, passed(): lax.ppermute(values, 'space', [(i, (i + step) % count) for i in range(cou...  2.78 us
  transfers between devices with their start and end apart: 8, of which 4 were waited for; matrix products, arithmetic and copies ran while one was open for 0% of the time, Pallas kernels for 28%

profile of v7, /device:TPU:0, one launch (start us, length us, event | category | flops | bytes accessed | tf_op | source)
XLA Modules:
  0.0 118.1 jit_solution(2108093270500359188)
XLA Ops:
  0.6 2.0 %shard_map.95 = (f32[8,144,128]{2,1,0:T(8,128)}, f32[13,4,512]{2,1,0:T(4,128)}, f32[1,4096]{1,0:T(1,128)}, f32[1,4096]{1,0:T(1,128)}) custom-call(f32[3,4,4096]{2,1,0:T(4,128)} %x_ref.5, f32[3,4,4096]{2,1,0:T(4,128)} %p_ref.3, f32[2,3,4,4096]{3,2,1,0:T(4,128)} %noise_ref.1, s32[1,4096]{1,0:T(1,128)} %bitcast.34, s32[5,32]{1,0:T(8,128)} %bitcast.29), custom_call_target="tpu_custom_call" | custom-call | flops 1024 | bytes 4194304 | tf_op jit(solution)/shard_map/pallas_call | solution.py:319
  2.7 0.0 copy-start.9
  2.7 0.0 copy-start.5
  2.7 0.0 copy-start
  2.7 0.0 copy-start.1
  2.7 6.5 %all-to-all-start = ((f32[8,144,128]{2,1,0:T(8,128)}), f32[8,144,128]{2,1,0:T(8,128)S(1)}, u32[]{:S(2)}, u32[]{:S(2)}) async-start(f32[8,144,128]{2,1,0:T(8,128)} %get-tuple-element.14), calls=%async_computation | async-start | bytes 1179648 | tf_op jit(solution)/shard_map/all_to_all | solution.py:585
  9.1 0.0 copy-start.8
  9.2 0.0 copy-done.9
  9.2 2.5 %collective-permute-start = (f32[13,4,512]{2,1,0:T(4,128)S(1)}, f32[13,4,512]{2,1,0:T(4,128)S(1)}, u32[]{:S(2)}, u32[]{:S(2)}) collective-permute-start(f32[13,4,512]{2,1,0:T(4,128)S(1)} %copy-done.9), channel_id=1, source_target_pairs={{0,3},{1,0},{2,1},{3,2},{4,7},{5,4},{6,5},{7,6},{8,11},{9,8},{10,9... | collective-permute-start | bytes 319496 | tf_op jit(solution)/shard_map/ppermute | solution.py:590
  11.7 0.0 copy-done.5
  11.7 0.1 slice.54
  11.7 0.0 copy-done.8
  11.7 0.0 copy-start.6
  11.7 0.0 copy-done
  11.7 0.0 copy-done.1
  11.8 0.7 copy-done.6
  12.5 10.7 %shard_map.96.front_ref = f32[4,48,128]{2,1,0:T(8,128)S(1)} custom-call(s32[5,32]{1,0:T(8,128)S(1)} %bitcast.31, s32[1,4096]{1,0:T(1,128)S(1)} %bitcast.35, f32[3,4,4096]{2,1,0:T(4,128)S(1)} %copy-done, f32[3,4,4096]{2,1,0:T(4,128)S(1)} %copy-done.1), custom_call_target="tpu_custom_call" | custom-call | flops 104858624 | bytes 4194304 | tf_op jit(solution)/shard_map/pallas_call | solution.py:319
  23.1 0.0 collective-permute-done.message_ref
  23.2 0.0 copy-start.7
  23.2 0.1 reshape_squeeze.3
  23.3 0.1 all-to-all-done
  23.3 3.4 %collective-permute-start.1 = (f32[8,144,128]{2,1,0:T(8,128)S(1)}, f32[8,144,128]{2,1,0:T(8,128)S(1)}, u32[]{:S(2)}, u32[]{:S(2)}) collective-permute-start(f32[8,144,128]{2,1,0:T(8,128)S(1)} %all-to-all-done), channel_id=1, source_target_pairs={{8,0},{16,8},{24,16},{28,24},{20,28},{12,20},{4,12},{1,4},{9,1},{1... | collective-permute-start | bytes 1769480 | tf_op jit(solution)/shard_map/ppermute | solution.py:602
  26.7 0.1 pad_add_fusion.lists_ref
  26.8 0.0 copy-done.7
  26.8 11.3 %shard_map.97 = f32[8,48,128]{2,1,0:T(8,128)} custom-call(s32[5,32]{1,0:T(8,128)S(1)} %pad_add_fusion.lists_ref, f32[1,5120]{1,0:T(1,128)S(1)} %pad_maximum_fusion.1.charge_ref, f32[3,4,4096]{2,1,0:T(4,128)S(1)} %copy-done, f32[13,4,512]{2,1,0:T(4,128)S(1)} %collective-permute-done.message_ref, f32[3,4,4096]{2,1,0:T(4,128)S(1)} %copy-done.1, ...), custom_call_target="tpu_custom_call" | custom-call | flops 104858624 | bytes 4194304 | tf_op jit(solution)/shard_map/pallas_call | solution.py:319
  38.1 0.0 collective-permute-done.1.rest_ref.refs_4_
  38.1 0.0 copy-start.2
  38.1 3.7 %all-to-all-start.1 = ((f32[8,48,128]{2,1,0:T(8,128)}), f32[8,48,128]{2,1,0:T(8,128)S(1)}, u32[]{:S(2)}, u32[]{:S(2)}) async-start(f32[8,48,128]{2,1,0:T(8,128)} %shard_map.97), calls=%async_computation.1 | async-start | bytes 393216 | tf_op jit(solution)/shard_map/all_to_all | solution.py:585
  41.8 0.0 copy-start.3
  41.9 0.0 copy-start.4
  41.9 7.6 %all-to-all-done.1.p_ref = f32[8,48,128]{2,1,0:T(8,128)S(1)} async-done(((f32[8,48,128]{2,1,0:T(8,128)}), f32[8,48,128]{2,1,0:T(8,128)S(1)}, u32[]{:S(2)}, u32[]{:S(2)}) %all-to-all-start.1) | async-done | bytes 196640 | tf_op jit(solution)/shard_map/all_to_all | solution.py:585
  49.5 0.0 copy-done.2
  49.5 0.0 copy-done.3
  49.5 0.0 copy-done.4
  49.5 1.2 %shard_map.98 = (f32[8,48,128]{2,1,0:T(8,128)S(1)}, f32[8,48,128]{2,1,0:T(8,128)S(1)}) custom-call(f32[8,144,128]{2,1,0:T(8,128)S(1)} %collective-permute-done.1.rest_ref.refs_4_, f32[8,48,128]{2,1,0:T(8,128)S(1)} %all-to-all-done.1.p_ref, f32[1,4096]{1,0:T(1,128)S(1)} %pad_maximum_fusion.2.mass_ref.refs_5_, f32[32,32]{1,0:T(8,128)S(1)} %copy-done.3, ...), custom_call_target="tpu_custom_call" | custom-call | flops 1024 | bytes 4194304 | tf_op jit(solution)/shard_map/pallas_call | solution.py:319
  50.8 0.1 collective-permute-start.2
  50.9 2.6 %collective-permute-start.3 = (f32[8,48,128]{2,1,0:T(8,128)S(1)}, f32[8,48,128]{2,1,0:T(8,128)S(1)}, u32[]{:S(2)}, u32[]{:S(2)}) collective-permute-start(f32[8,48,128]{2,1,0:T(8,128)S(1)} %get-tuple-element.20.refs_1_), channel_id=1, source_target_pairs={{8,0},{16,8},{24,16},{28,24},{20,28},{12,20},{4,12},{1,4},{9,1},{1... | collective-permute-start | bytes 589832 | tf_op jit(solution)/shard_map/ppermute | solution.py:602
  53.5 4.7 %collective-permute-done.2.refs_0_ = f32[8,48,128]{2,1,0:T(8,128)S(1)} collective-permute-done((f32[8,48,128]{2,1,0:T(8,128)S(1)}, f32[8,48,128]{2,1,0:T(8,128)S(1)}, u32[]{:S(2)}, u32[]{:S(2)}) %collective-permute-start.2) | collective-permute-done | bytes 196640 | tf_op jit(solution)/shard_map/ppermute | solution.py:602
  58.2 0.0 collective-permute-done.3.refs_2_
  58.2 22.9 %shard_map.99 = f32[8,96,128]{2,1,0:T(8,128)} custom-call(s32[5,32]{1,0:T(8,128)S(1)} %pad_add_fusion.lists_ref, f32[1,5120]{1,0:T(1,128)S(1)} %pad_maximum_fusion.1.charge_ref, f32[8,48,128]{2,1,0:T(8,128)S(1)} %collective-permute-done.2.refs_0_, f32[8,48,128]{2,1,0:T(8,128)S(1)} %get-tuple-element.20.refs_1_, ...), custom_call_target="tpu_custom_call" | custom-call | flops 209716224 | bytes 4194304 | tf_op jit(solution)/shard_map/pallas_call | solution.py:319
  81.1 3.5 %all-to-all-start.2 = ((f32[8,96,128]{2,1,0:T(8,128)}), f32[8,96,128]{2,1,0:T(8,128)S(1)}, u32[]{:S(2)}, u32[]{:S(2)}) async-start(f32[8,96,128]{2,1,0:T(8,128)} %shard_map.99), calls=%async_computation.2 | async-start | bytes 786432 | tf_op jit(solution)/shard_map/all_to_all | solution.py:585
  84.6 10.9 %all-to-all-done.2.both_ref = f32[8,96,128]{2,1,0:T(8,128)S(1)} async-done(((f32[8,96,128]{2,1,0:T(8,128)}), f32[8,96,128]{2,1,0:T(8,128)S(1)}, u32[]{:S(2)}, u32[]{:S(2)}) %all-to-all-start.2) | async-done | bytes 393248 | tf_op jit(solution)/shard_map/all_to_all | solution.py:585
  95.7 0.3 collective-permute-start.4
  96.0 10.7 %shard_map.100.upper_ref = f32[3,4,2048]{2,1,0:T(4,128)S(1)} custom-call(s32[5,32]{1,0:T(8,128)S(1)} %bitcast.32, f32[1,5120]{1,0:T(1,128)S(1)} %pad_maximum_fusion.1.charge_ref, f32[8,96,128]{2,1,0:T(8,128)S(1)} %all-to-all-done.2.both_ref), custom_call_target="tpu_custom_call" | custom-call | flops 104858624 | bytes 4194304 | tf_op jit(solution)/shard_map/pallas_call | solution.py:319
  106.6 0.0 collective-permute-done.4.message_ref
  106.7 11.4 %shard_map.101 = (f32[3,4,4096]{2,1,0:T(4,128)}, f32[3,4,4096]{2,1,0:T(4,128)}) custom-call(s32[5,32]{1,0:T(8,128)S(1)} %bitcast.33, f32[1,3072]{1,0:T(1,128)S(1)} %pad_maximum_fusion.3.charge_ref, f32[8,96,128]{2,1,0:T(8,128)S(1)} %all-to-all-done.2.both_ref, f32[10,4,512]{2,1,0:T(4,128)S(1)} %collective-permute-done.4.message_ref, ...), custom_call_target="tpu_custom_call" | custom-call | flops 104858624 | bytes 4194304 | tf_op jit(solution)/shard_map/pallas_call | solution.py:319
  (18 shorter events, 0.2 us)
Async XLA Ops:
  2.7 6.5 %copy-start.9 = (f32[13,4,512]{2,1,0:T(4,128)S(1)}, f32[13,4,512]{2,1,0:T(4,128)}, u32[]{:S(2)}) copy-start(f32[13,4,512]{2,1,0:T(4,128)} %get-tuple-element.12) | copy-start | bytes 319492
  2.7 9.0 %copy-start.5 = (s32[32,5]{0,1:T(8,128)S(1)}, s32[32,5]{0,1:T(8,128)}, u32[]{:S(2)}) copy-start(s32[32,5]{0,1:T(8,128)} %param.11) | copy-start | bytes 1924
  2.7 9.1 %copy-start = (f32[3,4,4096]{2,1,0:T(4,128)S(1)}, f32[3,4,4096]{2,1,0:T(4,128)}, u32[]{:S(2)}) copy-start(f32[3,4,4096]{2,1,0:T(4,128)} %x_ref.5) | copy-start | bytes 589828
  2.7 9.1 %copy-start.1 = (f32[3,4,4096]{2,1,0:T(4,128)S(1)}, f32[3,4,4096]{2,1,0:T(4,128)}, u32[]{:S(2)}) copy-start(f32[3,4,4096]{2,1,0:T(4,128)} %p_ref.3) | copy-start | bytes 589828
  2.7 20.6 %all-to-all-start = ((f32[8,144,128]{2,1,0:T(8,128)}), f32[8,144,128]{2,1,0:T(8,128)S(1)}, u32[]{:S(2)}, u32[]{:S(2)}) async-start(f32[8,144,128]{2,1,0:T(8,128)} %get-tuple-element.14), calls=%async_computation | async-start | bytes 1179648 | tf_op jit(solution)/shard_map/all_to_all | solution.py:585
  9.1 2.6 %copy-start.8 = (f32[1,4096]{1,0:T(1,128)S(1)}, f32[1,4096]{1,0:T(1,128)}, u32[]{:S(2)}) copy-start(f32[1,4096]{1,0:T(1,128)} %get-tuple-element.19) | copy-start | bytes 49156
  9.2 14.0 %collective-permute-start = (f32[13,4,512]{2,1,0:T(4,128)S(1)}, f32[13,4,512]{2,1,0:T(4,128)S(1)}, u32[]{:S(2)}, u32[]{:S(2)}) collective-permute-start(f32[13,4,512]{2,1,0:T(4,128)S(1)} %copy-done.9), channel_id=1, source_target_pairs={{0,3},{1,0},{2,1},{3,2},{4,7},{5,4},{6,5},{7,6},{8,11},{9,8},{10,9... | collective-permute-start | bytes 319496 | tf_op jit(solution)/shard_map/ppermute | solution.py:590
  11.7 0.7 copy-start.6
  23.2 3.6 %copy-start.7 = (f32[1,4096]{1,0:T(1,128)S(1)}, f32[1,4096]{1,0:T(1,128)}, u32[]{:S(2)}) copy-start(f32[1,4096]{1,0:T(1,128)} %get-tuple-element.13) | copy-start | bytes 49156
  23.3 14.8 %collective-permute-start.1 = (f32[8,144,128]{2,1,0:T(8,128)S(1)}, f32[8,144,128]{2,1,0:T(8,128)S(1)}, u32[]{:S(2)}, u32[]{:S(2)}) collective-permute-start(f32[8,144,128]{2,1,0:T(8,128)S(1)} %all-to-all-done), channel_id=1, source_target_pairs={{8,0},{16,8},{24,16},{28,24},{20,28},{12,20},{4,12},{1,4},{9,1},{1... | collective-permute-start | bytes 1769480 | tf_op jit(solution)/shard_map/ppermute | solution.py:602
  38.1 11.4 %copy-start.2 = (f32[5,32,128]{2,1,0:T(8,128)S(1)}, f32[5,32,128]{2,1,0:T(8,128)}, u32[]{:S(2)}) copy-start(f32[5,32,128]{2,1,0:T(8,128)} %constant.18.clone.table_ref.refs_8_) | copy-start | bytes 245764
  38.1 11.4 %all-to-all-start.1 = ((f32[8,48,128]{2,1,0:T(8,128)}), f32[8,48,128]{2,1,0:T(8,128)S(1)}, u32[]{:S(2)}, u32[]{:S(2)}) async-start(f32[8,48,128]{2,1,0:T(8,128)} %shard_map.97), calls=%async_computation.1 | async-start | bytes 393216 | tf_op jit(solution)/shard_map/all_to_all | solution.py:585
  41.8 7.7 %copy-start.3 = (f32[32,32]{1,0:T(8,128)S(1)}, f32[32,32]{1,0:T(8,128)}, u32[]{:S(2)}) copy-start(f32[32,32]{1,0:T(8,128)} %constant.16.clone.matrix_ref.refs_6_) | copy-start | bytes 12292
  41.9 7.7 %copy-start.4 = (f32[32,32]{1,0:T(8,128)S(1)}, f32[32,32]{1,0:T(8,128)}, u32[]{:S(2)}) copy-start(f32[32,32]{1,0:T(8,128)} %constant.17.clone.matrix_t_ref.refs_7_) | copy-start | bytes 12292
  50.8 7.4 %collective-permute-start.2 = (f32[8,48,128]{2,1,0:T(8,128)S(1)}, f32[8,48,128]{2,1,0:T(8,128)S(1)}, u32[]{:S(2)}, u32[]{:S(2)}) collective-permute-start(f32[8,48,128]{2,1,0:T(8,128)S(1)} %get-tuple-element.20.refs_1_), channel_id=1, source_target_pairs={{7,0},{0,8},{8,16},{16,24},{24,28},{28,20},{20,12},{12,4},{4,1},{1... | collective-permute-start | bytes 589832 | tf_op jit(solution)/shard_map/ppermute | solution.py:602
  50.9 7.3 %collective-permute-start.3 = (f32[8,48,128]{2,1,0:T(8,128)S(1)}, f32[8,48,128]{2,1,0:T(8,128)S(1)}, u32[]{:S(2)}, u32[]{:S(2)}) collective-permute-start(f32[8,48,128]{2,1,0:T(8,128)S(1)} %get-tuple-element.20.refs_1_), channel_id=1, source_target_pairs={{8,0},{16,8},{24,16},{28,24},{20,28},{12,20},{4,12},{1,4},{9,1},{1... | collective-permute-start | bytes 589832 | tf_op jit(solution)/shard_map/ppermute | solution.py:602
  81.1 14.4 %all-to-all-start.2 = ((f32[8,96,128]{2,1,0:T(8,128)}), f32[8,96,128]{2,1,0:T(8,128)S(1)}, u32[]{:S(2)}, u32[]{:S(2)}) async-start(f32[8,96,128]{2,1,0:T(8,128)} %shard_map.99), calls=%async_computation.2 | async-start | bytes 786432 | tf_op jit(solution)/shard_map/all_to_all | solution.py:585
  95.7 11.0 %collective-permute-start.4 = (f32[10,4,512]{2,1,0:T(4,128)S(1)}, f32[10,4,512]{2,1,0:T(4,128)S(1)}, u32[]{:S(2)}, u32[]{:S(2)}) collective-permute-start(f32[10,4,512]{2,1,0:T(4,128)S(1)} %pad_maximum_fusion), channel_id=1, source_target_pairs={{0,1},{1,2},{2,3},{3,0},{4,5},{5,6},{6,7},{7,4},{8,9},{9,10},{10,1... | collective-permute-start | bytes 245768 | tf_op jit(solution)/shard_map/ppermute | solution.py:590

commit v8 on v7

--- a/solution.py
+++ b/solution.py
@@ -58,6 +58,15 @@
     tables = np.stack([np.cos(angle), ratio, frequency * np.sin(angle), damping, kick])
     tables = np.broadcast_to(tables[:, :, None], tables.shape + (BLOCK,))
     return matrix.astype(np.float32), np.ascontiguousarray(tables).astype(np.float32)
+
+
+def split_rows(matrix):
+    parts = []
+    for _ in range(3):
+        parts.append(matrix.astype(jnp.bfloat16))
+        matrix = matrix - parts[-1].astype(np.float32)
+    one, two, three = parts
+    return jnp.asarray(np.concatenate([one, one, two, two, one, three], axis=1))
 
 
 def split3(v):
@@ -236,9 +245,12 @@
         ]
         return jnp.concatenate(columns, axis=1)
 
-    def weighted(at, pair, both):
-        table = heavy_ref[at, pair]
-        return jnp.dot(jnp.concatenate([table, table], axis=1), both, preferred_element_type=f32)
+    def sums(ats, pair, weight_ref):
+        tables = [heavy_ref[at, pair] for at in ats]
+        return jnp.dot(
+            jnp.concatenate([part for table in tables for part in (table, table)], axis=1),
+            weight_ref[...], preferred_element_type=f32,
+        )
 
     def keep(total, slot):
         for i in range(2):
@@ -254,25 +266,17 @@
             now, other = turn % 2, (turn + 1) % 2
             ats, pair = places(unit)
             near = own_columns(unit, turn % 2)
-            total = jnp.zeros((2 * SUM_ROWS, 2 * BLOCK), f32)
+            keep(sums(before_ats, before_pair, weight_refs[other]), jnp.where(unit == 0, units, unit - 1))
             for m in range(listed):
                 spot = slice(2 * m * BLOCK, 2 * (m + 1) * BLOCK)
                 weight_refs[now][spot, :] = jnp.concatenate(parts(squares(ats, pair, near, m)), axis=0)
-                total = total + weighted(before_ats[m], before_pair, weight_refs[other][spot, :])
-            keep(total, jnp.where(unit == 0, units, unit - 1))
             before_ats, before_pair = ats, pair
         return carry
 
     group = math.gcd(units, group)
     lax.fori_loop(0, units // group, body, 0)
     last_ats, last_pair = places(units - 1)
-    keep(
-        sum(
-            weighted(last_ats[m], last_pair, weight_refs[(group - 1) % 2][2 * m * BLOCK:2 * (m + 1) * BLOCK, :])
-            for m in range(listed)
-        ),
-        units - 1,
-    )
+    keep(sums(last_ats, last_pair, weight_refs[(group - 1) % 2]), units - 1)
 
     def one_block(block, slot):
         at_frame = block // frame
@@ -508,15 +512,24 @@
     spread = kick * jnp.sqrt(thermal * mass)
     drift = ratio / mass
     stiff = stiffness * mass
-    multiply = functools.partial(jnp.dot, precision=lax.Precision.HIGHEST, preferred_element_type=f32)
-    for c in range(3):
-        mode_x = multiply(matrix_t_ref[...], coords[c])
-        mode_p = damping * multiply(matrix_t_ref[...], moments[c]) + spread * noises[c]
-        store(
-            c,
-            multiply(matrix_ref[...], cosine * mode_x + drift * mode_p),
-            multiply(matrix_ref[...], cosine * mode_p - stiff * mode_x),
-        )
+
+    def multiply(matrix, values):
+        joined = jnp.concatenate(values, axis=1)
+        one, two, three = [part.astype(bf16) for part in split3(joined)]
+        rows = jnp.concatenate([one, two, one, two, three, one], axis=0)
+        out = jnp.dot(matrix, rows, preferred_element_type=f32)
+        return [out[:, i * width:(i + 1) * width] for i in range(len(values))]
+
+    mode = multiply(matrix_t_ref[...], coords + moments)
+    next_x, next_p = [], []
+    for c in range(3):
+        mode_x = mode[c]
+        mode_p = damping * mode[3 + c] + spread * noises[c]
+        next_x.append(cosine * mode_x + drift * mode_p)
+        next_p.append(cosine * mode_p - stiff * mode_x)
+    beads_now = multiply(matrix_ref[...], next_x + next_p)
+    for c in range(3):
+        store(c, beads_now[c], beads_now[3 + c])
 
 
 def modes_kernel(
@@ -643,7 +656,7 @@
     matrix, tables = mode_constants(beads)
     at = np.concatenate([order.index(g) * local + np.arange(local) for g in range(count)])
     matrix = matrix[at][:, at]
-    fixed = (moved_mass, jnp.asarray(matrix), jnp.asarray(np.ascontiguousarray(matrix.T)), jnp.asarray(tables[:, at]))
+    fixed = (moved_mass, split_rows(matrix), split_rows(matrix.T), jnp.asarray(tables[:, at]))
 
     pairs = beads * blocks * listed * BLOCK * BLOCK
     half = domain // 2

time: 119 us -> 119 us (level)
  transfers between devices with their start and end apart: 8 -> 8, of which waited for: 4 -> 3; matrix products, arithmetic and copies ran while one was open for 0% -> 0% of each run, Pallas kernels for 28% -> 28%
where the time goes in v8:
time: 119 us; the launch traced here: 118 us
  Pallas kernels  70.8 us (59%)
  waiting for transfers between devices  23.4 us (20%)
  starting transfers between devices  22.1 us (19%)
    pallas_call x7, Pallas kernels, call(): pl.pallas_call(kernel, out_shape=[jax.ShapeDtypeStruct(shape, f32) for sh...  70.8 us
    all_to_all x3, waiting for transfers between devices, exchange(): lax.all_to_all(pieces, 'bead', split_axis=0, concat_axis=0, axis_index_gr...  18.7 us
    all_to_all x3, starting transfers between devices, exchange(): lax.all_to_all(pieces, 'bead', split_axis=0, concat_axis=0, axis_index_gr...  13.4 us
    ppermute x3, starting transfers between devices, round_ring(): lax.ppermute(values, ('bead', 'space'), [(device[(at + hop) % total], dev...  5.84 us
    ppermute x3, waiting for transfers between devices, round_ring(): lax.ppermute(values, ('bead', 'space'), [(device[(at + hop) % total], dev...  4.7 us
    ppermute x2, starting transfers between devices, passed(): lax.ppermute(values, 'space', [(i, (i + step) % count) for i in range(cou...  2.79 us
  transfers between devices with their start and end apart: 8, of which 3 were waited for; matrix products, arithmetic and copies ran while one was open for 0% of the time, Pallas kernels for 28%

profile of v8, /device:TPU:0, one launch (start us, length us, event | category | flops | bytes accessed | tf_op | source)
XLA Modules:
  0.0 118.4 jit_solution(4352264457733580362)
XLA Ops:
  0.6 2.0 %shard_map.95 = (f32[8,144,128]{2,1,0:T(8,128)}, f32[13,4,512]{2,1,0:T(4,128)}, f32[1,4096]{1,0:T(1,128)}, f32[1,4096]{1,0:T(1,128)}) custom-call(f32[3,4,4096]{2,1,0:T(4,128)} %x_ref.5, f32[3,4,4096]{2,1,0:T(4,128)} %p_ref.3, f32[2,3,4,4096]{3,2,1,0:T(4,128)} %noise_ref.1, s32[1,4096]{1,0:T(1,128)} %bitcast.34, s32[5,32]{1,0:T(8,128)} %bitcast.29), custom_call_target="tpu_custom_call" | custom-call | flops 1024 | bytes 4194304 | tf_op jit(solution)/shard_map/pallas_call | solution.py:323
  2.7 0.0 copy-start.9
  2.7 0.0 copy-start.5
  2.7 0.0 copy-start
  2.7 0.0 copy-start.1
  2.7 6.5 %all-to-all-start = ((f32[8,144,128]{2,1,0:T(8,128)}), f32[8,144,128]{2,1,0:T(8,128)S(1)}, u32[]{:S(2)}, u32[]{:S(2)}) async-start(f32[8,144,128]{2,1,0:T(8,128)} %get-tuple-element.14), calls=%async_computation | async-start | bytes 1179648 | tf_op jit(solution)/shard_map/all_to_all | solution.py:598
  9.1 0.0 copy-start.8
  9.2 0.0 copy-done.9
  9.2 2.5 %collective-permute-start = (f32[13,4,512]{2,1,0:T(4,128)S(1)}, f32[13,4,512]{2,1,0:T(4,128)S(1)}, u32[]{:S(2)}, u32[]{:S(2)}) collective-permute-start(f32[13,4,512]{2,1,0:T(4,128)S(1)} %copy-done.9), channel_id=1, source_target_pairs={{0,3},{1,0},{2,1},{3,2},{4,7},{5,4},{6,5},{7,6},{8,11},{9,8},{10,9... | collective-permute-start | bytes 319496 | tf_op jit(solution)/shard_map/ppermute | solution.py:603
  11.7 0.0 copy-done.5
  11.7 0.1 slice.54
  11.7 0.0 copy-done.8
  11.7 0.0 copy-start.6
  11.7 0.0 copy-done
  11.7 0.0 copy-done.1
  11.8 0.7 copy-done.6
  12.5 10.9 %shard_map.96.front_ref = f32[4,48,128]{2,1,0:T(8,128)S(1)} custom-call(s32[5,32]{1,0:T(8,128)S(1)} %bitcast.31, s32[1,4096]{1,0:T(1,128)S(1)} %bitcast.35, f32[3,4,4096]{2,1,0:T(4,128)S(1)} %copy-done, f32[3,4,4096]{2,1,0:T(4,128)S(1)} %copy-done.1), custom_call_target="tpu_custom_call" | custom-call | flops 104858624 | bytes 4194304 | tf_op jit(solution)/shard_map/pallas_call | solution.py:323
  23.4 0.0 collective-permute-done.message_ref
  23.4 0.0 copy-start.7
  23.4 0.1 reshape_squeeze.3
  23.5 0.0 all-to-all-done
  23.5 3.1 %collective-permute-start.1 = (f32[8,144,128]{2,1,0:T(8,128)S(1)}, f32[8,144,128]{2,1,0:T(8,128)S(1)}, u32[]{:S(2)}, u32[]{:S(2)}) collective-permute-start(f32[8,144,128]{2,1,0:T(8,128)S(1)} %all-to-all-done), channel_id=1, source_target_pairs={{8,0},{16,8},{24,16},{28,24},{20,28},{12,20},{4,12},{1,4},{9,1},{1... | collective-permute-start | bytes 1769480 | tf_op jit(solution)/shard_map/ppermute | solution.py:615
  26.7 0.1 pad_add_fusion.lists_ref
  26.8 0.0 copy-done.7
  26.8 11.6 %shard_map.97 = f32[8,48,128]{2,1,0:T(8,128)} custom-call(s32[5,32]{1,0:T(8,128)S(1)} %pad_add_fusion.lists_ref, f32[1,5120]{1,0:T(1,128)S(1)} %pad_maximum_fusion.1.charge_ref, f32[3,4,4096]{2,1,0:T(4,128)S(1)} %copy-done, f32[13,4,512]{2,1,0:T(4,128)S(1)} %collective-permute-done.message_ref, f32[3,4,4096]{2,1,0:T(4,128)S(1)} %copy-done.1, ...), custom_call_target="tpu_custom_call" | custom-call | flops 104858624 | bytes 4194304 | tf_op jit(solution)/shard_map/pallas_call | solution.py:323
  38.4 0.0 collective-permute-done.1.rest_ref.refs_4_
  38.4 0.0 copy-start.2
  38.4 3.5 %all-to-all-start.1 = ((f32[8,48,128]{2,1,0:T(8,128)}), f32[8,48,128]{2,1,0:T(8,128)S(1)}, u32[]{:S(2)}, u32[]{:S(2)}) async-start(f32[8,48,128]{2,1,0:T(8,128)} %shard_map.97), calls=%async_computation.1 | async-start | bytes 393216 | tf_op jit(solution)/shard_map/all_to_all | solution.py:598
  41.9 0.0 copy-start.3
  42.0 0.0 copy-start.4
  42.0 7.8 %all-to-all-done.1.p_ref = f32[8,48,128]{2,1,0:T(8,128)S(1)} async-done(((f32[8,48,128]{2,1,0:T(8,128)}), f32[8,48,128]{2,1,0:T(8,128)S(1)}, u32[]{:S(2)}, u32[]{:S(2)}) %all-to-all-start.1) | async-done | bytes 196640 | tf_op jit(solution)/shard_map/all_to_all | solution.py:598
  49.8 0.0 copy-done.2
  49.8 0.0 copy-done.3
  49.8 0.0 copy-done.4
  49.8 0.7 shard_map.98
  50.5 0.1 collective-permute-start.2
  50.6 2.6 %collective-permute-start.3 = (f32[8,48,128]{2,1,0:T(8,128)S(1)}, f32[8,48,128]{2,1,0:T(8,128)S(1)}, u32[]{:S(2)}, u32[]{:S(2)}) collective-permute-start(f32[8,48,128]{2,1,0:T(8,128)S(1)} %get-tuple-element.20.refs_1_), channel_id=1, source_target_pairs={{8,0},{16,8},{24,16},{28,24},{20,28},{12,20},{4,12},{1,4},{9,1},{1... | collective-permute-start | bytes 589832 | tf_op jit(solution)/shard_map/ppermute | solution.py:615
  53.2 4.7 %collective-permute-done.2.refs_0_ = f32[8,48,128]{2,1,0:T(8,128)S(1)} collective-permute-done((f32[8,48,128]{2,1,0:T(8,128)S(1)}, f32[8,48,128]{2,1,0:T(8,128)S(1)}, u32[]{:S(2)}, u32[]{:S(2)}) %collective-permute-start.2) | collective-permute-done | bytes 196640 | tf_op jit(solution)/shard_map/ppermute | solution.py:615
  57.9 0.0 collective-permute-done.3.refs_2_
  57.9 22.9 %shard_map.99 = f32[8,96,128]{2,1,0:T(8,128)} custom-call(s32[5,32]{1,0:T(8,128)S(1)} %pad_add_fusion.lists_ref, f32[1,5120]{1,0:T(1,128)S(1)} %pad_maximum_fusion.1.charge_ref, f32[8,48,128]{2,1,0:T(8,128)S(1)} %collective-permute-done.2.refs_0_, f32[8,48,128]{2,1,0:T(8,128)S(1)} %get-tuple-element.20.refs_1_, ...), custom_call_target="tpu_custom_call" | custom-call | flops 209716224 | bytes 4194304 | tf_op jit(solution)/shard_map/pallas_call | solution.py:323
  80.8 3.5 %all-to-all-start.2 = ((f32[8,96,128]{2,1,0:T(8,128)}), f32[8,96,128]{2,1,0:T(8,128)S(1)}, u32[]{:S(2)}, u32[]{:S(2)}) async-start(f32[8,96,128]{2,1,0:T(8,128)} %shard_map.99), calls=%async_computation.2 | async-start | bytes 786432 | tf_op jit(solution)/shard_map/all_to_all | solution.py:598
  84.3 10.9 %all-to-all-done.2.both_ref = f32[8,96,128]{2,1,0:T(8,128)S(1)} async-done(((f32[8,96,128]{2,1,0:T(8,128)}), f32[8,96,128]{2,1,0:T(8,128)S(1)}, u32[]{:S(2)}, u32[]{:S(2)}) %all-to-all-start.2) | async-done | bytes 393248 | tf_op jit(solution)/shard_map/all_to_all | solution.py:598
  95.4 0.3 collective-permute-start.4
  95.7 10.9 %shard_map.100.upper_ref = f32[3,4,2048]{2,1,0:T(4,128)S(1)} custom-call(s32[5,32]{1,0:T(8,128)S(1)} %bitcast.32, f32[1,5120]{1,0:T(1,128)S(1)} %pad_maximum_fusion.1.charge_ref, f32[8,96,128]{2,1,0:T(8,128)S(1)} %all-to-all-done.2.both_ref), custom_call_target="tpu_custom_call" | custom-call | flops 104858624 | bytes 4194304 | tf_op jit(solution)/shard_map/pallas_call | solution.py:323
  106.6 0.0 collective-permute-done.4.message_ref
  106.7 11.7 %shard_map.101 = (f32[3,4,4096]{2,1,0:T(4,128)}, f32[3,4,4096]{2,1,0:T(4,128)}) custom-call(s32[5,32]{1,0:T(8,128)S(1)} %bitcast.33, f32[1,3072]{1,0:T(1,128)S(1)} %pad_maximum_fusion.3.charge_ref, f32[8,96,128]{2,1,0:T(8,128)S(1)} %all-to-all-done.2.both_ref, f32[10,4,512]{2,1,0:T(4,128)S(1)} %collective-permute-done.4.message_ref, ...), custom_call_target="tpu_custom_call" | custom-call | flops 104858624 | bytes 4194304 | tf_op jit(solution)/shard_map/pallas_call | solution.py:323
  (18 shorter events, 0.2 us)
Async XLA Ops:
  2.7 6.5 %copy-start.9 = (f32[13,4,512]{2,1,0:T(4,128)S(1)}, f32[13,4,512]{2,1,0:T(4,128)}, u32[]{:S(2)}) copy-start(f32[13,4,512]{2,1,0:T(4,128)} %get-tuple-element.12) | copy-start | bytes 319492
  2.7 9.0 %copy-start.5 = (s32[32,5]{0,1:T(8,128)S(1)}, s32[32,5]{0,1:T(8,128)}, u32[]{:S(2)}) copy-start(s32[32,5]{0,1:T(8,128)} %param.11) | copy-start | bytes 1924
  2.7 9.1 %copy-start = (f32[3,4,4096]{2,1,0:T(4,128)S(1)}, f32[3,4,4096]{2,1,0:T(4,128)}, u32[]{:S(2)}) copy-start(f32[3,4,4096]{2,1,0:T(4,128)} %x_ref.5) | copy-start | bytes 589828
  2.7 9.1 %copy-start.1 = (f32[3,4,4096]{2,1,0:T(4,128)S(1)}, f32[3,4,4096]{2,1,0:T(4,128)}, u32[]{:S(2)}) copy-start(f32[3,4,4096]{2,1,0:T(4,128)} %p_ref.3) | copy-start | bytes 589828
  2.7 20.9 %all-to-all-start = ((f32[8,144,128]{2,1,0:T(8,128)}), f32[8,144,128]{2,1,0:T(8,128)S(1)}, u32[]{:S(2)}, u32[]{:S(2)}) async-start(f32[8,144,128]{2,1,0:T(8,128)} %get-tuple-element.14), calls=%async_computation | async-start | bytes 1179648 | tf_op jit(solution)/shard_map/all_to_all | solution.py:598
  9.1 2.6 %copy-start.8 = (f32[1,4096]{1,0:T(1,128)S(1)}, f32[1,4096]{1,0:T(1,128)}, u32[]{:S(2)}) copy-start(f32[1,4096]{1,0:T(1,128)} %get-tuple-element.19) | copy-start | bytes 49156
  9.2 14.2 %collective-permute-start = (f32[13,4,512]{2,1,0:T(4,128)S(1)}, f32[13,4,512]{2,1,0:T(4,128)S(1)}, u32[]{:S(2)}, u32[]{:S(2)}) collective-permute-start(f32[13,4,512]{2,1,0:T(4,128)S(1)} %copy-done.9), channel_id=1, source_target_pairs={{0,3},{1,0},{2,1},{3,2},{4,7},{5,4},{6,5},{7,6},{8,11},{9,8},{10,9... | collective-permute-start | bytes 319496 | tf_op jit(solution)/shard_map/ppermute | solution.py:603
  11.7 0.7 copy-start.6
  23.4 3.3 %copy-start.7 = (f32[1,4096]{1,0:T(1,128)S(1)}, f32[1,4096]{1,0:T(1,128)}, u32[]{:S(2)}) copy-start(f32[1,4096]{1,0:T(1,128)} %get-tuple-element.13) | copy-start | bytes 49156
  23.5 14.9 %collective-permute-start.1 = (f32[8,144,128]{2,1,0:T(8,128)S(1)}, f32[8,144,128]{2,1,0:T(8,128)S(1)}, u32[]{:S(2)}, u32[]{:S(2)}) collective-permute-start(f32[8,144,128]{2,1,0:T(8,128)S(1)} %all-to-all-done), channel_id=1, source_target_pairs={{8,0},{16,8},{24,16},{28,24},{20,28},{12,20},{4,12},{1,4},{9,1},{1... | collective-permute-start | bytes 1769480 | tf_op jit(solution)/shard_map/ppermute | solution.py:615
  38.4 11.4 %copy-start.2 = (f32[5,32,128]{2,1,0:T(8,128)S(1)}, f32[5,32,128]{2,1,0:T(8,128)}, u32[]{:S(2)}) copy-start(f32[5,32,128]{2,1,0:T(8,128)} %constant.18.clone.table_ref.refs_8_) | copy-start | bytes 245764
  38.4 11.4 %all-to-all-start.1 = ((f32[8,48,128]{2,1,0:T(8,128)}), f32[8,48,128]{2,1,0:T(8,128)S(1)}, u32[]{:S(2)}, u32[]{:S(2)}) async-start(f32[8,48,128]{2,1,0:T(8,128)} %shard_map.97), calls=%async_computation.1 | async-start | bytes 393216 | tf_op jit(solution)/shard_map/all_to_all | solution.py:598
  41.9 7.9 %copy-start.3 = (bf16[32,192]{1,0:T(8,128)(2,1)S(1)}, bf16[32,192]{1,0:T(8,128)(2,1)}, u32[]{:S(2)}) copy-start(bf16[32,192]{1,0:T(8,128)(2,1)} %constant.16.clone.matrix_ref.refs_6_) | copy-start | bytes 36868
  42.0 7.9 %copy-start.4 = (bf16[32,192]{1,0:T(8,128)(2,1)S(1)}, bf16[32,192]{1,0:T(8,128)(2,1)}, u32[]{:S(2)}) copy-start(bf16[32,192]{1,0:T(8,128)(2,1)} %constant.17.clone.matrix_t_ref.refs_7_) | copy-start | bytes 36868
  50.5 7.4 %collective-permute-start.2 = (f32[8,48,128]{2,1,0:T(8,128)S(1)}, f32[8,48,128]{2,1,0:T(8,128)S(1)}, u32[]{:S(2)}, u32[]{:S(2)}) collective-permute-start(f32[8,48,128]{2,1,0:T(8,128)S(1)} %get-tuple-element.20.refs_1_), channel_id=1, source_target_pairs={{7,0},{0,8},{8,16},{16,24},{24,28},{28,20},{20,12},{12,4},{4,1},{1... | collective-permute-start | bytes 589832 | tf_op jit(solution)/shard_map/ppermute | solution.py:615
  50.6 7.3 %collective-permute-start.3 = (f32[8,48,128]{2,1,0:T(8,128)S(1)}, f32[8,48,128]{2,1,0:T(8,128)S(1)}, u32[]{:S(2)}, u32[]{:S(2)}) collective-permute-start(f32[8,48,128]{2,1,0:T(8,128)S(1)} %get-tuple-element.20.refs_1_), channel_id=1, source_target_pairs={{8,0},{16,8},{24,16},{28,24},{20,28},{12,20},{4,12},{1,4},{9,1},{1... | collective-permute-start | bytes 589832 | tf_op jit(solution)/shard_map/ppermute | solution.py:615
  80.8 14.4 %all-to-all-start.2 = ((f32[8,96,128]{2,1,0:T(8,128)}), f32[8,96,128]{2,1,0:T(8,128)S(1)}, u32[]{:S(2)}, u32[]{:S(2)}) async-start(f32[8,96,128]{2,1,0:T(8,128)} %shard_map.99), calls=%async_computation.2 | async-start | bytes 786432 | tf_op jit(solution)/shard_map/all_to_all | solution.py:598
  95.4 11.2 %collective-permute-start.4 = (f32[10,4,512]{2,1,0:T(4,128)S(1)}, f32[10,4,512]{2,1,0:T(4,128)S(1)}, u32[]{:S(2)}, u32[]{:S(2)}) collective-permute-start(f32[10,4,512]{2,1,0:T(4,128)S(1)} %pad_maximum_fusion), channel_id=1, source_target_pairs={{0,1},{1,2},{2,3},{3,0},{4,5},{5,6},{6,7},{7,4},{8,9},{9,10},{10,1... | collective-permute-start | bytes 245768 | tf_op jit(solution)/shard_map/ppermute | solution.py:603

commit v9 on v8

--- a/solution.py
+++ b/solution.py
@@ -182,6 +182,10 @@
             put(sums_ref, slot, k, nothing)
     blank = jnp.zeros((PAIR_PAD, BLOCK), bf16)
     passes = width // at_once
+    square = (BLOCK, BLOCK)
+    unit_matrix = (
+        lax.broadcasted_iota(jnp.int32, square, 0) == lax.broadcasted_iota(jnp.int32, square, 1)
+    ).astype(f32).astype(bf16)
 
     def one_table(step, slot):
         at_frame = step // passes
@@ -199,7 +203,9 @@
                 four = jnp.concatenate(
                     [rows_ref[slot, pl.ds(low + j, PAIR_PAD, stride=apart), :] for j in range(QUAD)], axis=0
                 )
-                far_ref[at, quad] = jnp.transpose(four.astype(bf16))
+                far_ref[at, quad] = lax.dot_general(
+                    unit_matrix, four.astype(bf16), (((1,), (1,)), ((), ())), preferred_element_type=f32
+                ).astype(bf16)
                 for half in range(2):
                     heavy_ref[at, 2 * quad + half] = jnp.concatenate(
                         [
@@ -245,12 +251,9 @@
         ]
         return jnp.concatenate(columns, axis=1)
 
-    def sums(ats, pair, weight_ref):
-        tables = [heavy_ref[at, pair] for at in ats]
-        return jnp.dot(
-            jnp.concatenate([part for table in tables for part in (table, table)], axis=1),
-            weight_ref[...], preferred_element_type=f32,
-        )
+    def weighted(at, pair, both):
+        table = heavy_ref[at, pair]
+        return jnp.dot(jnp.concatenate([table, table], axis=1), both, preferred_element_type=f32)
 
     def keep(total, slot):
         for i in range(2):
@@ -266,17 +269,25 @@
             now, other = turn % 2, (turn + 1) % 2
             ats, pair = places(unit)
             near = own_columns(unit, turn % 2)
-            keep(sums(before_ats, before_pair, weight_refs[other]), jnp.where(unit == 0, units, unit - 1))
+            total = jnp.zeros((2 * SUM_ROWS, 2 * BLOCK), f32)
             for m in range(listed):
                 spot = slice(2 * m * BLOCK, 2 * (m + 1) * BLOCK)
                 weight_refs[now][spot, :] = jnp.concatenate(parts(squares(ats, pair, near, m)), axis=0)
+                total = total + weighted(before_ats[m], before_pair, weight_refs[other][spot, :])
+            keep(total, jnp.where(unit == 0, units, unit - 1))
             before_ats, before_pair = ats, pair
         return carry
 
     group = math.gcd(units, group)
     lax.fori_loop(0, units // group, body, 0)
     last_ats, last_pair = places(units - 1)
-    keep(sums(last_ats, last_pair, weight_refs[(group - 1) % 2]), units - 1)
+    keep(
+        sum(
+            weighted(last_ats[m], last_pair, weight_refs[(group - 1) % 2][2 * m * BLOCK:2 * (m + 1) * BLOCK, :])
+            for m in range(listed)
+        ),
+        units - 1,
+    )
 
     def one_block(block, slot):
         at_frame = block // frame

time: 119 us -> 119 us (level)
  no operation moved by 1% of the time
where the time goes in v9:
time: 119 us; the launch traced here: 118 us
  Pallas kernels  70.7 us (59%)
  waiting for transfers between devices  23.4 us (20%)
  starting transfers between devices  22.1 us (19%)
    pallas_call x7, Pallas kernels, call(): pl.pallas_call(kernel, out_shape=[jax.ShapeDtypeStruct(shape, f32) for sh...  70.7 us
    all_to_all x3, waiting for transfers between devices, exchange(): lax.all_to_all(pieces, 'bead', split_axis=0, concat_axis=0, axis_index_gr...  18.7 us
    all_to_all x3, starting transfers between devices, exchange(): lax.all_to_all(pieces, 'bead', split_axis=0, concat_axis=0, axis_index_gr...  13.4 us
    ppermute x3, starting transfers between devices, round_ring(): lax.ppermute(values, ('bead', 'space'), [(device[(at + hop) % total], dev...  5.86 us
    ppermute x3, waiting for transfers between devices, round_ring(): lax.ppermute(values, ('bead', 'space'), [(device[(at + hop) % total], dev...  4.7 us
    ppermute x2, starting transfers between devices, passed(): lax.ppermute(values, 'space', [(i, (i + step) % count) for i in range(cou...  2.78 us
  transfers between devices with their start and end apart: 8, of which 3 were waited for; matrix products, arithmetic and copies ran while one was open for 0% of the time, Pallas kernels for 28%

profile of v9, /device:TPU:0, one launch (start us, length us, event | category | flops | bytes accessed | tf_op | source)
XLA Modules:
  0.0 118.2 jit_solution(2500247258144310460)
XLA Ops:
  0.6 2.0 %shard_map.95 = (f32[8,144,128]{2,1,0:T(8,128)}, f32[13,4,512]{2,1,0:T(4,128)}, f32[1,4096]{1,0:T(1,128)}, f32[1,4096]{1,0:T(1,128)}) custom-call(f32[3,4,4096]{2,1,0:T(4,128)} %x_ref.5, f32[3,4,4096]{2,1,0:T(4,128)} %p_ref.3, f32[2,3,4,4096]{3,2,1,0:T(4,128)} %noise_ref.1, s32[1,4096]{1,0:T(1,128)} %bitcast.34, s32[5,32]{1,0:T(8,128)} %bitcast.29), custom_call_target="tpu_custom_call" | custom-call | flops 1024 | bytes 4194304 | tf_op jit(solution)/shard_map/pallas_call | solution.py:334
  2.7 0.0 copy-start.9
  2.7 0.0 copy-start.5
  2.7 0.0 copy-start
  2.7 0.0 copy-start.1
  2.7 6.5 %all-to-all-start = ((f32[8,144,128]{2,1,0:T(8,128)}), f32[8,144,128]{2,1,0:T(8,128)S(1)}, u32[]{:S(2)}, u32[]{:S(2)}) async-start(f32[8,144,128]{2,1,0:T(8,128)} %get-tuple-element.14), calls=%async_computation | async-start | bytes 1179648 | tf_op jit(solution)/shard_map/all_to_all | solution.py:609
  9.1 0.0 copy-start.8
  9.2 0.0 copy-done.9
  9.2 2.5 %collective-permute-start = (f32[13,4,512]{2,1,0:T(4,128)S(1)}, f32[13,4,512]{2,1,0:T(4,128)S(1)}, u32[]{:S(2)}, u32[]{:S(2)}) collective-permute-start(f32[13,4,512]{2,1,0:T(4,128)S(1)} %copy-done.9), channel_id=1, source_target_pairs={{0,3},{1,0},{2,1},{3,2},{4,7},{5,4},{6,5},{7,6},{8,11},{9,8},{10,9... | collective-permute-start | bytes 319496 | tf_op jit(solution)/shard_map/ppermute | solution.py:614
  11.7 0.0 copy-done.5
  11.7 0.1 slice.54
  11.7 0.0 copy-done.8
  11.7 0.0 copy-start.6
  11.7 0.0 copy-done
  11.7 0.0 copy-done.1
  11.8 0.7 copy-done.6
  12.5 10.9 %shard_map.96.front_ref = f32[4,48,128]{2,1,0:T(8,128)S(1)} custom-call(s32[5,32]{1,0:T(8,128)S(1)} %bitcast.31, s32[1,4096]{1,0:T(1,128)S(1)} %bitcast.35, f32[3,4,4096]{2,1,0:T(4,128)S(1)} %copy-done, f32[3,4,4096]{2,1,0:T(4,128)S(1)} %copy-done.1), custom_call_target="tpu_custom_call" | custom-call | flops 104858624 | bytes 4194304 | tf_op jit(solution)/shard_map/pallas_call | solution.py:334
  23.4 0.0 collective-permute-done.message_ref
  23.4 0.0 copy-start.7
  23.4 0.1 reshape_squeeze.3
  23.5 0.0 all-to-all-done
  23.5 3.2 %collective-permute-start.1 = (f32[8,144,128]{2,1,0:T(8,128)S(1)}, f32[8,144,128]{2,1,0:T(8,128)S(1)}, u32[]{:S(2)}, u32[]{:S(2)}) collective-permute-start(f32[8,144,128]{2,1,0:T(8,128)S(1)} %all-to-all-done), channel_id=1, source_target_pairs={{8,0},{16,8},{24,16},{28,24},{20,28},{12,20},{4,12},{1,4},{9,1},{1... | collective-permute-start | bytes 1769480 | tf_op jit(solution)/shard_map/ppermute | solution.py:626
  26.7 0.1 pad_add_fusion.lists_ref
  26.8 0.0 copy-done.7
  26.8 11.6 %shard_map.97 = f32[8,48,128]{2,1,0:T(8,128)} custom-call(s32[5,32]{1,0:T(8,128)S(1)} %pad_add_fusion.lists_ref, f32[1,5120]{1,0:T(1,128)S(1)} %pad_maximum_fusion.1.charge_ref, f32[3,4,4096]{2,1,0:T(4,128)S(1)} %copy-done, f32[13,4,512]{2,1,0:T(4,128)S(1)} %collective-permute-done.message_ref, f32[3,4,4096]{2,1,0:T(4,128)S(1)} %copy-done.1, ...), custom_call_target="tpu_custom_call" | custom-call | flops 104858624 | bytes 4194304 | tf_op jit(solution)/shard_map/pallas_call | solution.py:334
  38.4 0.0 collective-permute-done.1.rest_ref.refs_4_
  38.4 0.0 copy-start.2
  38.4 3.5 %all-to-all-start.1 = ((f32[8,48,128]{2,1,0:T(8,128)}), f32[8,48,128]{2,1,0:T(8,128)S(1)}, u32[]{:S(2)}, u32[]{:S(2)}) async-start(f32[8,48,128]{2,1,0:T(8,128)} %shard_map.97), calls=%async_computation.1 | async-start | bytes 393216 | tf_op jit(solution)/shard_map/all_to_all | solution.py:609
  41.9 0.0 copy-start.3
  41.9 0.0 copy-start.4
  42.0 7.8 %all-to-all-done.1.p_ref = f32[8,48,128]{2,1,0:T(8,128)S(1)} async-done(((f32[8,48,128]{2,1,0:T(8,128)}), f32[8,48,128]{2,1,0:T(8,128)S(1)}, u32[]{:S(2)}, u32[]{:S(2)}) %all-to-all-start.1) | async-done | bytes 196640 | tf_op jit(solution)/shard_map/all_to_all | solution.py:609
  49.8 0.0 copy-done.2
  49.8 0.0 copy-done.3
  49.8 0.0 copy-done.4
  49.8 0.7 shard_map.98
  50.5 0.1 collective-permute-start.2
  50.5 2.6 %collective-permute-start.3 = (f32[8,48,128]{2,1,0:T(8,128)S(1)}, f32[8,48,128]{2,1,0:T(8,128)S(1)}, u32[]{:S(2)}, u32[]{:S(2)}) collective-permute-start(f32[8,48,128]{2,1,0:T(8,128)S(1)} %get-tuple-element.20.refs_1_), channel_id=1, source_target_pairs={{8,0},{16,8},{24,16},{28,24},{20,28},{12,20},{4,12},{1,4},{9,1},{1... | collective-permute-start | bytes 589832 | tf_op jit(solution)/shard_map/ppermute | solution.py:626
  53.2 4.7 %collective-permute-done.2.refs_0_ = f32[8,48,128]{2,1,0:T(8,128)S(1)} collective-permute-done((f32[8,48,128]{2,1,0:T(8,128)S(1)}, f32[8,48,128]{2,1,0:T(8,128)S(1)}, u32[]{:S(2)}, u32[]{:S(2)}) %collective-permute-start.2) | collective-permute-done | bytes 196640 | tf_op jit(solution)/shard_map/ppermute | solution.py:626
  57.9 0.0 collective-permute-done.3.refs_2_
  57.9 22.9 %shard_map.99 = f32[8,96,128]{2,1,0:T(8,128)} custom-call(s32[5,32]{1,0:T(8,128)S(1)} %pad_add_fusion.lists_ref, f32[1,5120]{1,0:T(1,128)S(1)} %pad_maximum_fusion.1.charge_ref, f32[8,48,128]{2,1,0:T(8,128)S(1)} %collective-permute-done.2.refs_0_, f32[8,48,128]{2,1,0:T(8,128)S(1)} %get-tuple-element.20.refs_1_, ...), custom_call_target="tpu_custom_call" | custom-call | flops 209716224 | bytes 4194304 | tf_op jit(solution)/shard_map/pallas_call | solution.py:334
  80.8 3.5 %all-to-all-start.2 = ((f32[8,96,128]{2,1,0:T(8,128)}), f32[8,96,128]{2,1,0:T(8,128)S(1)}, u32[]{:S(2)}, u32[]{:S(2)}) async-start(f32[8,96,128]{2,1,0:T(8,128)} %shard_map.99), calls=%async_computation.2 | async-start | bytes 786432 | tf_op jit(solution)/shard_map/all_to_all | solution.py:609
  84.3 10.9 %all-to-all-done.2.both_ref = f32[8,96,128]{2,1,0:T(8,128)S(1)} async-done(((f32[8,96,128]{2,1,0:T(8,128)}), f32[8,96,128]{2,1,0:T(8,128)S(1)}, u32[]{:S(2)}, u32[]{:S(2)}) %all-to-all-start.2) | async-done | bytes 393248 | tf_op jit(solution)/shard_map/all_to_all | solution.py:609
  95.3 0.3 collective-permute-start.4
  95.6 10.9 %shard_map.100.upper_ref = f32[3,4,2048]{2,1,0:T(4,128)S(1)} custom-call(s32[5,32]{1,0:T(8,128)S(1)} %bitcast.32, f32[1,5120]{1,0:T(1,128)S(1)} %pad_maximum_fusion.1.charge_ref, f32[8,96,128]{2,1,0:T(8,128)S(1)} %all-to-all-done.2.both_ref), custom_call_target="tpu_custom_call" | custom-call | flops 104858624 | bytes 4194304 | tf_op jit(solution)/shard_map/pallas_call | solution.py:334
  106.6 0.0 collective-permute-done.4.message_ref
  106.6 11.6 %shard_map.101 = (f32[3,4,4096]{2,1,0:T(4,128)}, f32[3,4,4096]{2,1,0:T(4,128)}) custom-call(s32[5,32]{1,0:T(8,128)S(1)} %bitcast.33, f32[1,3072]{1,0:T(1,128)S(1)} %pad_maximum_fusion.3.charge_ref, f32[8,96,128]{2,1,0:T(8,128)S(1)} %all-to-all-done.2.both_ref, f32[10,4,512]{2,1,0:T(4,128)S(1)} %collective-permute-done.4.message_ref, ...), custom_call_target="tpu_custom_call" | custom-call | flops 104858624 | bytes 4194304 | tf_op jit(solution)/shard_map/pallas_call | solution.py:334
  (18 shorter events, 0.2 us)
Async XLA Ops:
  2.7 6.5 %copy-start.9 = (f32[13,4,512]{2,1,0:T(4,128)S(1)}, f32[13,4,512]{2,1,0:T(4,128)}, u32[]{:S(2)}) copy-start(f32[13,4,512]{2,1,0:T(4,128)} %get-tuple-element.12) | copy-start | bytes 319492
  2.7 9.0 %copy-start.5 = (s32[32,5]{0,1:T(8,128)S(1)}, s32[32,5]{0,1:T(8,128)}, u32[]{:S(2)}) copy-start(s32[32,5]{0,1:T(8,128)} %param.11) | copy-start | bytes 1924
  2.7 9.1 %copy-start = (f32[3,4,4096]{2,1,0:T(4,128)S(1)}, f32[3,4,4096]{2,1,0:T(4,128)}, u32[]{:S(2)}) copy-start(f32[3,4,4096]{2,1,0:T(4,128)} %x_ref.5) | copy-start | bytes 589828
  2.7 9.1 %copy-start.1 = (f32[3,4,4096]{2,1,0:T(4,128)S(1)}, f32[3,4,4096]{2,1,0:T(4,128)}, u32[]{:S(2)}) copy-start(f32[3,4,4096]{2,1,0:T(4,128)} %p_ref.3) | copy-start | bytes 589828
  2.7 20.8 %all-to-all-start = ((f32[8,144,128]{2,1,0:T(8,128)}), f32[8,144,128]{2,1,0:T(8,128)S(1)}, u32[]{:S(2)}, u32[]{:S(2)}) async-start(f32[8,144,128]{2,1,0:T(8,128)} %get-tuple-element.14), calls=%async_computation | async-start | bytes 1179648 | tf_op jit(solution)/shard_map/all_to_all | solution.py:609
  9.1 2.6 %copy-start.8 = (f32[1,4096]{1,0:T(1,128)S(1)}, f32[1,4096]{1,0:T(1,128)}, u32[]{:S(2)}) copy-start(f32[1,4096]{1,0:T(1,128)} %get-tuple-element.19) | copy-start | bytes 49156
  9.2 14.2 %collective-permute-start = (f32[13,4,512]{2,1,0:T(4,128)S(1)}, f32[13,4,512]{2,1,0:T(4,128)S(1)}, u32[]{:S(2)}, u32[]{:S(2)}) collective-permute-start(f32[13,4,512]{2,1,0:T(4,128)S(1)} %copy-done.9), channel_id=1, source_target_pairs={{0,3},{1,0},{2,1},{3,2},{4,7},{5,4},{6,5},{7,6},{8,11},{9,8},{10,9... | collective-permute-start | bytes 319496 | tf_op jit(solution)/shard_map/ppermute | solution.py:614
  11.7 0.7 copy-start.6
  23.4 3.3 %copy-start.7 = (f32[1,4096]{1,0:T(1,128)S(1)}, f32[1,4096]{1,0:T(1,128)}, u32[]{:S(2)}) copy-start(f32[1,4096]{1,0:T(1,128)} %get-tuple-element.13) | copy-start | bytes 49156
  23.5 14.9 %collective-permute-start.1 = (f32[8,144,128]{2,1,0:T(8,128)S(1)}, f32[8,144,128]{2,1,0:T(8,128)S(1)}, u32[]{:S(2)}, u32[]{:S(2)}) collective-permute-start(f32[8,144,128]{2,1,0:T(8,128)S(1)} %all-to-all-done), channel_id=1, source_target_pairs={{8,0},{16,8},{24,16},{28,24},{20,28},{12,20},{4,12},{1,4},{9,1},{1... | collective-permute-start | bytes 1769480 | tf_op jit(solution)/shard_map/ppermute | solution.py:626
  38.4 11.4 %copy-start.2 = (f32[5,32,128]{2,1,0:T(8,128)S(1)}, f32[5,32,128]{2,1,0:T(8,128)}, u32[]{:S(2)}) copy-start(f32[5,32,128]{2,1,0:T(8,128)} %constant.18.clone.table_ref.refs_8_) | copy-start | bytes 245764
  38.4 11.4 %all-to-all-start.1 = ((f32[8,48,128]{2,1,0:T(8,128)}), f32[8,48,128]{2,1,0:T(8,128)S(1)}, u32[]{:S(2)}, u32[]{:S(2)}) async-start(f32[8,48,128]{2,1,0:T(8,128)} %shard_map.97), calls=%async_computation.1 | async-start | bytes 393216 | tf_op jit(solution)/shard_map/all_to_all | solution.py:609
  41.9 7.9 %copy-start.3 = (bf16[32,192]{1,0:T(8,128)(2,1)S(1)}, bf16[32,192]{1,0:T(8,128)(2,1)}, u32[]{:S(2)}) copy-start(bf16[32,192]{1,0:T(8,128)(2,1)} %constant.16.clone.matrix_ref.refs_6_) | copy-start | bytes 36868
  41.9 7.9 %copy-start.4 = (bf16[32,192]{1,0:T(8,128)(2,1)S(1)}, bf16[32,192]{1,0:T(8,128)(2,1)}, u32[]{:S(2)}) copy-start(bf16[32,192]{1,0:T(8,128)(2,1)} %constant.17.clone.matrix_t_ref.refs_7_) | copy-start | bytes 36868
  50.5 7.4 %collective-permute-start.2 = (f32[8,48,128]{2,1,0:T(8,128)S(1)}, f32[8,48,128]{2,1,0:T(8,128)S(1)}, u32[]{:S(2)}, u32[]{:S(2)}) collective-permute-start(f32[8,48,128]{2,1,0:T(8,128)S(1)} %get-tuple-element.20.refs_1_), channel_id=1, source_target_pairs={{7,0},{0,8},{8,16},{16,24},{24,28},{28,20},{20,12},{12,4},{4,1},{1... | collective-permute-start | bytes 589832 | tf_op jit(solution)/shard_map/ppermute | solution.py:626
  50.5 7.3 %collective-permute-start.3 = (f32[8,48,128]{2,1,0:T(8,128)S(1)}, f32[8,48,128]{2,1,0:T(8,128)S(1)}, u32[]{:S(2)}, u32[]{:S(2)}) collective-permute-start(f32[8,48,128]{2,1,0:T(8,128)S(1)} %get-tuple-element.20.refs_1_), channel_id=1, source_target_pairs={{8,0},{16,8},{24,16},{28,24},{20,28},{12,20},{4,12},{1,4},{9,1},{1... | collective-permute-start | bytes 589832 | tf_op jit(solution)/shard_map/ppermute | solution.py:626
  80.8 14.4 %all-to-all-start.2 = ((f32[8,96,128]{2,1,0:T(8,128)}), f32[8,96,128]{2,1,0:T(8,128)S(1)}, u32[]{:S(2)}, u32[]{:S(2)}) async-start(f32[8,96,128]{2,1,0:T(8,128)} %shard_map.99), calls=%async_computation.2 | async-start | bytes 786432 | tf_op jit(solution)/shard_map/all_to_all | solution.py:609
  95.3 11.2 %collective-permute-start.4 = (f32[10,4,512]{2,1,0:T(4,128)S(1)}, f32[10,4,512]{2,1,0:T(4,128)S(1)}, u32[]{:S(2)}, u32[]{:S(2)}) collective-permute-start(f32[10,4,512]{2,1,0:T(4,128)S(1)} %pad_maximum_fusion), channel_id=1, source_target_pairs={{0,1},{1,2},{2,3},{3,0},{4,5},{5,6},{6,7},{7,4},{8,9},{9,10},{10,1... | collective-permute-start | bytes 245768 | tf_op jit(solution)/shard_map/ppermute | solution.py:614

commit v10 on v9

--- a/solution.py
+++ b/solution.py
@@ -182,10 +182,6 @@
             put(sums_ref, slot, k, nothing)
     blank = jnp.zeros((PAIR_PAD, BLOCK), bf16)
     passes = width // at_once
-    square = (BLOCK, BLOCK)
-    unit_matrix = (
-        lax.broadcasted_iota(jnp.int32, square, 0) == lax.broadcasted_iota(jnp.int32, square, 1)
-    ).astype(f32).astype(bf16)
 
     def one_table(step, slot):
         at_frame = step // passes
@@ -203,9 +199,7 @@
                 four = jnp.concatenate(
                     [rows_ref[slot, pl.ds(low + j, PAIR_PAD, stride=apart), :] for j in range(QUAD)], axis=0
                 )
-                far_ref[at, quad] = lax.dot_general(
-                    unit_matrix, four.astype(bf16), (((1,), (1,)), ((), ())), preferred_element_type=f32
-                ).astype(bf16)
+                far_ref[at, quad] = jnp.transpose(four.astype(bf16))
                 for half in range(2):
                     heavy_ref[at, 2 * quad + half] = jnp.concatenate(
                         [

time: 119 us -> 118 us (level)
  Pallas kernels: 70.7 us -> 69.1 us
    pallas_call x7, Pallas kernels: 70.7 us -> 69.1 us  [call(): pl.pallas_call(kernel, out_shape=[jax.ShapeDtypeStruct(shape, f32) for sh...]
  transfers between devices with their start and end apart: 8 -> 8, of which waited for: 3 -> 4; matrix products, arithmetic and copies ran while one was open for 0% -> 0% of each run, Pallas kernels for 28% -> 28%
where the time goes in v10:
time: 118 us; the launch traced here: 117 us
  Pallas kernels  69.1 us (59%)
  waiting for transfers between devices  23.5 us (20%)
  starting transfers between devices  22.3 us (19%)
    pallas_call x7, Pallas kernels, call(): pl.pallas_call(kernel, out_shape=[jax.ShapeDtypeStruct(shape, f32) for sh...  69.1 us
    all_to_all x3, waiting for transfers between devices, exchange(): lax.all_to_all(pieces, 'bead', split_axis=0, concat_axis=0, axis_index_gr...  18.8 us
    all_to_all x3, starting transfers between devices, exchange(): lax.all_to_all(pieces, 'bead', split_axis=0, concat_axis=0, axis_index_gr...  13.4 us
    ppermute x3, starting transfers between devices, round_ring(): lax.ppermute(values, ('bead', 'space'), [(device[(at + hop) % total], dev...  6.05 us
    ppermute x3, waiting for transfers between devices, round_ring(): lax.ppermute(values, ('bead', 'space'), [(device[(at + hop) % total], dev...  4.69 us
    ppermute x2, starting transfers between devices, passed(): lax.ppermute(values, 'space', [(i, (i + step) % count) for i in range(cou...  2.79 us
  transfers between devices with their start and end apart: 8, of which 4 were waited for; matrix products, arithmetic and copies ran while one was open for 0% of the time, Pallas kernels for 28%

profile of v10, /device:TPU:0, one launch (start us, length us, event | category | flops | bytes accessed | tf_op | source)
XLA Modules:
  0.0 116.9 jit_solution(2620054223214990166)
XLA Ops:
  0.6 2.0 %shard_map.95 = (f32[8,144,128]{2,1,0:T(8,128)}, f32[13,4,512]{2,1,0:T(4,128)}, f32[1,4096]{1,0:T(1,128)}, f32[1,4096]{1,0:T(1,128)}) custom-call(f32[3,4,4096]{2,1,0:T(4,128)} %x_ref.5, f32[3,4,4096]{2,1,0:T(4,128)} %p_ref.3, f32[2,3,4,4096]{3,2,1,0:T(4,128)} %noise_ref.1, s32[1,4096]{1,0:T(1,128)} %bitcast.34, s32[5,32]{1,0:T(8,128)} %bitcast.29), custom_call_target="tpu_custom_call" | custom-call | flops 1024 | bytes 4194304 | tf_op jit(solution)/shard_map/pallas_call | solution.py:328
  2.7 0.0 copy-start.9
  2.7 0.0 copy-start.5
  2.7 0.0 copy-start
  2.7 0.0 copy-start.1
  2.7 6.5 %all-to-all-start = ((f32[8,144,128]{2,1,0:T(8,128)}), f32[8,144,128]{2,1,0:T(8,128)S(1)}, u32[]{:S(2)}, u32[]{:S(2)}) async-start(f32[8,144,128]{2,1,0:T(8,128)} %get-tuple-element.14), calls=%async_computation | async-start | bytes 1179648 | tf_op jit(solution)/shard_map/all_to_all | solution.py:603
  9.1 0.0 copy-start.8
  9.2 0.0 copy-done.9
  9.2 2.5 %collective-permute-start = (f32[13,4,512]{2,1,0:T(4,128)S(1)}, f32[13,4,512]{2,1,0:T(4,128)S(1)}, u32[]{:S(2)}, u32[]{:S(2)}) collective-permute-start(f32[13,4,512]{2,1,0:T(4,128)S(1)} %copy-done.9), channel_id=1, source_target_pairs={{0,3},{1,0},{2,1},{3,2},{4,7},{5,4},{6,5},{7,6},{8,11},{9,8},{10,9... | collective-permute-start | bytes 319496 | tf_op jit(solution)/shard_map/ppermute | solution.py:608
  11.7 0.0 copy-done.5
  11.7 0.1 slice.54
  11.7 0.0 copy-done.8
  11.7 0.0 copy-start.6
  11.7 0.0 copy-done
  11.7 0.0 copy-done.1
  11.8 0.7 copy-done.6
  12.5 10.7 %shard_map.96.front_ref = f32[4,48,128]{2,1,0:T(8,128)S(1)} custom-call(s32[5,32]{1,0:T(8,128)S(1)} %bitcast.31, s32[1,4096]{1,0:T(1,128)S(1)} %bitcast.35, f32[3,4,4096]{2,1,0:T(4,128)S(1)} %copy-done, f32[3,4,4096]{2,1,0:T(4,128)S(1)} %copy-done.1), custom_call_target="tpu_custom_call" | custom-call | flops 104858624 | bytes 4194304 | tf_op jit(solution)/shard_map/pallas_call | solution.py:328
  23.1 0.0 collective-permute-done.message_ref
  23.2 0.0 copy-start.7
  23.2 0.1 reshape_squeeze.3
  23.3 0.1 all-to-all-done
  23.3 3.4 %collective-permute-start.1 = (f32[8,144,128]{2,1,0:T(8,128)S(1)}, f32[8,144,128]{2,1,0:T(8,128)S(1)}, u32[]{:S(2)}, u32[]{:S(2)}) collective-permute-start(f32[8,144,128]{2,1,0:T(8,128)S(1)} %all-to-all-done), channel_id=1, source_target_pairs={{8,0},{16,8},{24,16},{28,24},{20,28},{12,20},{4,12},{1,4},{9,1},{1... | collective-permute-start | bytes 1769480 | tf_op jit(solution)/shard_map/ppermute | solution.py:620
  26.7 0.1 pad_add_fusion.lists_ref
  26.8 0.0 copy-done.7
  26.8 11.3 %shard_map.97 = f32[8,48,128]{2,1,0:T(8,128)} custom-call(s32[5,32]{1,0:T(8,128)S(1)} %pad_add_fusion.lists_ref, f32[1,5120]{1,0:T(1,128)S(1)} %pad_maximum_fusion.1.charge_ref, f32[3,4,4096]{2,1,0:T(4,128)S(1)} %copy-done, f32[13,4,512]{2,1,0:T(4,128)S(1)} %collective-permute-done.message_ref, f32[3,4,4096]{2,1,0:T(4,128)S(1)} %copy-done.1, ...), custom_call_target="tpu_custom_call" | custom-call | flops 104858624 | bytes 4194304 | tf_op jit(solution)/shard_map/pallas_call | solution.py:328
  38.1 0.0 collective-permute-done.1.rest_ref.refs_4_
  38.1 0.0 copy-start.2
  38.1 3.5 %all-to-all-start.1 = ((f32[8,48,128]{2,1,0:T(8,128)}), f32[8,48,128]{2,1,0:T(8,128)S(1)}, u32[]{:S(2)}, u32[]{:S(2)}) async-start(f32[8,48,128]{2,1,0:T(8,128)} %shard_map.97), calls=%async_computation.1 | async-start | bytes 393216 | tf_op jit(solution)/shard_map/all_to_all | solution.py:603
  41.7 0.0 copy-start.3
  41.7 0.0 copy-start.4
  41.7 7.8 %all-to-all-done.1.p_ref = f32[8,48,128]{2,1,0:T(8,128)S(1)} async-done(((f32[8,48,128]{2,1,0:T(8,128)}), f32[8,48,128]{2,1,0:T(8,128)S(1)}, u32[]{:S(2)}, u32[]{:S(2)}) %all-to-all-start.1) | async-done | bytes 196640 | tf_op jit(solution)/shard_map/all_to_all | solution.py:603
  49.5 0.0 copy-done.2
  49.5 0.0 copy-done.3
  49.5 0.0 copy-done.4
  49.5 0.7 shard_map.98
  50.2 0.1 collective-permute-start.2
  50.3 2.6 %collective-permute-start.3 = (f32[8,48,128]{2,1,0:T(8,128)S(1)}, f32[8,48,128]{2,1,0:T(8,128)S(1)}, u32[]{:S(2)}, u32[]{:S(2)}) collective-permute-start(f32[8,48,128]{2,1,0:T(8,128)S(1)} %get-tuple-element.20.refs_1_), channel_id=1, source_target_pairs={{8,0},{16,8},{24,16},{28,24},{20,28},{12,20},{4,12},{1,4},{9,1},{1... | collective-permute-start | bytes 589832 | tf_op jit(solution)/shard_map/ppermute | solution.py:620
  52.9 4.7 %collective-permute-done.2.refs_0_ = f32[8,48,128]{2,1,0:T(8,128)S(1)} collective-permute-done((f32[8,48,128]{2,1,0:T(8,128)S(1)}, f32[8,48,128]{2,1,0:T(8,128)S(1)}, u32[]{:S(2)}, u32[]{:S(2)}) %collective-permute-start.2) | collective-permute-done | bytes 196640 | tf_op jit(solution)/shard_map/ppermute | solution.py:620
  57.6 0.0 collective-permute-done.3.refs_2_
  57.6 22.4 %shard_map.99 = f32[8,96,128]{2,1,0:T(8,128)} custom-call(s32[5,32]{1,0:T(8,128)S(1)} %pad_add_fusion.lists_ref, f32[1,5120]{1,0:T(1,128)S(1)} %pad_maximum_fusion.1.charge_ref, f32[8,48,128]{2,1,0:T(8,128)S(1)} %collective-permute-done.2.refs_0_, f32[8,48,128]{2,1,0:T(8,128)S(1)} %get-tuple-element.20.refs_1_, ...), custom_call_target="tpu_custom_call" | custom-call | flops 209716224 | bytes 4194304 | tf_op jit(solution)/shard_map/pallas_call | solution.py:328
  80.0 3.5 %all-to-all-start.2 = ((f32[8,96,128]{2,1,0:T(8,128)}), f32[8,96,128]{2,1,0:T(8,128)S(1)}, u32[]{:S(2)}, u32[]{:S(2)}) async-start(f32[8,96,128]{2,1,0:T(8,128)} %shard_map.99), calls=%async_computation.2 | async-start | bytes 786432 | tf_op jit(solution)/shard_map/all_to_all | solution.py:603
  83.5 10.9 %all-to-all-done.2.both_ref = f32[8,96,128]{2,1,0:T(8,128)S(1)} async-done(((f32[8,96,128]{2,1,0:T(8,128)}), f32[8,96,128]{2,1,0:T(8,128)S(1)}, u32[]{:S(2)}, u32[]{:S(2)}) %all-to-all-start.2) | async-done | bytes 393248 | tf_op jit(solution)/shard_map/all_to_all | solution.py:603
  94.6 0.3 collective-permute-start.4
  94.9 10.7 %shard_map.100.upper_ref = f32[3,4,2048]{2,1,0:T(4,128)S(1)} custom-call(s32[5,32]{1,0:T(8,128)S(1)} %bitcast.32, f32[1,5120]{1,0:T(1,128)S(1)} %pad_maximum_fusion.1.charge_ref, f32[8,96,128]{2,1,0:T(8,128)S(1)} %all-to-all-done.2.both_ref), custom_call_target="tpu_custom_call" | custom-call | flops 104858624 | bytes 4194304 | tf_op jit(solution)/shard_map/pallas_call | solution.py:328
  105.5 0.0 collective-permute-done.4.message_ref
  105.6 11.4 %shard_map.101 = (f32[3,4,4096]{2,1,0:T(4,128)}, f32[3,4,4096]{2,1,0:T(4,128)}) custom-call(s32[5,32]{1,0:T(8,128)S(1)} %bitcast.33, f32[1,3072]{1,0:T(1,128)S(1)} %pad_maximum_fusion.3.charge_ref, f32[8,96,128]{2,1,0:T(8,128)S(1)} %all-to-all-done.2.both_ref, f32[10,4,512]{2,1,0:T(4,128)S(1)} %collective-permute-done.4.message_ref, ...), custom_call_target="tpu_custom_call" | custom-call | flops 104858624 | bytes 4194304 | tf_op jit(solution)/shard_map/pallas_call | solution.py:328
  (18 shorter events, 0.2 us)
Async XLA Ops:
  2.7 6.5 %copy-start.9 = (f32[13,4,512]{2,1,0:T(4,128)S(1)}, f32[13,4,512]{2,1,0:T(4,128)}, u32[]{:S(2)}) copy-start(f32[13,4,512]{2,1,0:T(4,128)} %get-tuple-element.12) | copy-start | bytes 319492
  2.7 9.0 %copy-start.5 = (s32[32,5]{0,1:T(8,128)S(1)}, s32[32,5]{0,1:T(8,128)}, u32[]{:S(2)}) copy-start(s32[32,5]{0,1:T(8,128)} %param.11) | copy-start | bytes 1924
  2.7 9.1 %copy-start = (f32[3,4,4096]{2,1,0:T(4,128)S(1)}, f32[3,4,4096]{2,1,0:T(4,128)}, u32[]{:S(2)}) copy-start(f32[3,4,4096]{2,1,0:T(4,128)} %x_ref.5) | copy-start | bytes 589828
  2.7 9.1 %copy-start.1 = (f32[3,4,4096]{2,1,0:T(4,128)S(1)}, f32[3,4,4096]{2,1,0:T(4,128)}, u32[]{:S(2)}) copy-start(f32[3,4,4096]{2,1,0:T(4,128)} %p_ref.3) | copy-start | bytes 589828
  2.7 20.6 %all-to-all-start = ((f32[8,144,128]{2,1,0:T(8,128)}), f32[8,144,128]{2,1,0:T(8,128)S(1)}, u32[]{:S(2)}, u32[]{:S(2)}) async-start(f32[8,144,128]{2,1,0:T(8,128)} %get-tuple-element.14), calls=%async_computation | async-start | bytes 1179648 | tf_op jit(solution)/shard_map/all_to_all | solution.py:603
  9.1 2.6 %copy-start.8 = (f32[1,4096]{1,0:T(1,128)S(1)}, f32[1,4096]{1,0:T(1,128)}, u32[]{:S(2)}) copy-start(f32[1,4096]{1,0:T(1,128)} %get-tuple-element.19) | copy-start | bytes 49156
  9.2 14.0 %collective-permute-start = (f32[13,4,512]{2,1,0:T(4,128)S(1)}, f32[13,4,512]{2,1,0:T(4,128)S(1)}, u32[]{:S(2)}, u32[]{:S(2)}) collective-permute-start(f32[13,4,512]{2,1,0:T(4,128)S(1)} %copy-done.9), channel_id=1, source_target_pairs={{0,3},{1,0},{2,1},{3,2},{4,7},{5,4},{6,5},{7,6},{8,11},{9,8},{10,9... | collective-permute-start | bytes 319496 | tf_op jit(solution)/shard_map/ppermute | solution.py:608
  11.7 0.7 copy-start.6
  23.2 3.6 %copy-start.7 = (f32[1,4096]{1,0:T(1,128)S(1)}, f32[1,4096]{1,0:T(1,128)}, u32[]{:S(2)}) copy-start(f32[1,4096]{1,0:T(1,128)} %get-tuple-element.13) | copy-start | bytes 49156
  23.3 14.8 %collective-permute-start.1 = (f32[8,144,128]{2,1,0:T(8,128)S(1)}, f32[8,144,128]{2,1,0:T(8,128)S(1)}, u32[]{:S(2)}, u32[]{:S(2)}) collective-permute-start(f32[8,144,128]{2,1,0:T(8,128)S(1)} %all-to-all-done), channel_id=1, source_target_pairs={{8,0},{16,8},{24,16},{28,24},{20,28},{12,20},{4,12},{1,4},{9,1},{1... | collective-permute-start | bytes 1769480 | tf_op jit(solution)/shard_map/ppermute | solution.py:620
  38.1 11.4 %copy-start.2 = (f32[5,32,128]{2,1,0:T(8,128)S(1)}, f32[5,32,128]{2,1,0:T(8,128)}, u32[]{:S(2)}) copy-start(f32[5,32,128]{2,1,0:T(8,128)} %constant.18.clone.table_ref.refs_8_) | copy-start | bytes 245764
  38.1 11.4 %all-to-all-start.1 = ((f32[8,48,128]{2,1,0:T(8,128)}), f32[8,48,128]{2,1,0:T(8,128)S(1)}, u32[]{:S(2)}, u32[]{:S(2)}) async-start(f32[8,48,128]{2,1,0:T(8,128)} %shard_map.97), calls=%async_computation.1 | async-start | bytes 393216 | tf_op jit(solution)/shard_map/all_to_all | solution.py:603
  41.7 7.9 %copy-start.3 = (bf16[32,192]{1,0:T(8,128)(2,1)S(1)}, bf16[32,192]{1,0:T(8,128)(2,1)}, u32[]{:S(2)}) copy-start(bf16[32,192]{1,0:T(8,128)(2,1)} %constant.16.clone.matrix_ref.refs_6_) | copy-start | bytes 36868
  41.7 7.9 %copy-start.4 = (bf16[32,192]{1,0:T(8,128)(2,1)S(1)}, bf16[32,192]{1,0:T(8,128)(2,1)}, u32[]{:S(2)}) copy-start(bf16[32,192]{1,0:T(8,128)(2,1)} %constant.17.clone.matrix_t_ref.refs_7_) | copy-start | bytes 36868
  50.2 7.4 %collective-permute-start.2 = (f32[8,48,128]{2,1,0:T(8,128)S(1)}, f32[8,48,128]{2,1,0:T(8,128)S(1)}, u32[]{:S(2)}, u32[]{:S(2)}) collective-permute-start(f32[8,48,128]{2,1,0:T(8,128)S(1)} %get-tuple-element.20.refs_1_), channel_id=1, source_target_pairs={{7,0},{0,8},{8,16},{16,24},{24,28},{28,20},{20,12},{12,4},{4,1},{1... | collective-permute-start | bytes 589832 | tf_op jit(solution)/shard_map/ppermute | solution.py:620
  50.3 7.3 %collective-permute-start.3 = (f32[8,48,128]{2,1,0:T(8,128)S(1)}, f32[8,48,128]{2,1,0:T(8,128)S(1)}, u32[]{:S(2)}, u32[]{:S(2)}) collective-permute-start(f32[8,48,128]{2,1,0:T(8,128)S(1)} %get-tuple-element.20.refs_1_), channel_id=1, source_target_pairs={{8,0},{16,8},{24,16},{28,24},{20,28},{12,20},{4,12},{1,4},{9,1},{1... | collective-permute-start | bytes 589832 | tf_op jit(solution)/shard_map/ppermute | solution.py:620
  80.0 14.4 %all-to-all-start.2 = ((f32[8,96,128]{2,1,0:T(8,128)}), f32[8,96,128]{2,1,0:T(8,128)S(1)}, u32[]{:S(2)}, u32[]{:S(2)}) async-start(f32[8,96,128]{2,1,0:T(8,128)} %shard_map.99), calls=%async_computation.2 | async-start | bytes 786432 | tf_op jit(solution)/shard_map/all_to_all | solution.py:603
  94.6 11.0 %collective-permute-start.4 = (f32[10,4,512]{2,1,0:T(4,128)S(1)}, f32[10,4,512]{2,1,0:T(4,128)S(1)}, u32[]{:S(2)}, u32[]{:S(2)}) collective-permute-start(f32[10,4,512]{2,1,0:T(4,128)S(1)} %pad_maximum_fusion), channel_id=1, source_target_pairs={{0,1},{1,2},{2,3},{3,0},{4,5},{5,6},{6,7},{7,4},{8,9},{9,10},{10,1... | collective-permute-start | bytes 245768 | tf_op jit(solution)/shard_map/ppermute | solution.py:608
